TPU v7x, 32 devices: a whole 2x2x4 slice. The times are simulated.
32 devices in a mesh: section: 4 (over y, x), row: 2 (over core), col: 4 (over z).
Axes of the slice: x: 2, y: 2, z: 4, core: 2. Of those that a mesh axis runs over, the one named last changes fastest.
Arguments:
- inputs: bfloat16 [4, 128, 4096], P('section', 'col', 'row'), may hold values from -6 to 6
- gate_pre: bfloat16 [4, 128, 14336], P('section', None, 'col'), may hold values from -8 to 8
- up_weight: bfloat16 [4096, 14336], P('row', 'col'), may hold values from -0.09375 to 0.09375
- down_weight: bfloat16 [14336, 4096], P('col', 'row'), may hold values from -0.046875 to 0.046875
- output_grad: bfloat16 [4, 128, 4096], P('section', 'col', 'row'), may hold values from -6 to 6
Outputs:
- handed_forward: bfloat16 [4, 128, 4096], P('section', 'col', 'row')
- gate_grad: bfloat16 [4, 128, 14336], P('section', 'row', 'col')
- handed_back: bfloat16 [4, 128, 4096], P('section', 'col', 'row')
All inputs are finite; a program needn't handle non-finite values.
Results may differ from a plain program's by a relative error of at most 0.0041.
Values may be sent and summed in bfloat16 or wider, within the bound.
No kernel may reach another device: no remote copies, remote signals or barrier semaphores. Data moves between devices by JAX's collectives and lax.ppermute only.
A program may use at most 64 MiB of HBM per device.

v0:
```python
import jax
import jax.numpy as jnp
from jax import lax
from jax.sharding import PartitionSpec as P


def shifted(value, axis, steps):
    count = lax.axis_size(axis)
    pairs = [(source, (source + steps) % count) for source in range(count)]
    return lax.ppermute(value, axis, pairs)


def row_product(pieces, matrix, contract):
    gathered = lax.all_gather(pieces, "col", axis=0, tiled=True)
    return lax.psum_scatter(
        lax.dot_general(gathered, matrix, (contract, ((), ())), preferred_element_type=jnp.float32),
        "row",
        scatter_dimension=0,
        tiled=True,
    )


def col_product(values, matrix, contract):
    gathered = lax.all_gather(values, "row", axis=0, tiled=True)
    return lax.psum_scatter(
        lax.dot_general(gathered, matrix, (contract, ((), ())), preferred_element_type=jnp.float32),
        "col",
        scatter_dimension=0,
        tiled=True,
    )


def handoff(values, offset):
    return shifted(values, "section", offset)


def shards(inputs, gate_pre, up_weight, down_weight, output_grad):
    activations = inputs[0]
    grad_tile = output_grad[0]
    gate_full = gate_pre[0].astype(jnp.float32)
    own_rows = gate_full.shape[0] // lax.axis_size("row")
    row_start = lax.axis_index("row") * own_rows
    gate_used = lax.dynamic_slice_in_dim(gate_full, row_start, own_rows, 0)
    up_act = row_product(activations, up_weight, ((1,), (0,)))
    sigmoid_gate = jax.nn.sigmoid(gate_used)
    hidden = (gate_used * sigmoid_gate * up_act).astype(jnp.bfloat16)
    mixed = col_product(hidden, down_weight, ((1,), (0,)))
    layer_out = (activations.astype(jnp.float32) + mixed).astype(jnp.bfloat16)
    handed_forward = handoff(layer_out, 1)
    hidden_grad = row_product(grad_tile, down_weight, ((1,), (1,)))
    up_grad = (hidden_grad * gate_used * sigmoid_gate).astype(jnp.bfloat16)
    gate_grad = (
        hidden_grad * up_act * sigmoid_gate * (1.0 + gate_used * (1.0 - sigmoid_gate))
    ).astype(jnp.bfloat16)
    back_sum = col_product(up_grad, up_weight, ((1,), (1,)))
    input_grad = (grad_tile.astype(jnp.float32) + back_sum).astype(jnp.bfloat16)
    handed_back = handoff(input_grad, -1)
    return (handed_forward[None], gate_grad[None], handed_back[None])


def solution(mesh):
    placed = (
        P("section", "col", "row"),
        P("section", None, "col"),
        P("row", "col"),
        P("col", "row"),
        P("section", "col", "row"),
    )
    return jax.shard_map(
        shards,
        mesh=mesh,
        in_specs=placed,
        out_specs=(
            P("section", "col", "row"),
            P("section", "row", "col"),
            P("section", "col", "row"),
        ),
        check_vma=False,
    )
```

profile of v0, /device:TPU:0, one launch (start us, length us, event | category | flops | bytes accessed | tf_op | source)
XLA Modules:
  0.0 158.6 jit_solution(7184507581413897773)
XLA Ops:
  7.2 0.0 copy-start.1
  7.2 0.0 reduce-scatter.9.cloned.1.call-start
  7.2 17.6 %all-gather.1 = bf16[1,128,2048]{2,1,0:T(8,128)(2,1)S(1)} all-gather(bf16[1,32,2048]{2,1,0:T(8,128)(2,1)} %param.9), channel_id=3, replica_groups=mesh['section'=4,'row'=2,'col'=4] {'col'}, dimensions={1}, use_global_device_ids=true | all-gather | bytes 655360 | tf_op jit(solution)/shard_map/all_gather | solution.py:14
  24.8 11.3 %fusion.10 = f32[128,3584]{1,0:T(8,128)} fusion(bf16[3584,2048]{1,0:T(8,128)(2,1)} %param.8, bf16[1,128,2048]{2,1,0:T(8,128)(2,1)S(1)} %all-gather.1), kind=kOutput, calls=%fused_computation.14 | convolution fusion | flops 1879048192 | bytes 17039360 | tf_op jit(solution)/shard_map/dot_general | solution.py:16
  36.1 0.0 reduce-scatter.9.cloned.1.call-update
  36.2 0.0 reduce-scatter.5.cloned.1.call-start
  36.2 0.0 copy-done.1
  36.2 16.4 %all-gather = bf16[1,128,2048]{2,1,0:T(8,128)(2,1)S(1)} all-gather(bf16[1,32,2048]{2,1,0:T(8,128)(2,1)S(1)} %copy-done.1), channel_id=2, replica_groups=mesh['section'=4,'row'=2,'col'=4] {'col'}, dimensions={1}, use_global_device_ids=true | all-gather | bytes 655360 | tf_op jit(solution)/shard_map/all_gather | solution.py:14
  52.6 8.5 %fusion.12 = f32[128,3584]{1,0:T(8,128)} fusion(bf16[2048,3584]{1,0:T(8,128)(2,1)} %param.7, bf16[1,128,2048]{2,1,0:T(8,128)(2,1)S(1)} %all-gather), kind=kOutput, calls=%fused_computation.16 | convolution fusion | flops 1879048192 | bytes 17039360 | tf_op jit(solution)/shard_map/dot_general | solution.py:16
  61.1 0.0 reduce-scatter.5.cloned.1.call-update
  61.2 0.0 reduce-scatter.11.cloned.1.call-start
  61.2 0.0 reduce-scatter.9.cloned.1.call-done
  61.2 9.8 %reduce-scatter.5.cloned.1.call-done = f32[64,3584]{1,0:T(8,128)} async-done(((f32[128,3584]{1,0:T(8,128)}), f32[64,3584]{1,0:T(8,128)}) %reduce-scatter.5.cloned.1.call-update) | async-done | bytes 917520 | tf_op jit(solution)/shard_map/reduce_scatter | solution.py:15
  71.1 0.0 copy-done.2
  71.1 2.7 %fusion.9 = (bf16[64,3584]{1,0:T(8,128)(2,1)S(1)}, bf16[1,64,3584]{2,1,0:T(8,128)(2,1)}, bf16[64,3584]{1,0:T(8,128)(2,1)S(1)}) fusion(f32[64,3584]{1,0:T(8,128)} %reduce-scatter.9.cloned.1.call-done, bf16[1,128,3584]{2,1,0:T(8,128)(2,1)S(1)} %copy-done.2, s32[]{:T(128)S(6)} %select_n.3, f32[64,3584]{1,0:T(8,128)} %reduce-scatter.5.cloned.1.call-done), kind=kLoop, calls=%fused_computation.13 | loop fusion | flops 3899392 | bytes 3670020 | tf_op jit(solution)/shard_map/convert_element_type | solution.py:51
  73.8 2.4 %all_gather.15 = bf16[128,3584]{1,0:T(8,128)(2,1)S(1)} all-gather(bf16[64,3584]{1,0:T(8,128)(2,1)S(1)} %get-tuple-element.3), channel_id=1, replica_groups=mesh['section'=4,'row'=2,'col'=4] {'row'}, dimensions={0}, use_global_device_ids=true | all-gather | bytes 1376256 | tf_op jit(solution)/shard_map/all_gather | solution.py:24
  76.3 11.0 %fusion.18 = f32[128,2048]{1,0:T(8,128)} fusion(bf16[128,3584]{1,0:T(8,128)(2,1)S(1)} %all_gather.15, bf16[2048,3584]{1,0:T(8,128)(2,1)} %param.7), kind=kOutput, calls=%fused_computation.24 | convolution fusion | flops 1879048192 | bytes 16646144 | tf_op jit(solution)/shard_map/dot_general | solution.py:26
  87.2 0.0 reduce-scatter.11.cloned.1.call-update
  87.3 0.0 reduce-scatter.7.cloned.1.call-start
  87.3 2.5 %all_gather.13 = bf16[128,3584]{1,0:T(8,128)(2,1)S(1)} all-gather(bf16[64,3584]{1,0:T(8,128)(2,1)S(1)} %get-tuple-element.5), channel_id=1, replica_groups=mesh['section'=4,'row'=2,'col'=4] {'row'}, dimensions={0}, use_global_device_ids=true | all-gather | bytes 1376256 | tf_op jit(solution)/shard_map/all_gather | solution.py:24
  89.8 8.6 %fusion.17 = f32[128,2048]{1,0:T(8,128)} fusion(bf16[128,3584]{1,0:T(8,128)(2,1)S(1)} %all_gather.13, bf16[3584,2048]{1,0:T(8,128)(2,1)} %param.8), kind=kOutput, calls=%fused_computation.23 | convolution fusion | flops 1879048192 | bytes 16646144 | tf_op jit(solution)/shard_map/dot_general | solution.py:26
  98.4 0.0 reduce-scatter.7.cloned.1.call-update
  98.4 17.3 %reduce-scatter.11.cloned.1.call-done = f32[32,2048]{1,0:T(8,128)} async-done(((f32[128,2048]{1,0:T(8,128)}), f32[32,2048]{1,0:T(8,128)}) %reduce-scatter.11.cloned.1.call-update) | async-done | bytes 262160 | tf_op jit(solution)/shard_map/reduce_scatter | solution.py:25
  115.7 1.0 fusion.15
  116.7 2.4 %collective-permute-start.1 = (bf16[32,2048]{1,0:T(8,128)(2,1)S(1)}, bf16[32,2048]{1,0:T(8,128)(2,1)S(1)}, u32[]{:S(2)}, u32[]{:S(2)}) collective-permute-start(bf16[32,2048]{1,0:T(8,128)(2,1)S(1)} %fusion.15), channel_id=1, source_target_pairs={{0,24},{8,0},{16,8},{24,16},{1,25},{9,1},{17,9},{25,17},{2,26},{10... | collective-permute-start | bytes 393224 | tf_op jit(solution)/shard_map/ppermute | solution.py:10
  119.1 24.7 %reduce-scatter.7.cloned.1.call-done = f32[32,2048]{1,0:T(8,128)} async-done(((f32[128,2048]{1,0:T(8,128)}), f32[32,2048]{1,0:T(8,128)}) %reduce-scatter.7.cloned.1.call-update) | async-done | bytes 262160 | tf_op jit(solution)/shard_map/reduce_scatter | solution.py:25
  143.8 1.0 fusion.16
  144.8 1.5 collective-permute-start
  146.3 0.0 collective-permute-done.1
  146.3 4.5 %collective-permute-done = bf16[32,2048]{1,0:T(8,128)(2,1)S(1)} collective-permute-done((bf16[32,2048]{1,0:T(8,128)(2,1)S(1)}, bf16[32,2048]{1,0:T(8,128)(2,1)S(1)}, u32[]{:S(2)}, u32[]{:S(2)}) %collective-permute-start) | collective-permute-done | bytes 131104 | tf_op jit(solution)/shard_map/ppermute | solution.py:10
  150.8 0.7 copy.10
  151.4 0.7 copy.11
  (3 shorter events, 0.0 us)
Async XLA Ops:
  7.2 29.0 %copy-start.1 = (bf16[1,32,2048]{2,1,0:T(8,128)(2,1)S(1)}, bf16[1,32,2048]{2,1,0:T(8,128)(2,1)}, u32[]{:S(2)}) copy-start(bf16[1,32,2048]{2,1,0:T(8,128)(2,1)} %param.5) | copy-start | bytes 393220
  7.2 54.1 %reduce-scatter.9.cloned.1.call-start = ((), (), s32[]{:S(2)}) async-start(), calls=%async_computation.6 | async-start | bytes 2752512 | tf_op jit(solution)/shard_map/reduce_scatter | solution.py:15
  36.1 35.0 %copy-start.2 = (bf16[1,128,3584]{2,1,0:T(8,128)(2,1)S(1)}, bf16[1,128,3584]{2,1,0:T(8,128)(2,1)}, u32[]{:S(2)}) copy-start(bf16[1,128,3584]{2,1,0:T(8,128)(2,1)} %param.6) | copy-start | bytes 2752516
  36.2 34.9 %reduce-scatter.5.cloned.1.call-start = ((), (), s32[]{:S(2)}) async-start(), calls=%async_computation.4 | async-start | bytes 2752512 | tf_op jit(solution)/shard_map/reduce_scatter | solution.py:15
  61.2 54.5 %reduce-scatter.11.cloned.1.call-start = ((), (), s32[]{:S(2)}) async-start(), calls=%async_computation.7 | async-start | bytes 1310720 | tf_op jit(solution)/shard_map/reduce_scatter | solution.py:25
  87.2 28.5 %copy-start = (bf16[1,32,2048]{2,1,0:T(8,128)(2,1)S(1)}, bf16[1,32,2048]{2,1,0:T(8,128)(2,1)}, u32[]{:S(2)}) copy-start(bf16[1,32,2048]{2,1,0:T(8,128)(2,1)} %param.9) | copy-start | bytes 393220
  87.3 56.6 %reduce-scatter.7.cloned.1.call-start = ((), (), s32[]{:S(2)}) async-start(), calls=%async_computation.5 | async-start | bytes 1310720 | tf_op jit(solution)/shard_map/reduce_scatter | solution.py:25
  116.7 29.6 %collective-permute-start.1 = (bf16[32,2048]{1,0:T(8,128)(2,1)S(1)}, bf16[32,2048]{1,0:T(8,128)(2,1)S(1)}, u32[]{:S(2)}, u32[]{:S(2)}) collective-permute-start(bf16[32,2048]{1,0:T(8,128)(2,1)S(1)} %fusion.15), channel_id=1, source_target_pairs={{0,24},{8,0},{16,8},{24,16},{1,25},{9,1},{17,9},{25,17},{2,26},{10... | collective-permute-start | bytes 393224 | tf_op jit(solution)/shard_map/ppermute | solution.py:10
  144.8 6.0 %collective-permute-start = (bf16[32,2048]{1,0:T(8,128)(2,1)S(1)}, bf16[32,2048]{1,0:T(8,128)(2,1)S(1)}, u32[]{:S(2)}, u32[]{:S(2)}) collective-permute-start(bf16[32,2048]{1,0:T(8,128)(2,1)S(1)} %fusion.16), channel_id=1, source_target_pairs={{0,8},{8,16},{16,24},{24,0},{1,9},{9,17},{17,25},{25,1},{2,10},{10... | collective-permute-start | bytes 393224 | tf_op jit(solution)/shard_map/ppermute | solution.py:10
Sparse Core Ops, SparseCore 0:
  36.3 11.1 reduce-scatter.8
  61.3 9.7 reduce-scatter.4
  87.4 28.2 reduce-scatter.10
  118.0 25.8 reduce-scatter.6
where the time goes:
time: 159 us
  waiting for transfers between devices  56.4 us (35%)
  matrix products  39.5 us (25%)
  blocking collectives  38.9 us (24%)
  between operations  13.8 us (9%)
  other arithmetic  4.67 us (3%)
  starting transfers between devices  4.12 us (3%)
    reduce_scatter x2, waiting for transfers between devices, col_product(): lax.psum_scatter(lax.dot_general(gathered, matrix, (contract, ((), ())),...  41.9 us
    all_gather x2, blocking collectives, row_product(): gathered = lax.all_gather(pieces, 'col', axis=0, tiled=True)  34 us
    dot_general x2, matrix products, row_product(): lax.dot_general(gathered, matrix, (contract, ((), ())), preferred_element...  19.8 us
    dot_general x2, matrix products, col_product(): lax.dot_general(gathered, matrix, (contract, ((), ())), preferred_element...  19.6 us
    reduce_scatter x2, waiting for transfers between devices, row_product(): lax.psum_scatter(lax.dot_general(gathered, matrix, (contract, ((), ())),...  9.86 us
    all_gather x2, blocking collectives, col_product(): gathered = lax.all_gather(values, 'row', axis=0, tiled=True)  4.91 us
    ppermute x2, waiting for transfers between devices, shifted(): return lax.ppermute(value, axis, pairs)  4.49 us
    ppermute x2, starting transfers between devices, shifted(): return lax.ppermute(value, axis, pairs)  3.96 us
  transfers between devices with their start and end apart: 6, of which 4 were waited for; matrix products, arithmetic and copies ran while one was open for 12% of the time, Pallas kernels for 0%

commit v1 on v0

v1 whole, which is shorter than its diff:
```python
import functools

import jax
import jax.numpy as jnp
from jax import lax
from jax.experimental import pallas as pl
from jax.experimental.pallas import tpu as pltpu
from jax.sharding import PartitionSpec as P

MIB = 1 << 20
VMEM = pl.BlockSpec(memory_space=pltpu.VMEM)
SMEM = pl.BlockSpec(memory_space=pltpu.SMEM)
F32 = jnp.float32
BF16 = jnp.bfloat16


def spans(extent, width):
    return [(start, min(width, extent - start)) for start in range(0, extent, width)]


def halves(extent):
    first = -(-extent // 256) * 128
    return [(0, first), (first, extent - first)]


def kernel_call(body, name, outs, args, flops=0, scratch=(), limit=12 * MIB, smem=0):
    moved = sum(a.size * a.dtype.itemsize for a in args)
    return pl.pallas_call(
        body,
        name=name,
        out_shape=outs,
        in_specs=[SMEM] * smem + [VMEM] * (len(args) - smem),
        out_specs=[VMEM] * len(outs),
        scratch_shapes=list(scratch),
        compiler_params=pltpu.CompilerParams(vmem_limit_bytes=limit),
        cost_estimate=pl.CostEstimate(flops=flops, bytes_accessed=moved, transcendentals=0),
    )(*args)


def shape(dims, dtype):
    return jax.ShapeDtypeStruct(tuple(dims), dtype)


def gates(place, gate, row_count):
    tokens, hidden = gate.shape
    own = tokens // row_count

    def body(place_ref, gate_ref, silu_ref, slope_ref):
        start = pl.multiple_of(place_ref[1] * own, own)
        for at, wide in spans(hidden, 512):
            value = gate_ref[:, at : at + wide].astype(F32)
            sig = 1.0 / (1.0 + jnp.exp(-value))
            silu_ref[:, at : at + wide] = value * sig
            value = gate_ref[pl.ds(start, own), at : at + wide].astype(F32)
            sig = 1.0 / (1.0 + jnp.exp(-value))
            slope_ref[:, at : at + wide] = sig * (1.0 + value * (1.0 - sig))

    return kernel_call(
        body,
        "gates",
        [shape((tokens, hidden), F32), shape((own, hidden), F32)],
        [place, gate],
        smem=1,
    )


def first_product(place, pieces, weight, part, weight_rows, name):
    gathered = not isinstance(pieces, list)
    at0, wide0 = part
    inner = weight.shape[1] if weight_rows else weight.shape[0]

    def multiply(tokens_ref, weight_ref, out_ref):
        for at, wide in spans(wide0, 256):
            cut = slice(at0 + at, at0 + at + wide)
            if weight_rows:
                value = lax.dot_general(
                    weight_ref[cut, :], tokens_ref[...], (((1,), (1,)), ((), ())), preferred_element_type=F32
                ).T
            else:
                value = jnp.dot(tokens_ref[...], weight_ref[:, cut], preferred_element_type=F32)
            out_ref[:, at : at + wide] = value

    if gathered:
        tokens = pieces.shape[0]

        def body(tokens_ref, weight_ref, out_ref):
            multiply(tokens_ref, weight_ref, out_ref)

        return kernel_call(
            body, name, [shape((tokens, wide0), F32)], [pieces, weight], flops=2 * tokens * inner * wide0
        )[0]

    count = len(pieces)
    rows = pieces[0].shape[0]
    tokens = rows * count
    direct = rows % 16 == 0

    def body(place_ref, *refs):
        piece_refs, (weight_ref, out_ref, tokens_ref), scratch = refs[:count], refs[count : count + 3], refs[count + 3 :]
        held = tokens_ref if direct else scratch[0]
        for k in range(count):
            at = pl.multiple_of(lax.bitwise_xor(place_ref[0], k) * rows, rows)
            held[pl.ds(at, rows), :] = piece_refs[k][...].astype(held.dtype)
        if not direct:
            tokens_ref[...] = held[...].astype(BF16)
        multiply(tokens_ref, weight_ref, out_ref)

    return kernel_call(
        body,
        name,
        [shape((tokens, wide0), F32), shape((tokens, inner), BF16)],
        [place] + pieces + [weight],
        flops=2 * tokens * inner * wide0,
        scratch=[] if direct else [pltpu.VMEM((tokens, inner), F32)],
        smem=1,
    )


def blend(silu, mine, theirs, parts, name):
    tokens, hidden = silu.shape
    count = len(parts)

    def body(silu_ref, *refs):
        out_ref = refs[-1]
        for k, (at0, wide0) in enumerate(parts):
            for at, wide in spans(wide0, 256):
                total = refs[k][:, at : at + wide] + refs[count + k][:, at : at + wide]
                out_ref[:, at0 + at : at0 + at + wide] = (silu_ref[:, at0 + at : at0 + at + wide] * total).astype(BF16)

    return kernel_call(body, name, [shape((tokens, hidden), BF16)], [silu] + mine + theirs)[0]


def second_product(place, values, weight, residual, part, weight_rows, blocks, name):
    tokens, hidden = values.shape
    rows = tokens // blocks
    at0, wide0 = part

    def body(place_ref, values_ref, weight_ref, residual_ref, *refs):
        outs, total_ref = refs[:blocks], refs[blocks]
        for at, wide in spans(wide0, 256):
            cut = slice(at0 + at, at0 + at + wide)
            if weight_rows:
                total = lax.dot_general(
                    weight_ref[cut, :], values_ref[...], (((1,), (1,)), ((), ())), preferred_element_type=F32
                ).T
            else:
                total = jnp.dot(values_ref[...], weight_ref[:, cut], preferred_element_type=F32)
            total_ref[:, at : at + wide] = total
        for k in range(blocks):
            start = pl.multiple_of(lax.bitwise_xor(place_ref[0], k) * rows, rows)
            piece = total_ref[pl.ds(start, rows), :]
            if k == 0:
                piece = piece + residual_ref[:, at0 : at0 + wide0].astype(F32)
            outs[k][...] = piece.astype(BF16)

    return kernel_call(
        body,
        name,
        [shape((rows, wide0), BF16)] * blocks,
        [place, values, weight, residual],
        flops=2 * tokens * hidden * wide0,
        scratch=[pltpu.VMEM((tokens, wide0), F32)],
        smem=1,
    )


def gate_gradient(place, slope, up_mine, up_theirs, back_mine, back_theirs, parts):
    own, hidden = slope.shape
    count = len(parts)

    def body(place_ref, slope_ref, *refs):
        out_ref = refs[-1]
        start = pl.multiple_of(place_ref[1] * own, own)
        rows = pl.ds(start, own)
        for k, (at0, wide0) in enumerate(parts):
            for at, wide in spans(wide0, 256):
                cut = slice(at, at + wide)
                up = refs[k][rows, cut] + refs[count + k][rows, cut]
                back = refs[2 * count + k][rows, cut] + refs[3 * count + k][rows, cut]
                whole = slice(at0 + at, at0 + at + wide)
                out_ref[:, whole] = (back * up * slope_ref[:, whole]).astype(BF16)

    return kernel_call(
        body,
        "gate_gradient",
        [shape((own, hidden), BF16)],
        [place, slope] + up_mine + up_theirs + back_mine + back_theirs,
        smem=1,
    )[0]


def collect(pieces, name):
    rows = pieces[0][0].shape[0]
    widths = [part[0].shape[1] for part in pieces]
    blocks = len(pieces[0])

    def body(*refs):
        out_ref = refs[-1]
        at = 0
        for p, wide in enumerate(widths):
            total = refs[p * blocks][...].astype(F32)
            for k in range(1, blocks):
                total = total + refs[p * blocks + k][...].astype(F32)
            out_ref[:, at : at + wide] = total.astype(BF16)
            at += wide

    return kernel_call(body, name, [shape((rows, sum(widths)), BF16)], [a for part in pieces for a in part])[0]


def shards(sections, cols, row_count, inputs, gate_pre, up_weight, down_weight, output_grad):
    own_x, own_g, gate = inputs[0], output_grad[0], gate_pre[0]
    place = jnp.stack([lax.axis_index("col"), lax.axis_index("row")]).astype(jnp.int32)

    def from_xor(value, k):
        return lax.ppermute(value, "col", [(c, c ^ k) for c in range(cols)])

    def to_block(value, k, step):
        pairs = [
            (s * cols + c, (s + step) % sections * cols + (c ^ k)) for s in range(sections) for c in range(cols)
        ]
        return lax.ppermute(value, ("section", "col"), pairs)

    def other_row(value):
        return lax.ppermute(value, "row", [(r, (r + 1) % row_count) for r in range(row_count)])

    hidden = gate.shape[1]
    hidden_parts = halves(hidden)
    width_parts = halves(own_x.shape[1])

    x_pieces = [own_x] + [from_xor(own_x, k) for k in range(1, cols)]
    silu, slope = gates(place, gate, row_count)
    late_g, silu, slope = lax.optimization_barrier((own_g, silu, slope))
    g_pieces = [own_g] + [from_xor(late_g, k) for k in range(1, cols)]

    def rounds(pieces, first_weight, second_weight, residual, weight_rows, step, name):
        part0, tokens = first_product(place, pieces, first_weight, hidden_parts[0], weight_rows, name + "_a")
        mine, theirs = [part0], [other_row(part0)]
        for part in hidden_parts[1:]:
            mine.append(first_product(place, tokens, first_weight, part, weight_rows, name + "_b"))
            theirs.append(other_row(mine[-1]))
        values = blend(silu, mine, theirs, hidden_parts, name + "_blend")
        arrived = []
        for part in width_parts:
            blocks = second_product(place, values, second_weight, residual, part, weight_rows, cols, name + "_out")
            arrived.append([to_block(block, k, step) for k, block in enumerate(blocks)])
        return mine, theirs, arrived

    up_mine, up_theirs, forward = rounds(x_pieces, up_weight, down_weight, own_x, False, 1, "fore")
    back_mine, back_theirs, backward = rounds(g_pieces, down_weight, up_weight, own_g, True, -1, "back")
    gate_grad = gate_gradient(place, slope, up_mine, up_theirs, back_mine, back_theirs, hidden_parts)
    handed_forward = collect(forward, "fore_collect")
    handed_back = collect(backward, "back_collect")
    return handed_forward[None], gate_grad[None], handed_back[None]


def solution(mesh):
    placed = (
        P("section", "col", "row"),
        P("section", None, "col"),
        P("row", "col"),
        P("col", "row"),
        P("section", "col", "row"),
    )
    sizes = mesh.shape
    return jax.shard_map(
        functools.partial(shards, sizes["section"], sizes["col"], sizes["row"]),
        mesh=mesh,
        in_specs=placed,
        out_specs=(
            P("section", "col", "row"),
            P("section", "row", "col"),
            P("section", "col", "row"),
        ),
        check_vma=False,
    )
```

time: 159 us -> 91.8 us (0.58)
  waiting for transfers between devices: 56.4 us -> 10.7 us
  starting transfers between devices: 4.12 us -> 45.3 us
  matrix products: 39.5 us -> 0 us
  blocking collectives: 38.9 us -> 0 us
  Pallas kernels: 0 us -> 21.5 us
  between operations: 13.8 us -> 0.82 us
  local copies, waits for them, and re-layouts: 1.32 us -> 13.3 us
  other arithmetic: 4.67 us -> 0.07 us
    reduce_scatter x4 -> x0, waiting for transfers between devices: 51.8 us -> none  [the longest x2 41.9 us: col_product(): lax.psum_scatter(lax.dot_general(gathered, matrix, (contract, ((), ())),...]
    ppermute x2 -> x26, starting transfers between devices: 3.96 us -> 45.3 us  [the longest x16 30.8 us: to_block(): return lax.ppermute(value, ('section', 'col'), pairs)]
    dot_general x4 -> x0, matrix products: 39.5 us -> none  [the longest x2 19.8 us: row_product(): lax.dot_general(gathered, matrix, (contract, ((), ())), preferred_element...]
    all_gather x4 -> x0, blocking collectives: 38.9 us -> none  [the longest x2 34 us: row_product(): gathered = lax.all_gather(pieces, 'col', axis=0, tiled=True)]
    pallas_call x0 -> x14, Pallas kernels: none -> 21.5 us  [kernel_call(): pl.pallas_call(body, name=name, out_shape=outs, in_specs=[SMEM] * smem +...]
    unnamed x8 -> x12, local copies, waits for them, and re-layouts: 1.32 us -> 13.3 us
    ppermute x2 -> x26, waiting for transfers between devices: 4.49 us -> 10.7 us  [the longest x6 7.04 us: from_xor(): return lax.ppermute(value, 'col', [(c, c ^ k) for c in range(cols)])]
    convert_element_type x3 -> x0, other arithmetic: 4.67 us -> none  [the longest x1 2.72 us: shards(): up_grad = (hidden_grad * gate_used * sigmoid_gate).astype(jnp.bfloat16)]
  transfers between devices with their start and end apart: 6 -> 26, of which waited for: 4 -> 2; matrix products, arithmetic and copies ran while one was open for 12% -> 0% of each run, Pallas kernels for 0% -> 23%
where the time goes in v1:
time: 91.8 us; the launch traced here: 91.6 us
  starting transfers between devices  45.3 us (49%)
  Pallas kernels  21.5 us (23%)
  local copies, waits for them, and re-layouts  13.3 us (14%)
  waiting for transfers between devices  10.7 us (12%)
    ppermute x16, starting transfers between devices, to_block(): return lax.ppermute(value, ('section', 'col'), pairs)  30.8 us
    pallas_call x14, Pallas kernels, kernel_call(): pl.pallas_call(body, name=name, out_shape=outs, in_specs=[SMEM] * smem +...  21.5 us
    ppermute x6, starting transfers between devices, from_xor(): return lax.ppermute(value, 'col', [(c, c ^ k) for c in range(cols)])  13.4 us
    unnamed x12, local copies, waits for them, and re-layouts  13.3 us
    ppermute x6, waiting for transfers between devices, from_xor(): return lax.ppermute(value, 'col', [(c, c ^ k) for c in range(cols)])  7.04 us
    ppermute x16, waiting for transfers between devices, to_block(): return lax.ppermute(value, ('section', 'col'), pairs)  3.61 us
  transfers between devices with their start and end apart: 26, of which 2 were waited for; matrix products, arithmetic and copies ran while one was open for 0% of the time, Pallas kernels for 23%

profile of v1, /device:TPU:0, one launch (start us, length us, event | category | flops | bytes accessed | tf_op | source)
XLA Modules:
  0.0 91.6 jit_solution(8303758430603454986)
XLA Ops:
  0.6 5.1 %collective-permute-start.2 = (bf16[32,2048]{1,0:T(8,128)(2,1)}, bf16[32,2048]{1,0:T(8,128)(2,1)S(1)}, u32[]{:S(2)}, u32[]{:S(2)}) collective-permute-start(bf16[32,2048]{1,0:T(8,128)(2,1)} %bitcast.8), channel_id=1, source_target_pairs={{0,3},{1,2},{2,1},{3,0},{4,7},{5,6},{6,5},{7,4},{8,11},{9,10},{10,... | collective-permute-start | bytes 393224 | tf_op jit(solution)/shard_map/ppermute | solution.py:215
  6.5 1.2 %copy-done.5 = bf16[1,128,3584]{2,1,0:T(8,128)(2,1)S(1)} copy-done((bf16[1,128,3584]{2,1,0:T(8,128)(2,1)S(1)}, bf16[1,128,3584]{2,1,0:T(8,128)(2,1)}, u32[]{:S(2)}) %copy-start.5) | copy-done | bytes 917528
  7.6 1.3 %gates.1 = (f32[128,3584]{1,0:T(8,128)S(1)}, f32[64,3584]{1,0:T(8,128)S(1)}) custom-call(s32[2]{0:T(128)S(1)} %pad_add_fusion.place_ref, bf16[128,3584]{1,0:T(8,128)(2,1)S(1)} %bitcast.20), custom_call_target="tpu_custom_call" | custom-call | bytes 917512 | tf_op jit(solution)/shard_map/gates/pallas_call | solution.py:28
  9.0 3.8 %collective-permute-start.15 = (bf16[32,2048]{1,0:T(8,128)(2,1)}, bf16[32,2048]{1,0:T(8,128)(2,1)S(1)}, u32[]{:S(2)}, u32[]{:S(2)}) collective-permute-start(bf16[32,2048]{1,0:T(8,128)(2,1)} %bitcast.14), channel_id=1, source_target_pairs={{0,3},{1,2},{2,1},{3,0},{4,7},{5,6},{6,5},{7,4},{8,11},{9,10},{10,... | collective-permute-start | bytes 393224 | tf_op jit(solution)/shard_map/ppermute | solution.py:215
  12.8 3.8 %collective-permute-start.13 = (bf16[32,2048]{1,0:T(8,128)(2,1)}, bf16[32,2048]{1,0:T(8,128)(2,1)S(1)}, u32[]{:S(2)}, u32[]{:S(2)}) collective-permute-start(bf16[32,2048]{1,0:T(8,128)(2,1)} %bitcast.16), channel_id=1, source_target_pairs={{0,1},{1,0},{2,3},{3,2},{4,5},{5,4},{6,7},{7,6},{8,9},{9,8},{10,11... | collective-permute-start | bytes 393224 | tf_op jit(solution)/shard_map/ppermute | solution.py:215
  16.6 7.0 %collective-permute-done.1.refs_2_ = bf16[32,2048]{1,0:T(8,128)(2,1)S(1)} collective-permute-done((bf16[32,2048]{1,0:T(8,128)(2,1)}, bf16[32,2048]{1,0:T(8,128)(2,1)S(1)}, u32[]{:S(2)}, u32[]{:S(2)}) %collective-permute-start.1) | collective-permute-done | bytes 131104 | tf_op jit(solution)/shard_map/ppermute | solution.py:215
  23.6 5.2 %copy-done = bf16[2048,3584]{1,0:T(8,128)(2,1)S(1)} copy-done((bf16[2048,3584]{1,0:T(8,128)(2,1)S(1)}, bf16[2048,3584]{1,0:T(8,128)(2,1)}, u32[]{:S(2)}) %copy-start) | copy-done | bytes 14680088
  28.8 0.9 copy-done.3
  29.7 1.7 %fore_a.1 = (f32[128,1792]{1,0:T(8,128)S(1)}, bf16[128,2048]{1,0:T(8,128)(2,1)S(1)}) custom-call(s32[2]{0:T(128)S(1)} %pad_add_fusion.place_ref, bf16[32,2048]{1,0:T(8,128)(2,1)S(1)} %bitcast.11, bf16[32,2048]{1,0:T(8,128)(2,1)S(1)} %collective-permute-done.refs_1_, bf16[32,2048]{1,0:T(8,128)(2,1)S(1)} %collective-permute-done.1.refs_2_, ...), custom_call_target="tpu_custom_call" | custom-call | flops 939524096 | bytes 15204360 | tf_op jit(solution)/shard_map/fore_a/pallas_call | solution.py:28
  31.4 3.5 %copy-done.1 = bf16[2048,3584]{1,0:T(8,128)(2,1)S(1)} copy-done((bf16[2048,3584]{1,0:T(8,128)(2,1)S(1)}, bf16[2048,3584]{1,0:T(8,128)(2,1)}, u32[]{:S(2)}) %copy-start.1) | copy-done | bytes 14680088
  34.9 1.1 %fore_b.1.refs_1_ = f32[128,1792]{1,0:T(8,128)S(1)} custom-call(bf16[128,2048]{1,0:T(8,128)(2,1)S(1)} %get-tuple-element.32.tokens_ref, bf16[2048,3584]{1,0:T(8,128)(2,1)S(1)} %copy-done.1), custom_call_target="tpu_custom_call" | custom-call | flops 939524096 | bytes 15204352 | tf_op jit(solution)/shard_map/fore_b/pallas_call | solution.py:28
  36.6 2.5 %copy-done.2 = bf16[3584,2048]{1,0:T(8,128)(2,1)S(1)} copy-done((bf16[3584,2048]{1,0:T(8,128)(2,1)S(1)}, bf16[3584,2048]{1,0:T(8,128)(2,1)}, u32[]{:S(2)}) %copy-start.2) | copy-done | bytes 14680088
  39.1 2.7 %back_a.1 = (f32[128,1792]{1,0:T(8,128)S(1)}, bf16[128,2048]{1,0:T(8,128)(2,1)S(1)}) custom-call(s32[2]{0:T(128)S(1)} %pad_add_fusion.place_ref, bf16[32,2048]{1,0:T(8,128)(2,1)S(1)} %bitcast.17, bf16[32,2048]{1,0:T(8,128)(2,1)S(1)} %collective-permute-done.13.refs_1_, bf16[32,2048]{1,0:T(8,128)(2,1)S(1)} %collective-permute-done.14.refs_2_, ...), custom_call_target="tpu_custom_call" | custom-call | flops 939524096 | bytes 15204360 | tf_op jit(solution)/shard_map/back_a/pallas_call | solution.py:28
  41.9 2.2 %back_b.1.refs_5_.refs_1_ = f32[128,1792]{1,0:T(8,128)S(1)} custom-call(bf16[128,2048]{1,0:T(8,128)(2,1)S(1)} %get-tuple-element.44.tokens_ref, bf16[3584,2048]{1,0:T(8,128)(2,1)S(1)} %copy-done.2), custom_call_target="tpu_custom_call" | custom-call | flops 939524096 | bytes 15204352 | tf_op jit(solution)/shard_map/back_b/pallas_call | solution.py:28
  44.8 1.8 %fore_out.3 = (bf16[32,1024]{1,0:T(8,128)(2,1)S(1)}, bf16[32,1024]{1,0:T(8,128)(2,1)S(1)}, bf16[32,1024]{1,0:T(8,128)(2,1)S(1)}, bf16[32,1024]{1,0:T(8,128)(2,1)S(1)}) custom-call(s32[2]{0:T(128)S(1)} %pad_add_fusion.place_ref, bf16[128,3584]{1,0:T(8,128)(2,1)S(1)} %fore_blend.1.values_ref, bf16[3584,2048]{1,0:T(8,128)(2,1)S(1)} %copy-done.2, ...), custom_call_target="tpu_custom_call" | custom-call | flops 939524096 | bytes 15728648 | tf_op jit(solution)/shard_map/fore_out/pallas_call | solution.py:28
  46.6 1.5 %collective-permute-start.9 = (bf16[32,1024]{1,0:T(8,128)(2,1)S(1)}, bf16[32,1024]{1,0:T(8,128)(2,1)S(1)}, u32[]{:S(2)}, u32[]{:S(2)}) collective-permute-start(bf16[32,1024]{1,0:T(8,128)(2,1)S(1)} %get-tuple-element.37), channel_id=1, source_target_pairs={{0,8},{1,9},{2,10},{3,11},{8,16},{9,17},{10,18},{11,19},{16,24},{1... | collective-permute-start | bytes 196616 | tf_op jit(solution)/shard_map/ppermute | solution.py:221
  49.1 4.2 %collective-permute-start.11 = (bf16[32,1024]{1,0:T(8,128)(2,1)S(1)}, bf16[32,1024]{1,0:T(8,128)(2,1)S(1)}, u32[]{:S(2)}, u32[]{:S(2)}) collective-permute-start(bf16[32,1024]{1,0:T(8,128)(2,1)S(1)} %get-tuple-element.39), channel_id=1, source_target_pairs={{0,10},{1,11},{2,8},{3,9},{8,18},{9,19},{10,16},{11,17},{16,26},{1... | collective-permute-start | bytes 196616 | tf_op jit(solution)/shard_map/ppermute | solution.py:221
  53.3 1.8 %fore_out.2 = (bf16[32,1024]{1,0:T(8,128)(2,1)S(1)}, bf16[32,1024]{1,0:T(8,128)(2,1)S(1)}, bf16[32,1024]{1,0:T(8,128)(2,1)S(1)}, bf16[32,1024]{1,0:T(8,128)(2,1)S(1)}) custom-call(s32[2]{0:T(128)S(1)} %pad_add_fusion.place_ref, bf16[128,3584]{1,0:T(8,128)(2,1)S(1)} %fore_blend.1.values_ref, bf16[3584,2048]{1,0:T(8,128)(2,1)S(1)} %copy-done.2, ...), custom_call_target="tpu_custom_call" | custom-call | flops 939524096 | bytes 15728648 | tf_op jit(solution)/shard_map/fore_out/pallas_call | solution.py:28
  55.1 1.1 %collective-permute-start.12 = (bf16[32,1024]{1,0:T(8,128)(2,1)S(1)}, bf16[32,1024]{1,0:T(8,128)(2,1)S(1)}, u32[]{:S(2)}, u32[]{:S(2)}) collective-permute-start(bf16[32,1024]{1,0:T(8,128)(2,1)S(1)} %get-tuple-element.40), channel_id=1, source_target_pairs={{0,11},{1,10},{2,9},{3,8},{8,19},{9,18},{10,17},{11,16},{16,27},{1... | collective-permute-start | bytes 196616 | tf_op jit(solution)/shard_map/ppermute | solution.py:221
  56.2 1.5 %collective-permute-start.5 = (bf16[32,1024]{1,0:T(8,128)(2,1)S(1)}, bf16[32,1024]{1,0:T(8,128)(2,1)S(1)}, u32[]{:S(2)}, u32[]{:S(2)}) collective-permute-start(bf16[32,1024]{1,0:T(8,128)(2,1)S(1)} %get-tuple-element.33), channel_id=1, source_target_pairs={{0,8},{1,9},{2,10},{3,11},{8,16},{9,17},{10,18},{11,19},{16,24},{1... | collective-permute-start | bytes 196616 | tf_op jit(solution)/shard_map/ppermute | solution.py:221
  58.0 2.7 %back_out.3 = (bf16[32,1024]{1,0:T(8,128)(2,1)S(1)}, bf16[32,1024]{1,0:T(8,128)(2,1)S(1)}, bf16[32,1024]{1,0:T(8,128)(2,1)S(1)}, bf16[32,1024]{1,0:T(8,128)(2,1)S(1)}) custom-call(s32[2]{0:T(128)S(1)} %pad_add_fusion.place_ref, bf16[128,3584]{1,0:T(8,128)(2,1)S(1)} %back_blend.1.values_ref, bf16[2048,3584]{1,0:T(8,128)(2,1)S(1)} %copy-done.1, ...), custom_call_target="tpu_custom_call" | custom-call | flops 939524096 | bytes 15728648 | tf_op jit(solution)/shard_map/back_out/pallas_call | solution.py:28
  60.8 5.1 %collective-permute-start.7 = (bf16[32,1024]{1,0:T(8,128)(2,1)S(1)}, bf16[32,1024]{1,0:T(8,128)(2,1)S(1)}, u32[]{:S(2)}, u32[]{:S(2)}) collective-permute-start(bf16[32,1024]{1,0:T(8,128)(2,1)S(1)} %get-tuple-element.35), channel_id=1, source_target_pairs={{0,10},{1,11},{2,8},{3,9},{8,18},{9,19},{10,16},{11,17},{16,26},{1... | collective-permute-start | bytes 196616 | tf_op jit(solution)/shard_map/ppermute | solution.py:221
  65.9 1.1 %collective-permute-start.8 = (bf16[32,1024]{1,0:T(8,128)(2,1)S(1)}, bf16[32,1024]{1,0:T(8,128)(2,1)S(1)}, u32[]{:S(2)}, u32[]{:S(2)}) collective-permute-start(bf16[32,1024]{1,0:T(8,128)(2,1)S(1)} %get-tuple-element.36), channel_id=1, source_target_pairs={{0,11},{1,10},{2,9},{3,8},{8,19},{9,18},{10,17},{11,16},{16,27},{1... | collective-permute-start | bytes 196616 | tf_op jit(solution)/shard_map/ppermute | solution.py:221
  67.0 2.4 %collective-permute-start.22 = (bf16[32,1024]{1,0:T(8,128)(2,1)S(1)}, bf16[32,1024]{1,0:T(8,128)(2,1)S(1)}, u32[]{:S(2)}, u32[]{:S(2)}) collective-permute-start(bf16[32,1024]{1,0:T(8,128)(2,1)S(1)} %get-tuple-element.49), channel_id=1, source_target_pairs={{0,24},{1,25},{2,26},{3,27},{8,0},{9,1},{10,2},{11,3},{16,8},{17,9... | collective-permute-start | bytes 196616 | tf_op jit(solution)/shard_map/ppermute | solution.py:221
  69.4 4.1 %collective-permute-start.24 = (bf16[32,1024]{1,0:T(8,128)(2,1)S(1)}, bf16[32,1024]{1,0:T(8,128)(2,1)S(1)}, u32[]{:S(2)}, u32[]{:S(2)}) collective-permute-start(bf16[32,1024]{1,0:T(8,128)(2,1)S(1)} %get-tuple-element.51), channel_id=1, source_target_pairs={{0,26},{1,27},{2,24},{3,25},{8,2},{9,3},{10,0},{11,1},{16,10},{17,... | collective-permute-start | bytes 196616 | tf_op jit(solution)/shard_map/ppermute | solution.py:221
  73.5 2.7 %back_out.2 = (bf16[32,1024]{1,0:T(8,128)(2,1)S(1)}, bf16[32,1024]{1,0:T(8,128)(2,1)S(1)}, bf16[32,1024]{1,0:T(8,128)(2,1)S(1)}, bf16[32,1024]{1,0:T(8,128)(2,1)S(1)}) custom-call(s32[2]{0:T(128)S(1)} %pad_add_fusion.place_ref, bf16[128,3584]{1,0:T(8,128)(2,1)S(1)} %back_blend.1.values_ref, bf16[2048,3584]{1,0:T(8,128)(2,1)S(1)} %copy-done.1, ...), custom_call_target="tpu_custom_call" | custom-call | flops 939524096 | bytes 15728648 | tf_op jit(solution)/shard_map/back_out/pallas_call | solution.py:28
  76.2 1.2 %collective-permute-start.25 = (bf16[32,1024]{1,0:T(8,128)(2,1)S(1)}, bf16[32,1024]{1,0:T(8,128)(2,1)S(1)}, u32[]{:S(2)}, u32[]{:S(2)}) collective-permute-start(bf16[32,1024]{1,0:T(8,128)(2,1)S(1)} %get-tuple-element.52), channel_id=1, source_target_pairs={{0,27},{1,26},{2,25},{3,24},{8,3},{9,2},{10,1},{11,0},{16,11},{17,... | collective-permute-start | bytes 196616 | tf_op jit(solution)/shard_map/ppermute | solution.py:221
  77.4 2.4 %collective-permute-start.18 = (bf16[32,1024]{1,0:T(8,128)(2,1)S(1)}, bf16[32,1024]{1,0:T(8,128)(2,1)S(1)}, u32[]{:S(2)}, u32[]{:S(2)}) collective-permute-start(bf16[32,1024]{1,0:T(8,128)(2,1)S(1)} %get-tuple-element.45), channel_id=1, source_target_pairs={{0,24},{1,25},{2,26},{3,27},{8,0},{9,1},{10,2},{11,3},{16,8},{17,9... | collective-permute-start | bytes 196616 | tf_op jit(solution)/shard_map/ppermute | solution.py:221
  79.9 4.1 %collective-permute-start.20 = (bf16[32,1024]{1,0:T(8,128)(2,1)S(1)}, bf16[32,1024]{1,0:T(8,128)(2,1)S(1)}, u32[]{:S(2)}, u32[]{:S(2)}) collective-permute-start(bf16[32,1024]{1,0:T(8,128)(2,1)S(1)} %get-tuple-element.47), channel_id=1, source_target_pairs={{0,26},{1,27},{2,24},{3,25},{8,2},{9,3},{10,0},{11,1},{16,10},{17,... | collective-permute-start | bytes 196616 | tf_op jit(solution)/shard_map/ppermute | solution.py:221
  83.9 1.1 %collective-permute-start.21 = (bf16[32,1024]{1,0:T(8,128)(2,1)S(1)}, bf16[32,1024]{1,0:T(8,128)(2,1)S(1)}, u32[]{:S(2)}, u32[]{:S(2)}) collective-permute-start(bf16[32,1024]{1,0:T(8,128)(2,1)S(1)} %get-tuple-element.48), channel_id=1, source_target_pairs={{0,27},{1,26},{2,25},{3,24},{8,3},{9,2},{10,1},{11,0},{16,11},{17,... | collective-permute-start | bytes 196616 | tf_op jit(solution)/shard_map/ppermute | solution.py:221
  85.1 1.5 %gate_gradient.1 = bf16[64,3584]{1,0:T(8,128)(2,1)} custom-call(s32[2]{0:T(128)S(1)} %pad_add_fusion.place_ref, f32[64,3584]{1,0:T(8,128)S(1)} %get-tuple-element.41.slope_ref, f32[128,1792]{1,0:T(8,128)S(1)} %get-tuple-element.31.refs_0_, f32[128,1792]{1,0:T(8,128)S(1)} %fore_b.1.refs_1_, f32[128,1792]{1,0:T(8,128)S(1)} %collective-permute-done.3.refs_2_, ...), custom_call_target="tpu_custom_call" | custom-call | bytes 8257544 | tf_op jit(solution)/shard_map/gate_gradient/pallas_call | solution.py:28
  87.3 3.6 %collective-permute-done.21.refs_3_ = bf16[32,1024]{1,0:T(8,128)(2,1)S(1)} collective-permute-done((bf16[32,1024]{1,0:T(8,128)(2,1)S(1)}, bf16[32,1024]{1,0:T(8,128)(2,1)S(1)}, u32[]{:S(2)}, u32[]{:S(2)}) %collective-permute-start.21) | collective-permute-done | bytes 65568 | tf_op jit(solution)/shard_map/ppermute | solution.py:221
  (47 shorter events, 4.8 us)
Async XLA Ops:
  0.6 12.2 %collective-permute-start.2 = (bf16[32,2048]{1,0:T(8,128)(2,1)}, bf16[32,2048]{1,0:T(8,128)(2,1)S(1)}, u32[]{:S(2)}, u32[]{:S(2)}) collective-permute-start(bf16[32,2048]{1,0:T(8,128)(2,1)} %bitcast.8), channel_id=1, source_target_pairs={{0,3},{1,2},{2,1},{3,0},{4,7},{5,6},{6,5},{7,4},{8,11},{9,10},{10,... | collective-permute-start | bytes 393224 | tf_op jit(solution)/shard_map/ppermute | solution.py:215
  5.7 17.9 %collective-permute-start.1 = (bf16[32,2048]{1,0:T(8,128)(2,1)}, bf16[32,2048]{1,0:T(8,128)(2,1)S(1)}, u32[]{:S(2)}, u32[]{:S(2)}) collective-permute-start(bf16[32,2048]{1,0:T(8,128)(2,1)} %bitcast.9), channel_id=1, source_target_pairs={{0,2},{1,3},{2,0},{3,1},{4,6},{5,7},{6,4},{7,5},{8,10},{9,11},{10,... | collective-permute-start | bytes 393224 | tf_op jit(solution)/shard_map/ppermute | solution.py:215
  5.7 17.9 %collective-permute-start = (bf16[32,2048]{1,0:T(8,128)(2,1)}, bf16[32,2048]{1,0:T(8,128)(2,1)S(1)}, u32[]{:S(2)}, u32[]{:S(2)}) collective-permute-start(bf16[32,2048]{1,0:T(8,128)(2,1)} %bitcast.10), channel_id=1, source_target_pairs={{0,1},{1,0},{2,3},{3,2},{4,5},{5,4},{6,7},{7,6},{8,9},{9,8},{10,11... | collective-permute-start | bytes 393224 | tf_op jit(solution)/shard_map/ppermute | solution.py:215
  6.5 1.2 %copy-start.5 = (bf16[1,128,3584]{2,1,0:T(8,128)(2,1)S(1)}, bf16[1,128,3584]{2,1,0:T(8,128)(2,1)}, u32[]{:S(2)}) copy-start(bf16[1,128,3584]{2,1,0:T(8,128)(2,1)} %param.6) | copy-start | bytes 2752516
  7.6 28.9 %copy-start.4 = (bf16[1,32,2048]{2,1,0:T(8,128)(2,1)S(1)}, bf16[1,32,2048]{2,1,0:T(8,128)(2,1)}, u32[]{:S(2)}) copy-start(bf16[1,32,2048]{2,1,0:T(8,128)(2,1)} %param.9) | copy-start | bytes 393220
  9.0 27.6 %collective-permute-start.15 = (bf16[32,2048]{1,0:T(8,128)(2,1)}, bf16[32,2048]{1,0:T(8,128)(2,1)S(1)}, u32[]{:S(2)}, u32[]{:S(2)}) collective-permute-start(bf16[32,2048]{1,0:T(8,128)(2,1)} %bitcast.14), channel_id=1, source_target_pairs={{0,3},{1,2},{2,1},{3,0},{4,7},{5,6},{6,5},{7,4},{8,11},{9,10},{10,... | collective-permute-start | bytes 393224 | tf_op jit(solution)/shard_map/ppermute | solution.py:215
  12.8 23.8 %collective-permute-start.14 = (bf16[32,2048]{1,0:T(8,128)(2,1)}, bf16[32,2048]{1,0:T(8,128)(2,1)S(1)}, u32[]{:S(2)}, u32[]{:S(2)}) collective-permute-start(bf16[32,2048]{1,0:T(8,128)(2,1)} %bitcast.15), channel_id=1, source_target_pairs={{0,2},{1,3},{2,0},{3,1},{4,6},{5,7},{6,4},{7,5},{8,10},{9,11},{10,... | collective-permute-start | bytes 393224 | tf_op jit(solution)/shard_map/ppermute | solution.py:215
  12.8 23.8 %collective-permute-start.13 = (bf16[32,2048]{1,0:T(8,128)(2,1)}, bf16[32,2048]{1,0:T(8,128)(2,1)S(1)}, u32[]{:S(2)}, u32[]{:S(2)}) collective-permute-start(bf16[32,2048]{1,0:T(8,128)(2,1)} %bitcast.16), channel_id=1, source_target_pairs={{0,1},{1,0},{2,3},{3,2},{4,5},{5,4},{6,7},{7,6},{8,9},{9,8},{10,11... | collective-permute-start | bytes 393224 | tf_op jit(solution)/shard_map/ppermute | solution.py:215
  23.6 5.2 %copy-start = (bf16[2048,3584]{1,0:T(8,128)(2,1)S(1)}, bf16[2048,3584]{1,0:T(8,128)(2,1)}, u32[]{:S(2)}) copy-start(bf16[2048,3584]{1,0:T(8,128)(2,1)} %weight_ref.11) | copy-start | bytes 44040196
  28.8 0.9 copy-start.3
  29.7 5.2 %copy-start.1 = (bf16[2048,3584]{1,0:T(8,128)(2,1)S(1)}, bf16[2048,3584]{1,0:T(8,128)(2,1)}, u32[]{:S(2)}) copy-start(bf16[2048,3584]{1,0:T(8,128)(2,1)} %weight_ref.11) | copy-start | bytes 44040196
  29.7 9.4 %copy-start.2 = (bf16[3584,2048]{1,0:T(8,128)(2,1)S(1)}, bf16[3584,2048]{1,0:T(8,128)(2,1)}, u32[]{:S(2)}) copy-start(bf16[3584,2048]{1,0:T(8,128)(2,1)} %weight_ref.9) | copy-start | bytes 44040196
  36.0 8.6 %collective-permute-start.4 = (f32[128,1792]{1,0:T(8,128)S(1)}, f32[128,1792]{1,0:T(8,128)S(1)}, u32[]{:S(2)}, u32[]{:S(2)}) collective-permute-start(f32[128,1792]{1,0:T(8,128)S(1)} %fore_b.1.refs_1_), channel_id=1, source_target_pairs={{0,4},{4,0},{1,5},{5,1},{2,6},{6,2},{3,7},{7,3},{8,12},{12,8},{9,1... | collective-permute-start | bytes 2752520 | tf_op jit(solution)/shard_map/ppermute | solution.py:224
  36.1 8.5 %collective-permute-start.3 = (f32[128,1792]{1,0:T(8,128)S(1)}, f32[128,1792]{1,0:T(8,128)S(1)}, u32[]{:S(2)}, u32[]{:S(2)}) collective-permute-start(f32[128,1792]{1,0:T(8,128)S(1)} %get-tuple-element.31.refs_0_), channel_id=1, source_target_pairs={{0,4},{4,0},{1,5},{5,1},{2,6},{6,2},{3,7},{7,3},{8,12},{12,8},{9,1... | collective-permute-start | bytes 2752520 | tf_op jit(solution)/shard_map/ppermute | solution.py:224
  44.0 11.0 %collective-permute-start.17 = (f32[128,1792]{1,0:T(8,128)S(1)}, f32[128,1792]{1,0:T(8,128)S(1)}, u32[]{:S(2)}, u32[]{:S(2)}) collective-permute-start(f32[128,1792]{1,0:T(8,128)S(1)} %back_b.1.refs_5_.refs_1_), channel_id=1, source_target_pairs={{0,4},{4,0},{1,5},{5,1},{2,6},{6,2},{3,7},{7,3},{8,12},{12,8},{9,1... | collective-permute-start | bytes 2752520 | tf_op jit(solution)/shard_map/ppermute | solution.py:224
  44.1 12.1 %collective-permute-start.16 = (f32[128,1792]{1,0:T(8,128)S(1)}, f32[128,1792]{1,0:T(8,128)S(1)}, u32[]{:S(2)}, u32[]{:S(2)}) collective-permute-start(f32[128,1792]{1,0:T(8,128)S(1)} %get-tuple-element.43.refs_4_.refs_0_), channel_id=1, source_target_pairs={{0,4},{4,0},{1,5},{5,1},{2,6},{6,2},{3,7},{7,3},{8,12},{12,8},{9,1... | collective-permute-start | bytes 2752520 | tf_op jit(solution)/shard_map/ppermute | solution.py:224
  46.6 11.3 %collective-permute-start.9 = (bf16[32,1024]{1,0:T(8,128)(2,1)S(1)}, bf16[32,1024]{1,0:T(8,128)(2,1)S(1)}, u32[]{:S(2)}, u32[]{:S(2)}) collective-permute-start(bf16[32,1024]{1,0:T(8,128)(2,1)S(1)} %get-tuple-element.37), channel_id=1, source_target_pairs={{0,8},{1,9},{2,10},{3,11},{8,16},{9,17},{10,18},{11,19},{16,24},{1... | collective-permute-start | bytes 196616 | tf_op jit(solution)/shard_map/ppermute | solution.py:221
  48.2 12.6 %collective-permute-start.10 = (bf16[32,1024]{1,0:T(8,128)(2,1)S(1)}, bf16[32,1024]{1,0:T(8,128)(2,1)S(1)}, u32[]{:S(2)}, u32[]{:S(2)}) collective-permute-start(bf16[32,1024]{1,0:T(8,128)(2,1)S(1)} %get-tuple-element.38), channel_id=1, source_target_pairs={{0,9},{1,8},{2,11},{3,10},{8,17},{9,16},{10,19},{11,18},{16,25},{1... | collective-permute-start | bytes 196616 | tf_op jit(solution)/shard_map/ppermute | solution.py:221
  49.1 16.8 %collective-permute-start.11 = (bf16[32,1024]{1,0:T(8,128)(2,1)S(1)}, bf16[32,1024]{1,0:T(8,128)(2,1)S(1)}, u32[]{:S(2)}, u32[]{:S(2)}) collective-permute-start(bf16[32,1024]{1,0:T(8,128)(2,1)S(1)} %get-tuple-element.39), channel_id=1, source_target_pairs={{0,10},{1,11},{2,8},{3,9},{8,18},{9,19},{10,16},{11,17},{16,26},{1... | collective-permute-start | bytes 196616 | tf_op jit(solution)/shard_map/ppermute | solution.py:221
  55.1 11.9 %collective-permute-start.12 = (bf16[32,1024]{1,0:T(8,128)(2,1)S(1)}, bf16[32,1024]{1,0:T(8,128)(2,1)S(1)}, u32[]{:S(2)}, u32[]{:S(2)}) collective-permute-start(bf16[32,1024]{1,0:T(8,128)(2,1)S(1)} %get-tuple-element.40), channel_id=1, source_target_pairs={{0,11},{1,10},{2,9},{3,8},{8,19},{9,18},{10,17},{11,16},{16,27},{1... | collective-permute-start | bytes 196616 | tf_op jit(solution)/shard_map/ppermute | solution.py:221
  56.2 13.2 %collective-permute-start.5 = (bf16[32,1024]{1,0:T(8,128)(2,1)S(1)}, bf16[32,1024]{1,0:T(8,128)(2,1)S(1)}, u32[]{:S(2)}, u32[]{:S(2)}) collective-permute-start(bf16[32,1024]{1,0:T(8,128)(2,1)S(1)} %get-tuple-element.33), channel_id=1, source_target_pairs={{0,8},{1,9},{2,10},{3,11},{8,16},{9,17},{10,18},{11,19},{16,24},{1... | collective-permute-start | bytes 196616 | tf_op jit(solution)/shard_map/ppermute | solution.py:221
  57.9 11.5 %collective-permute-start.6 = (bf16[32,1024]{1,0:T(8,128)(2,1)S(1)}, bf16[32,1024]{1,0:T(8,128)(2,1)S(1)}, u32[]{:S(2)}, u32[]{:S(2)}) collective-permute-start(bf16[32,1024]{1,0:T(8,128)(2,1)S(1)} %get-tuple-element.34), channel_id=1, source_target_pairs={{0,9},{1,8},{2,11},{3,10},{8,17},{9,16},{10,19},{11,18},{16,25},{1... | collective-permute-start | bytes 196616 | tf_op jit(solution)/shard_map/ppermute | solution.py:221
  60.8 15.5 %collective-permute-start.7 = (bf16[32,1024]{1,0:T(8,128)(2,1)S(1)}, bf16[32,1024]{1,0:T(8,128)(2,1)S(1)}, u32[]{:S(2)}, u32[]{:S(2)}) collective-permute-start(bf16[32,1024]{1,0:T(8,128)(2,1)S(1)} %get-tuple-element.35), channel_id=1, source_target_pairs={{0,10},{1,11},{2,8},{3,9},{8,18},{9,19},{10,16},{11,17},{16,26},{1... | collective-permute-start | bytes 196616 | tf_op jit(solution)/shard_map/ppermute | solution.py:221
  65.9 11.5 %collective-permute-start.8 = (bf16[32,1024]{1,0:T(8,128)(2,1)S(1)}, bf16[32,1024]{1,0:T(8,128)(2,1)S(1)}, u32[]{:S(2)}, u32[]{:S(2)}) collective-permute-start(bf16[32,1024]{1,0:T(8,128)(2,1)S(1)} %get-tuple-element.36), channel_id=1, source_target_pairs={{0,11},{1,10},{2,9},{3,8},{8,19},{9,18},{10,17},{11,16},{16,27},{1... | collective-permute-start | bytes 196616 | tf_op jit(solution)/shard_map/ppermute | solution.py:221
  67.0 12.9 %collective-permute-start.22 = (bf16[32,1024]{1,0:T(8,128)(2,1)S(1)}, bf16[32,1024]{1,0:T(8,128)(2,1)S(1)}, u32[]{:S(2)}, u32[]{:S(2)}) collective-permute-start(bf16[32,1024]{1,0:T(8,128)(2,1)S(1)} %get-tuple-element.49), channel_id=1, source_target_pairs={{0,24},{1,25},{2,26},{3,27},{8,0},{9,1},{10,2},{11,3},{16,8},{17,9... | collective-permute-start | bytes 196616 | tf_op jit(solution)/shard_map/ppermute | solution.py:221
  69.4 10.5 %collective-permute-start.23 = (bf16[32,1024]{1,0:T(8,128)(2,1)S(1)}, bf16[32,1024]{1,0:T(8,128)(2,1)S(1)}, u32[]{:S(2)}, u32[]{:S(2)}) collective-permute-start(bf16[32,1024]{1,0:T(8,128)(2,1)S(1)} %get-tuple-element.50), channel_id=1, source_target_pairs={{0,25},{1,24},{2,27},{3,26},{8,1},{9,0},{10,3},{11,2},{16,9},{17,8... | collective-permute-start | bytes 196616 | tf_op jit(solution)/shard_map/ppermute | solution.py:221
  69.4 14.5 %collective-permute-start.24 = (bf16[32,1024]{1,0:T(8,128)(2,1)S(1)}, bf16[32,1024]{1,0:T(8,128)(2,1)S(1)}, u32[]{:S(2)}, u32[]{:S(2)}) collective-permute-start(bf16[32,1024]{1,0:T(8,128)(2,1)S(1)} %get-tuple-element.51), channel_id=1, source_target_pairs={{0,26},{1,27},{2,24},{3,25},{8,2},{9,3},{10,0},{11,1},{16,10},{17,... | collective-permute-start | bytes 196616 | tf_op jit(solution)/shard_map/ppermute | solution.py:221
  76.2 11.1 %collective-permute-start.25 = (bf16[32,1024]{1,0:T(8,128)(2,1)S(1)}, bf16[32,1024]{1,0:T(8,128)(2,1)S(1)}, u32[]{:S(2)}, u32[]{:S(2)}) collective-permute-start(bf16[32,1024]{1,0:T(8,128)(2,1)S(1)} %get-tuple-element.52), channel_id=1, source_target_pairs={{0,27},{1,26},{2,25},{3,24},{8,3},{9,2},{10,1},{11,0},{16,11},{17,... | collective-permute-start | bytes 196616 | tf_op jit(solution)/shard_map/ppermute | solution.py:221
  77.4 9.9 %collective-permute-start.18 = (bf16[32,1024]{1,0:T(8,128)(2,1)S(1)}, bf16[32,1024]{1,0:T(8,128)(2,1)S(1)}, u32[]{:S(2)}, u32[]{:S(2)}) collective-permute-start(bf16[32,1024]{1,0:T(8,128)(2,1)S(1)} %get-tuple-element.45), channel_id=1, source_target_pairs={{0,24},{1,25},{2,26},{3,27},{8,0},{9,1},{10,2},{11,3},{16,8},{17,9... | collective-permute-start | bytes 196616 | tf_op jit(solution)/shard_map/ppermute | solution.py:221
  79.9 7.5 %collective-permute-start.19 = (bf16[32,1024]{1,0:T(8,128)(2,1)S(1)}, bf16[32,1024]{1,0:T(8,128)(2,1)S(1)}, u32[]{:S(2)}, u32[]{:S(2)}) collective-permute-start(bf16[32,1024]{1,0:T(8,128)(2,1)S(1)} %get-tuple-element.46), channel_id=1, source_target_pairs={{0,25},{1,24},{2,27},{3,26},{8,1},{9,0},{10,3},{11,2},{16,9},{17,8... | collective-permute-start | bytes 196616 | tf_op jit(solution)/shard_map/ppermute | solution.py:221
  79.9 7.5 %collective-permute-start.20 = (bf16[32,1024]{1,0:T(8,128)(2,1)S(1)}, bf16[32,1024]{1,0:T(8,128)(2,1)S(1)}, u32[]{:S(2)}, u32[]{:S(2)}) collective-permute-start(bf16[32,1024]{1,0:T(8,128)(2,1)S(1)} %get-tuple-element.47), channel_id=1, source_target_pairs={{0,26},{1,27},{2,24},{3,25},{8,2},{9,3},{10,0},{11,1},{16,10},{17,... | collective-permute-start | bytes 196616 | tf_op jit(solution)/shard_map/ppermute | solution.py:221
  83.9 7.0 %collective-permute-start.21 = (bf16[32,1024]{1,0:T(8,128)(2,1)S(1)}, bf16[32,1024]{1,0:T(8,128)(2,1)S(1)}, u32[]{:S(2)}, u32[]{:S(2)}) collective-permute-start(bf16[32,1024]{1,0:T(8,128)(2,1)S(1)} %get-tuple-element.48), channel_id=1, source_target_pairs={{0,27},{1,26},{2,25},{3,24},{8,3},{9,2},{10,1},{11,0},{16,11},{17,... | collective-permute-start | bytes 196616 | tf_op jit(solution)/shard_map/ppermute | solution.py:221

commit v2 on v0

v2 whole, which is shorter than its diff:
```python
import functools

import jax
import jax.numpy as jnp
from jax import lax
from jax.experimental import pallas as pl
from jax.experimental.pallas import tpu as pltpu
from jax.sharding import PartitionSpec as P

MIB = 1 << 20
COST = {"fore_first_0": 20_000_000_000, "back_second": 20_000_000_000, "prepare": 80_000_000_000}
VMEM = pl.BlockSpec(memory_space=pltpu.VMEM)
SMEM = pl.BlockSpec(memory_space=pltpu.SMEM)
ANY = pl.BlockSpec(memory_space=pl.ANY)
F32 = jnp.float32
BF16 = jnp.bfloat16


def spans(extent, width):
    return [(start, min(width, extent - start)) for start in range(0, extent, width)]


def halves(extent):
    first = -(-extent // 256) * 128
    return [(0, first), (first, extent - first)]


def shape(dims, dtype):
    return jax.ShapeDtypeStruct(tuple(dims), dtype)


def in_vmem(dims, dtype):
    return pltpu.VMEM(tuple(dims), dtype)


def from_hbm(value):
    return pltpu.with_memory_space_constraint(value, pltpu.HBM)


def kernel_call(body, name, outs, args, scratch=(), limit=8 * MIB, smem=0, far=0, aliases={}):
    return pl.pallas_call(
        body,
        name=name,
        out_shape=outs,
        in_specs=[SMEM] * smem + [VMEM] * (len(args) - smem - far) + [ANY] * far,
        out_specs=[VMEM] * len(outs),
        scratch_shapes=list(scratch),
        input_output_aliases=aliases,
        compiler_params=pltpu.CompilerParams(vmem_limit_bytes=limit),
        cost_estimate=pl.CostEstimate(flops=COST.get(name, 0), bytes_accessed=0, transcendentals=0),
    )(*args)


def row_copies(source, target, sems, cuts):
    deep = target.shape[0] // cuts
    return [
        pltpu.make_async_copy(
            source.at[pl.ds(c * deep, deep), :], target.at[pl.ds(c * deep, deep), :], sems.at[c]
        )
        for c in range(cuts)
    ]


def prepare(place, gate, weights, row_count):
    tokens, hidden = gate.shape
    own = tokens // row_count
    cuts = 4

    def body(place_ref, gate_hbm, *refs):
        weight_hbms, (silu_ref, slope_ref), refs = refs[:2], refs[2:4], refs[4:]
        weight_refs, (gate_ref, gate_sem, sems) = refs[:2], refs[2:]
        gate_copy = pltpu.make_async_copy(gate_hbm, gate_ref, gate_sem)
        gate_copy.start()
        copies = []
        for k in range(2):
            copies += row_copies(weight_hbms[k], weight_refs[k], sems.at[k], cuts)
        for copy in copies:
            copy.start()
        gate_copy.wait()
        start = pl.multiple_of(place_ref[1] * own, own)
        for at, wide in spans(hidden, 512):
            value = gate_ref[:, at : at + wide].astype(F32)
            sig = 1.0 / (1.0 + jnp.exp(-value))
            silu_ref[:, at : at + wide] = value * sig
            value = gate_ref[pl.ds(start, own), at : at + wide].astype(F32)
            sig = 1.0 / (1.0 + jnp.exp(-value))
            slope_ref[:, at : at + wide] = sig * (1.0 + value * (1.0 - sig))
        for copy in copies:
            copy.wait()

    return kernel_call(
        body,
        "prepare",
        [shape((tokens, hidden), F32), shape((own, hidden), F32)] + [in_vmem(w.shape, w.dtype) for w in weights],
        [place, from_hbm(gate)] + [from_hbm(w) for w in weights],
        scratch=[pltpu.VMEM(gate.shape, gate.dtype), pltpu.SemaphoreType.DMA, pltpu.SemaphoreType.DMA((2, cuts))],
        smem=1,
        far=3,
    )


def relay(value, after, name):
    def body(*refs):
        pass

    return kernel_call(
        body, name, [shape(value.shape, value.dtype)], [value] + list(after), far=len(after), aliases={0: 0}
    )[0]


def first_product(place, pieces, tokens, weight, part, transposed, name, keep=(), after=()):
    at0, wide0 = part
    fresh = tokens is None
    count = len(pieces) if fresh else 0
    inner = weight.shape[1] if transposed else weight.shape[0]
    rows = pieces[0].shape[0]
    total = rows * len(pieces)
    direct = rows % 16 == 0

    def body(place_ref, *refs):
        refs = list(refs)
        piece_refs = [refs.pop(0) for _ in range(count)]
        held_ref = None if fresh else refs.pop(0)
        weight_ref = refs.pop(0)
        del refs[: len(keep) + len(after)]
        out_ref = refs.pop(0)
        if fresh:
            held_ref = refs.pop(0)
            wide_ref = held_ref if direct else refs.pop(0)
            for k, piece_ref in enumerate(piece_refs):
                at = pl.multiple_of(lax.bitwise_xor(place_ref[0], k) * rows, rows)
                wide_ref[pl.ds(at, rows), :] = piece_ref[...].astype(wide_ref.dtype)
            if not direct:
                held_ref[...] = wide_ref[...].astype(BF16)
        for at, wide in spans(wide0, 512):
            cut = slice(at0 + at, at0 + at + wide)
            if transposed:
                value = lax.dot_general(
                    weight_ref[cut, :], held_ref[...], (((1,), (1,)), ((), ())), preferred_element_type=F32
                ).T
            else:
                value = jnp.dot(held_ref[...], weight_ref[:, cut], preferred_element_type=F32)
            out_ref[:, at : at + wide] = value

    outs = [shape((total, wide0), F32)]
    scratch = []
    if fresh:
        outs.append(shape((total, inner), BF16))
        if not direct:
            scratch.append(pltpu.VMEM((total, inner), F32))
    return kernel_call(
        body,
        name,
        outs,
        [place] + (pieces if fresh else [tokens]) + [weight] + list(keep) + list(after),
        scratch=scratch,
        smem=1,
        far=len(after),
    )


def blend(silu_ref, sum_refs, parts, values_ref):
    for (at0, wide0), (mine_ref, theirs_ref) in zip(parts, sum_refs):
        for at, wide in spans(wide0, 256):
            total = mine_ref[:, at : at + wide] + theirs_ref[:, at : at + wide]
            whole = slice(at0 + at, at0 + at + wide)
            values_ref[:, whole] = (silu_ref[:, whole] * total).astype(BF16)


def second_product(place, silu, sums, parts, residual, weight, transposed, blocks, paired, name, keep=(), after=()):
    tokens, hidden = silu.shape
    width = residual.shape[1]
    rows = tokens // blocks
    flat = [a for pair in sums for a in pair]
    odd = blocks // 2

    def body(place_ref, silu_ref, residual_ref, *refs):
        refs = list(refs)
        sum_refs = [(refs.pop(0), refs.pop(0)) for _ in parts]
        weight_ref = refs.pop(0)
        del refs[: len(keep) + len(after)]
        outs = [refs.pop(0) for _ in range(2 if paired else blocks)]
        values_ref, total_ref = refs
        blend(silu_ref, sum_refs, parts, values_ref)
        for at, wide in spans(width, 512):
            cut = slice(at, at + wide)
            if transposed:
                value = lax.dot_general(
                    weight_ref[cut, :], values_ref[...], (((1,), (1,)), ((), ())), preferred_element_type=F32
                ).T
            else:
                value = jnp.dot(values_ref[...], weight_ref[:, cut], preferred_element_type=F32)
            total_ref[:, cut] = value
            for k in range(blocks):
                start = pl.multiple_of(lax.bitwise_xor(place_ref[0], k) * rows, rows)
                piece = total_ref[pl.ds(start, rows), cut]
                if k == 0:
                    piece = piece + residual_ref[:, cut].astype(F32)
                if paired:
                    low = k // 2 * rows
                    outs[1 - k % 2][low : low + rows, cut] = piece.astype(outs[1 - k % 2].dtype)
                else:
                    outs[k][:, cut] = piece.astype(BF16)

    if paired:
        outs = [shape((odd * rows, width), BF16), shape((odd * rows, width), F32)]
    else:
        outs = [shape((rows, width), BF16)] * blocks
    return kernel_call(
        body,
        name,
        outs,
        [place, silu, residual] + flat + [weight] + list(keep) + list(after),
        scratch=[pltpu.VMEM((tokens, hidden), BF16), pltpu.VMEM((tokens, width), F32)],
        smem=1,
        far=len(after),
    )


def pair_sums(mine, theirs, count, name, after=()):
    rows = mine.shape[0] // count

    def body(mine_ref, theirs_ref, *refs):
        outs = refs[len(after) :]
        for k in range(count):
            low = slice(k * rows, (k + 1) * rows)
            outs[k][...] = (mine_ref[low, :] + theirs_ref[low, :].astype(F32)).astype(BF16)

    return kernel_call(
        body,
        name,
        [shape((rows, mine.shape[1]), BF16)] * count,
        [mine, theirs] + list(after),
        far=len(after),
    )


def gate_gradient(place, slope, up_sums, up_parts, back_sums, back_parts):
    own, hidden = slope.shape

    def body(place_ref, slope_ref, *refs):
        refs = list(refs)
        up_refs = [(refs.pop(0), refs.pop(0)) for _ in up_parts]
        back_refs = [(refs.pop(0), refs.pop(0)) for _ in back_parts]
        out_ref = refs[0]
        rows = pl.ds(pl.multiple_of(place_ref[1] * own, own), own)

        def total(pairs, parts, at):
            for (mine_ref, theirs_ref), (low, wide) in zip(pairs, parts):
                if low <= at < low + wide:
                    cut = slice(at - low, at - low + 128)
                    return mine_ref[rows, cut] + theirs_ref[rows, cut]

        for at in range(0, hidden, 128):
            up = total(up_refs, up_parts, at)
            back = total(back_refs, back_parts, at)
            out_ref[:, at : at + 128] = (back * up * slope_ref[:, at : at + 128]).astype(BF16)

    return kernel_call(
        body,
        "gate_gradient",
        [shape((own, hidden), BF16)],
        [place, slope] + [a for pair in up_sums for a in pair] + [a for pair in back_sums for a in pair],
        smem=1,
    )[0]


def collect(pieces, name):
    def body(*refs):
        out_ref = refs[-1]
        total = refs[0][...].astype(F32)
        for ref in refs[1:-1]:
            total = total + ref[...].astype(F32)
        out_ref[...] = total.astype(BF16)

    return kernel_call(body, name, [shape(pieces[0].shape, BF16)], pieces)[0]


def shards(sections, cols, row_count, inputs, gate_pre, up_weight, down_weight, output_grad):
    own_x, own_g, gate = inputs[0], output_grad[0], gate_pre[0]
    place = jnp.stack([lax.axis_index("col"), lax.axis_index("row")]).astype(jnp.int32)

    def from_xor(value, k):
        return lax.ppermute(value, "col", [(c, c ^ k) for c in range(cols)])

    def to_block(value, k, step):
        pairs = [
            (s * cols + c, (s + step) % sections * cols + (c ^ k)) for s in range(sections) for c in range(cols)
        ]
        return lax.ppermute(value, ("section", "col"), pairs)

    def other_row(value):
        return lax.ppermute(value, "row", [(r, (r + 1) % row_count) for r in range(row_count)])

    hidden = gate.shape[1]
    parts = halves(hidden)
    whole = [(0, hidden)]

    def first_pieces(own):
        pieces = [own] + [None] * (cols - 1)
        for k in list(range(2, cols, 2)) + [1]:
            pieces[k] = from_xor(own, k)
        return pieces

    def last_pieces(pieces, after, name):
        for k in range(3, cols, 2):
            pieces[k] = from_xor(relay(pieces[k - 1], after, name), 1)

    g_pieces, x_pieces = first_pieces(own_g), first_pieces(own_x)
    silu, slope, down, up = prepare(place, gate, [down_weight, up_weight], row_count)
    last_pieces(g_pieces, [silu], "relay_g")
    last_pieces(x_pieces, [silu], "relay_x")

    def sums_of(pieces, weight, transposed, cuts, name, keep, after=()):
        sums, tokens = [], None
        for part in cuts:
            got = first_product(
                place, pieces, tokens, weight, part, transposed, name + "_%d" % len(sums), keep, after
            )
            sums.append((got[0], other_row(got[0])))
            tokens = got[1] if tokens is None else tokens
            after = ()
        return sums

    def reduced(silu_sums, cuts, residual, weight, transposed, paired, step, name, keep, after):
        blocks = second_product(
            place, silu, silu_sums, cuts, residual, weight, transposed, cols, paired, name, keep, after
        )
        if not paired:
            return blocks[0], lambda after: [to_block(block, k, step) for k, block in enumerate(blocks)]
        theirs = from_xor(blocks[0], 1)

        def finish(after):
            halves_ = pair_sums(blocks[1], theirs, cols // 2, name + "_pair", after)
            return [to_block(block, 2 * k, step) for k, block in reversed(list(enumerate(halves_)))]

        return blocks[0], finish

    back_sums = sums_of(g_pieces, down, True, parts, "back_first", [up])
    up_sums = sums_of(x_pieces, up, False, whole, "fore_first", [down], [back_sums[-1][0]])
    token, finish_back = reduced(
        back_sums, parts, own_g, up, True, True, -1, "back_second", [down], [up_sums[-1][0]]
    )
    token, finish_fore = reduced(up_sums, whole, own_x, down, False, True, 1, "fore_second", [], [token])
    backward = finish_back([token])
    forward = finish_fore([])

    gate_grad = gate_gradient(place, slope, up_sums, whole, back_sums, parts)
    handed_back = collect(backward, "back_collect")
    handed_forward = collect(forward, "fore_collect")
    return handed_forward[None], gate_grad[None], handed_back[None]


def solution(mesh):
    placed = (
        P("section", "col", "row"),
        P("section", None, "col"),
        P("row", "col"),
        P("col", "row"),
        P("section", "col", "row"),
    )
    sizes = mesh.shape
    return jax.shard_map(
        functools.partial(shards, sizes["section"], sizes["col"], sizes["row"]),
        mesh=mesh,
        in_specs=placed,
        out_specs=(
            P("section", "col", "row"),
            P("section", "row", "col"),
            P("section", "col", "row"),
        ),
        check_vma=False,
    )
```

time: 159 us -> 65.6 us (0.41)
  waiting for transfers between devices: 56.4 us -> 15 us
  matrix products: 39.5 us -> 0 us
  blocking collectives: 38.9 us -> 0 us
  Pallas kernels: 0 us -> 29.7 us
  starting transfers between devices: 4.12 us -> 20 us
  between operations: 13.8 us -> 0.74 us
  other arithmetic: 4.67 us -> 0.07 us
    reduce_scatter x4 -> x0, waiting for transfers between devices: 51.8 us -> none  [the longest x2 41.9 us: col_product(): lax.psum_scatter(lax.dot_general(gathered, matrix, (contract, ((), ())),...]
    dot_general x4 -> x0, matrix products: 39.5 us -> none  [the longest x2 19.8 us: row_product(): lax.dot_general(gathered, matrix, (contract, ((), ())), preferred_element...]
    all_gather x4 -> x0, blocking collectives: 38.9 us -> none  [the longest x2 34 us: row_product(): gathered = lax.all_gather(pieces, 'col', axis=0, tiled=True)]
    pallas_call x0 -> x13, Pallas kernels: none -> 29.7 us  [kernel_call(): pl.pallas_call(body, name=name, out_shape=outs, in_specs=[SMEM] * smem +...]
    ppermute x2 -> x15, starting transfers between devices: 3.96 us -> 20 us  [the longest x8 10.5 us: from_xor(): return lax.ppermute(value, 'col', [(c, c ^ k) for c in range(cols)])]
    ppermute x2 -> x15, waiting for transfers between devices: 4.49 us -> 15 us  [the longest x8 10.2 us: from_xor(): return lax.ppermute(value, 'col', [(c, c ^ k) for c in range(cols)])]
    convert_element_type x3 -> x0, other arithmetic: 4.67 us -> none  [the longest x1 2.72 us: shards(): up_grad = (hidden_grad * gate_used * sigmoid_gate).astype(jnp.bfloat16)]
  transfers between devices with their start and end apart: 6 -> 15, of which waited for: 4 -> 5; matrix products, arithmetic and copies ran while one was open for 12% -> 0% of each run, Pallas kernels for 0% -> 44%
where the time goes in v2:
time: 65.6 us; the launch traced here: 65.4 us
  Pallas kernels  29.7 us (45%)
  starting transfers between devices  20 us (30%)
  waiting for transfers between devices  15 us (23%)
  between operations  0.74 us (1%)
    pallas_call x13, Pallas kernels, kernel_call(): pl.pallas_call(body, name=name, out_shape=outs, in_specs=[SMEM] * smem +...  29.7 us
    ppermute x8, starting transfers between devices, from_xor(): return lax.ppermute(value, 'col', [(c, c ^ k) for c in range(cols)])  10.5 us
    ppermute x8, waiting for transfers between devices, from_xor(): return lax.ppermute(value, 'col', [(c, c ^ k) for c in range(cols)])  10.2 us
    ppermute x4, starting transfers between devices, to_block(): return lax.ppermute(value, ('section', 'col'), pairs)  8.8 us
    ppermute x4, waiting for transfers between devices, to_block(): return lax.ppermute(value, ('section', 'col'), pairs)  4.79 us
  transfers between devices with their start and end apart: 15, of which 5 were waited for; matrix products, arithmetic and copies ran while one was open for 0% of the time, Pallas kernels for 44%

profile of v2, /device:TPU:0, one launch (start us, length us, event | category | flops | bytes accessed | tf_op | source)
XLA Modules:
  0.0 65.4 jit_solution(58427299743209684)
XLA Ops:
  0.6 4.1 %collective-permute-start.4 = (bf16[32,2048]{1,0:T(8,128)(2,1)}, bf16[32,2048]{1,0:T(8,128)(2,1)S(1)}, u32[]{:S(2)}, u32[]{:S(2)}) collective-permute-start(bf16[32,2048]{1,0:T(8,128)(2,1)} %bitcast.8), channel_id=1, source_target_pairs={{0,2},{1,3},{2,0},{3,1},{4,6},{5,7},{6,4},{7,5},{8,10},{9,11},{10,... | collective-permute-start | bytes 393224 | tf_op jit(solution)/shard_map/ppermute | solution.py:284
  4.7 1.6 %collective-permute-start.3 = (bf16[32,2048]{1,0:T(8,128)(2,1)}, bf16[32,2048]{1,0:T(8,128)(2,1)S(1)}, u32[]{:S(2)}, u32[]{:S(2)}) collective-permute-start(bf16[32,2048]{1,0:T(8,128)(2,1)} %bitcast.9), channel_id=1, source_target_pairs={{0,1},{1,0},{2,3},{3,2},{4,5},{5,4},{6,7},{7,6},{8,9},{9,8},{10,11... | collective-permute-start | bytes 393224 | tf_op jit(solution)/shard_map/ppermute | solution.py:284
  6.3 0.3 collective-permute-start.1
  6.6 0.1 pad_add_fusion.place_ref
  6.7 10.3 %prepare.1 = (f32[128,3584]{1,0:T(8,128)S(1)}, f32[64,3584]{1,0:T(8,128)S(1)}, bf16[3584,2048]{1,0:T(8,128)(2,1)S(1)}, bf16[2048,3584]{1,0:T(8,128)(2,1)S(1)}) custom-call(s32[2]{0:T(128)S(1)} %pad_add_fusion.place_ref, bf16[128,3584]{1,0:T(8,128)(2,1)} %bitcast.19, bf16[3584,2048]{1,0:T(8,128)(2,1)} %refs_0_.1, bf16[2048,3584]{1,0:T(8,128)(2,1)} %refs_1_.1), custom_call_target="tpu_custom_call" | custom-call | flops 80000000000 | tf_op jit(solution)/shard_map/prepare/pallas_call | solution.py:41
  17.1 0.0 collective-permute-done.4.refs_2_
  17.1 0.3 collective-permute-start.5
  17.4 1.8 %collective-permute-start = (bf16[32,2048]{1,0:T(8,128)(2,1)S(1)}, bf16[32,2048]{1,0:T(8,128)(2,1)S(1)}, u32[]{:S(2)}, u32[]{:S(2)}) collective-permute-start(bf16[32,2048]{1,0:T(8,128)(2,1)S(1)} %bitcast.13), channel_id=1, source_target_pairs={{0,1},{1,0},{2,3},{3,2},{4,5},{5,4},{6,7},{7,6},{8,9},{9,8},{10,11... | collective-permute-start | bytes 393224 | tf_op jit(solution)/shard_map/ppermute | solution.py:284
  19.2 0.3 collective-permute-start.2
  19.5 4.1 %collective-permute-done.5.refs_3_ = bf16[32,2048]{1,0:T(8,128)(2,1)S(1)} collective-permute-done((bf16[32,2048]{1,0:T(8,128)(2,1)S(1)}, bf16[32,2048]{1,0:T(8,128)(2,1)S(1)}, u32[]{:S(2)}, u32[]{:S(2)}) %collective-permute-start.5) | collective-permute-done | bytes 131104 | tf_op jit(solution)/shard_map/ppermute | solution.py:284
  23.6 2.7 %back_first_0.1 = (f32[128,1792]{1,0:T(8,128)S(1)}, bf16[128,2048]{1,0:T(8,128)(2,1)S(1)}) custom-call(s32[2]{0:T(128)S(1)} %pad_add_fusion.place_ref, bf16[32,2048]{1,0:T(8,128)(2,1)S(1)} %bitcast.10, bf16[32,2048]{1,0:T(8,128)(2,1)S(1)} %collective-permute-done.3.refs_1_, bf16[32,2048]{1,0:T(8,128)(2,1)S(1)} %collective-permute-done.4.refs_2_, ...), custom_call_target="tpu_custom_call" | custom-call | tf_op jit(solution)/shard_map/back_first_0/pallas_call | solution.py:41
  26.3 2.7 %back_first_1.1.refs_6_.refs_2_.refs_4_ = f32[128,1792]{1,0:T(8,128)S(1)} custom-call(s32[2]{0:T(128)S(1)} %pad_add_fusion.place_ref, bf16[128,2048]{1,0:T(8,128)(2,1)S(1)} %get-tuple-element.21.refs_0_, bf16[3584,2048]{1,0:T(8,128)(2,1)S(1)} %get-tuple-element.20.refs_4_.refs_1_.refs_5_.refs_2_, bf16[2048,3584]{1,0:T(8,128)(2,1)S(1)} %get-tuple-element.19.refs_5_.refs_2_.refs_4_), custom_call_target="tpu_custom_call" | custom-call | tf_op jit(solution)/shard_map/back_first_1/pallas_call | solution.py:41
  29.0 0.1 collective-permute-start.8
  29.1 0.5 collective-permute-start.7
  29.6 3.5 %fore_first_0.1 = (f32[128,3584]{1,0:T(8,128)S(1)}, bf16[128,2048]{1,0:T(8,128)(2,1)}) custom-call(s32[2]{0:T(128)S(1)} %pad_add_fusion.place_ref, bf16[32,2048]{1,0:T(8,128)(2,1)S(1)} %bitcast.14, bf16[32,2048]{1,0:T(8,128)(2,1)S(1)} %collective-permute-done.refs_1_, bf16[32,2048]{1,0:T(8,128)(2,1)S(1)} %collective-permute-done.1.refs_2_, ...), custom_call_target="tpu_custom_call" | custom-call | flops 20000000000 | tf_op jit(solution)/shard_map/fore_first_0/pallas_call | solution.py:41
  33.1 0.1 collective-permute-start.6
  33.2 4.6 %back_second.1 = (bf16[64,2048]{1,0:T(8,128)(2,1)S(1)}, f32[64,2048]{1,0:T(8,128)S(1)}) custom-call(s32[2]{0:T(128)S(1)} %pad_add_fusion.place_ref, f32[128,3584]{1,0:T(8,128)S(1)} %get-tuple-element.18.refs_1_.silu_ref, bf16[32,2048]{1,0:T(8,128)(2,1)S(1)} %bitcast.11, f32[128,1792]{1,0:T(8,128)S(1)} %get-tuple-element.23.refs_0_.refs_2_, ...), custom_call_target="tpu_custom_call" | custom-call | flops 20000000000 | tf_op jit(solution)/shard_map/back_second/pallas_call | solution.py:41
  37.8 0.3 collective-permute-start.12
  38.1 2.8 %fore_second.1 = (bf16[64,2048]{1,0:T(8,128)(2,1)S(1)}, f32[64,2048]{1,0:T(8,128)S(1)}) custom-call(s32[2]{0:T(128)S(1)} %pad_add_fusion.place_ref, f32[128,3584]{1,0:T(8,128)S(1)} %get-tuple-element.18.refs_1_.silu_ref, bf16[32,2048]{1,0:T(8,128)(2,1)S(1)} %bitcast.15, f32[128,3584]{1,0:T(8,128)S(1)} %get-tuple-element.22.refs_6_.refs_0_, ...), custom_call_target="tpu_custom_call" | custom-call | tf_op jit(solution)/shard_map/fore_second/pallas_call | solution.py:41
  40.9 1.9 %collective-permute-start.9 = (bf16[64,2048]{1,0:T(8,128)(2,1)S(1)}, bf16[64,2048]{1,0:T(8,128)(2,1)S(1)}, u32[]{:S(2)}, u32[]{:S(2)}) collective-permute-start(bf16[64,2048]{1,0:T(8,128)(2,1)S(1)} %get-tuple-element.26.refs_0_), channel_id=1, source_target_pairs={{0,1},{1,0},{2,3},{3,2},{4,5},{5,4},{6,7},{7,6},{8,9},{9,8},{10,11... | collective-permute-start | bytes 786440 | tf_op jit(solution)/shard_map/ppermute | solution.py:284
  42.8 4.2 %collective-permute-done.12.theirs_ref = bf16[64,2048]{1,0:T(8,128)(2,1)S(1)} collective-permute-done((bf16[64,2048]{1,0:T(8,128)(2,1)S(1)}, bf16[64,2048]{1,0:T(8,128)(2,1)S(1)}, u32[]{:S(2)}, u32[]{:S(2)}) %collective-permute-start.12) | collective-permute-done | bytes 262176 | tf_op jit(solution)/shard_map/ppermute | solution.py:284
  47.0 0.1 back_second_pair.1
  47.1 4.5 %collective-permute-start.13 = (bf16[32,2048]{1,0:T(8,128)(2,1)S(1)}, bf16[32,2048]{1,0:T(8,128)(2,1)S(1)}, u32[]{:S(2)}, u32[]{:S(2)}) collective-permute-start(bf16[32,2048]{1,0:T(8,128)(2,1)S(1)} %get-tuple-element.31), channel_id=1, source_target_pairs={{0,26},{1,27},{2,24},{3,25},{8,2},{9,3},{10,0},{11,1},{16,10},{17,... | collective-permute-start | bytes 393224 | tf_op jit(solution)/shard_map/ppermute | solution.py:290
  51.6 0.5 collective-permute-start.14
  52.1 1.8 %collective-permute-done.9.theirs_ref = bf16[64,2048]{1,0:T(8,128)(2,1)S(1)} collective-permute-done((bf16[64,2048]{1,0:T(8,128)(2,1)S(1)}, bf16[64,2048]{1,0:T(8,128)(2,1)S(1)}, u32[]{:S(2)}, u32[]{:S(2)}) %collective-permute-start.9) | collective-permute-done | bytes 262176 | tf_op jit(solution)/shard_map/ppermute | solution.py:284
  54.0 2.2 %collective-permute-start.10 = (bf16[32,2048]{1,0:T(8,128)(2,1)S(1)}, bf16[32,2048]{1,0:T(8,128)(2,1)S(1)}, u32[]{:S(2)}, u32[]{:S(2)}) collective-permute-start(bf16[32,2048]{1,0:T(8,128)(2,1)S(1)} %get-tuple-element.27), channel_id=1, source_target_pairs={{0,10},{1,11},{2,8},{3,9},{8,18},{9,19},{10,16},{11,17},{16,26},{1... | collective-permute-start | bytes 393224 | tf_op jit(solution)/shard_map/ppermute | solution.py:290
  56.3 1.5 %collective-permute-start.11 = (bf16[32,2048]{1,0:T(8,128)(2,1)S(1)}, bf16[32,2048]{1,0:T(8,128)(2,1)S(1)}, u32[]{:S(2)}, u32[]{:S(2)}) collective-permute-start(bf16[32,2048]{1,0:T(8,128)(2,1)S(1)} %get-tuple-element.28), channel_id=1, source_target_pairs={{0,8},{1,9},{2,10},{3,11},{8,16},{9,17},{10,18},{11,19},{16,24},{1... | collective-permute-start | bytes 393224 | tf_op jit(solution)/shard_map/ppermute | solution.py:290
  57.7 1.5 %gate_gradient.1 = bf16[64,3584]{1,0:T(8,128)(2,1)} custom-call(s32[2]{0:T(128)S(1)} %pad_add_fusion.place_ref, f32[64,3584]{1,0:T(8,128)S(1)} %get-tuple-element.29.slope_ref, f32[128,3584]{1,0:T(8,128)S(1)} %get-tuple-element.22.refs_6_.refs_0_, f32[128,3584]{1,0:T(8,128)S(1)} %collective-permute-done.6.refs_1_, ...), custom_call_target="tpu_custom_call" | custom-call | tf_op jit(solution)/shard_map/gate_gradient/pallas_call | solution.py:41
  59.3 0.7 %back_collect.1 = bf16[32,2048]{1,0:T(8,128)(2,1)} custom-call(bf16[32,2048]{1,0:T(8,128)(2,1)S(1)} %collective-permute-done.13.refs_0_, bf16[32,2048]{1,0:T(8,128)(2,1)S(1)} %collective-permute-done.14.refs_1_), custom_call_target="tpu_custom_call" | custom-call | tf_op jit(solution)/shard_map/back_collect/pallas_call | solution.py:41
  60.0 4.6 %collective-permute-done.10.refs_0_ = bf16[32,2048]{1,0:T(8,128)(2,1)S(1)} collective-permute-done((bf16[32,2048]{1,0:T(8,128)(2,1)S(1)}, bf16[32,2048]{1,0:T(8,128)(2,1)S(1)}, u32[]{:S(2)}, u32[]{:S(2)}) %collective-permute-start.10) | collective-permute-done | bytes 131104 | tf_op jit(solution)/shard_map/ppermute | solution.py:290
  64.6 0.1 collective-permute-done.11.refs_1_
  64.8 0.7 %fore_collect.1 = bf16[32,2048]{1,0:T(8,128)(2,1)} custom-call(bf16[32,2048]{1,0:T(8,128)(2,1)S(1)} %collective-permute-done.10.refs_0_, bf16[32,2048]{1,0:T(8,128)(2,1)S(1)} %collective-permute-done.11.refs_1_), custom_call_target="tpu_custom_call" | custom-call | tf_op jit(solution)/shard_map/fore_collect/pallas_call | solution.py:41
  (18 shorter events, 0.1 us)
Async XLA Ops:
  0.6 16.4 %collective-permute-start.4 = (bf16[32,2048]{1,0:T(8,128)(2,1)}, bf16[32,2048]{1,0:T(8,128)(2,1)S(1)}, u32[]{:S(2)}, u32[]{:S(2)}) collective-permute-start(bf16[32,2048]{1,0:T(8,128)(2,1)} %bitcast.8), channel_id=1, source_target_pairs={{0,2},{1,3},{2,0},{3,1},{4,6},{5,7},{6,4},{7,5},{8,10},{9,11},{10,... | collective-permute-start | bytes 393224 | tf_op jit(solution)/shard_map/ppermute | solution.py:284
  4.7 14.8 %collective-permute-start.3 = (bf16[32,2048]{1,0:T(8,128)(2,1)}, bf16[32,2048]{1,0:T(8,128)(2,1)S(1)}, u32[]{:S(2)}, u32[]{:S(2)}) collective-permute-start(bf16[32,2048]{1,0:T(8,128)(2,1)} %bitcast.9), channel_id=1, source_target_pairs={{0,1},{1,0},{2,3},{3,2},{4,5},{5,4},{6,7},{7,6},{8,9},{9,8},{10,11... | collective-permute-start | bytes 393224 | tf_op jit(solution)/shard_map/ppermute | solution.py:284
  6.3 12.9 %collective-permute-start.1 = (bf16[32,2048]{1,0:T(8,128)(2,1)}, bf16[32,2048]{1,0:T(8,128)(2,1)S(1)}, u32[]{:S(2)}, u32[]{:S(2)}) collective-permute-start(bf16[32,2048]{1,0:T(8,128)(2,1)} %bitcast.12), channel_id=1, source_target_pairs={{0,2},{1,3},{2,0},{3,1},{4,6},{5,7},{6,4},{7,5},{8,10},{9,11},{10,... | collective-permute-start | bytes 393224 | tf_op jit(solution)/shard_map/ppermute | solution.py:284
  6.7 10.6 %copy-start.1 = (bf16[1,32,2048]{2,1,0:T(8,128)(2,1)S(1)}, bf16[1,32,2048]{2,1,0:T(8,128)(2,1)}, u32[]{:S(2)}) copy-start(bf16[1,32,2048]{2,1,0:T(8,128)(2,1)} %param.5) | copy-start | bytes 393220
  6.7 16.9 %copy-start = (bf16[1,32,2048]{2,1,0:T(8,128)(2,1)S(1)}, bf16[1,32,2048]{2,1,0:T(8,128)(2,1)}, u32[]{:S(2)}) copy-start(bf16[1,32,2048]{2,1,0:T(8,128)(2,1)} %param.9) | copy-start | bytes 393220
  17.1 6.5 %collective-permute-start.5 = (bf16[32,2048]{1,0:T(8,128)(2,1)S(1)}, bf16[32,2048]{1,0:T(8,128)(2,1)S(1)}, u32[]{:S(2)}, u32[]{:S(2)}) collective-permute-start(bf16[32,2048]{1,0:T(8,128)(2,1)S(1)} %relay_g.1), channel_id=1, source_target_pairs={{0,1},{1,0},{2,3},{3,2},{4,5},{5,4},{6,7},{7,6},{8,9},{9,8},{10,11... | collective-permute-start | bytes 393224 | tf_op jit(solution)/shard_map/ppermute | solution.py:284
  17.4 12.3 %collective-permute-start = (bf16[32,2048]{1,0:T(8,128)(2,1)S(1)}, bf16[32,2048]{1,0:T(8,128)(2,1)S(1)}, u32[]{:S(2)}, u32[]{:S(2)}) collective-permute-start(bf16[32,2048]{1,0:T(8,128)(2,1)S(1)} %bitcast.13), channel_id=1, source_target_pairs={{0,1},{1,0},{2,3},{3,2},{4,5},{5,4},{6,7},{7,6},{8,9},{9,8},{10,11... | collective-permute-start | bytes 393224 | tf_op jit(solution)/shard_map/ppermute | solution.py:284
  19.2 10.4 %collective-permute-start.2 = (bf16[32,2048]{1,0:T(8,128)(2,1)S(1)}, bf16[32,2048]{1,0:T(8,128)(2,1)S(1)}, u32[]{:S(2)}, u32[]{:S(2)}) collective-permute-start(bf16[32,2048]{1,0:T(8,128)(2,1)S(1)} %relay_x.1), channel_id=1, source_target_pairs={{0,1},{1,0},{2,3},{3,2},{4,5},{5,4},{6,7},{7,6},{8,9},{9,8},{10,11... | collective-permute-start | bytes 393224 | tf_op jit(solution)/shard_map/ppermute | solution.py:284
  29.0 4.1 %collective-permute-start.8 = (f32[128,1792]{1,0:T(8,128)S(1)}, f32[128,1792]{1,0:T(8,128)S(1)}, u32[]{:S(2)}, u32[]{:S(2)}) collective-permute-start(f32[128,1792]{1,0:T(8,128)S(1)} %back_first_1.1.refs_6_.refs_2_.refs_4_), channel_id=1, source_target_pairs={{0,4},{4,0},{1,5},{5,1},{2,6},{6,2},{3,7},{7,3},{8,12},{12,8},{9,1... | collective-permute-start | bytes 2752520 | tf_op jit(solution)/shard_map/ppermute | solution.py:293
  29.1 4.1 %collective-permute-start.7 = (f32[128,1792]{1,0:T(8,128)S(1)}, f32[128,1792]{1,0:T(8,128)S(1)}, u32[]{:S(2)}, u32[]{:S(2)}) collective-permute-start(f32[128,1792]{1,0:T(8,128)S(1)} %get-tuple-element.23.refs_0_.refs_2_), channel_id=1, source_target_pairs={{0,4},{4,0},{1,5},{5,1},{2,6},{6,2},{3,7},{7,3},{8,12},{12,8},{9,1... | collective-permute-start | bytes 2752520 | tf_op jit(solution)/shard_map/ppermute | solution.py:293
  33.1 5.0 %collective-permute-start.6 = (f32[128,3584]{1,0:T(8,128)S(1)}, f32[128,3584]{1,0:T(8,128)S(1)}, u32[]{:S(2)}, u32[]{:S(2)}) collective-permute-start(f32[128,3584]{1,0:T(8,128)S(1)} %get-tuple-element.22.refs_6_.refs_0_), channel_id=1, source_target_pairs={{0,4},{4,0},{1,5},{5,1},{2,6},{6,2},{3,7},{7,3},{8,12},{12,8},{9,1... | collective-permute-start | bytes 5505032 | tf_op jit(solution)/shard_map/ppermute | solution.py:293
  37.8 9.2 %collective-permute-start.12 = (bf16[64,2048]{1,0:T(8,128)(2,1)S(1)}, bf16[64,2048]{1,0:T(8,128)(2,1)S(1)}, u32[]{:S(2)}, u32[]{:S(2)}) collective-permute-start(bf16[64,2048]{1,0:T(8,128)(2,1)S(1)} %get-tuple-element.24.refs_3_), channel_id=1, source_target_pairs={{0,1},{1,0},{2,3},{3,2},{4,5},{5,4},{6,7},{7,6},{8,9},{9,8},{10,11... | collective-permute-start | bytes 786440 | tf_op jit(solution)/shard_map/ppermute | solution.py:284
  40.9 13.1 %collective-permute-start.9 = (bf16[64,2048]{1,0:T(8,128)(2,1)S(1)}, bf16[64,2048]{1,0:T(8,128)(2,1)S(1)}, u32[]{:S(2)}, u32[]{:S(2)}) collective-permute-start(bf16[64,2048]{1,0:T(8,128)(2,1)S(1)} %get-tuple-element.26.refs_0_), channel_id=1, source_target_pairs={{0,1},{1,0},{2,3},{3,2},{4,5},{5,4},{6,7},{7,6},{8,9},{9,8},{10,11... | collective-permute-start | bytes 786440 | tf_op jit(solution)/shard_map/ppermute | solution.py:284
  47.1 12.2 %collective-permute-start.13 = (bf16[32,2048]{1,0:T(8,128)(2,1)S(1)}, bf16[32,2048]{1,0:T(8,128)(2,1)S(1)}, u32[]{:S(2)}, u32[]{:S(2)}) collective-permute-start(bf16[32,2048]{1,0:T(8,128)(2,1)S(1)} %get-tuple-element.31), channel_id=1, source_target_pairs={{0,26},{1,27},{2,24},{3,25},{8,2},{9,3},{10,0},{11,1},{16,10},{17,... | collective-permute-start | bytes 393224 | tf_op jit(solution)/shard_map/ppermute | solution.py:290
  51.6 7.7 %collective-permute-start.14 = (bf16[32,2048]{1,0:T(8,128)(2,1)S(1)}, bf16[32,2048]{1,0:T(8,128)(2,1)S(1)}, u32[]{:S(2)}, u32[]{:S(2)}) collective-permute-start(bf16[32,2048]{1,0:T(8,128)(2,1)S(1)} %get-tuple-element.32), channel_id=1, source_target_pairs={{0,24},{1,25},{2,26},{3,27},{8,0},{9,1},{10,2},{11,3},{16,8},{17,9... | collective-permute-start | bytes 393224 | tf_op jit(solution)/shard_map/ppermute | solution.py:290
  54.0 10.6 %collective-permute-start.10 = (bf16[32,2048]{1,0:T(8,128)(2,1)S(1)}, bf16[32,2048]{1,0:T(8,128)(2,1)S(1)}, u32[]{:S(2)}, u32[]{:S(2)}) collective-permute-start(bf16[32,2048]{1,0:T(8,128)(2,1)S(1)} %get-tuple-element.27), channel_id=1, source_target_pairs={{0,10},{1,11},{2,8},{3,9},{8,18},{9,19},{10,16},{11,17},{16,26},{1... | collective-permute-start | bytes 393224 | tf_op jit(solution)/shard_map/ppermute | solution.py:290
  56.3 8.5 %collective-permute-start.11 = (bf16[32,2048]{1,0:T(8,128)(2,1)S(1)}, bf16[32,2048]{1,0:T(8,128)(2,1)S(1)}, u32[]{:S(2)}, u32[]{:S(2)}) collective-permute-start(bf16[32,2048]{1,0:T(8,128)(2,1)S(1)} %get-tuple-element.28), channel_id=1, source_target_pairs={{0,8},{1,9},{2,10},{3,11},{8,16},{9,17},{10,18},{11,19},{16,24},{1... | collective-permute-start | bytes 393224 | tf_op jit(solution)/shard_map/ppermute | solution.py:290

commit v3 on v0

v3 whole, which is shorter than its diff:
```python
import functools

import jax
import jax.numpy as jnp
from jax import lax
from jax.experimental import pallas as pl
from jax.experimental.pallas import tpu as pltpu
from jax.sharding import PartitionSpec as P

MIB = 1 << 20
COST = {'prepare': 5000000000, 'back_first_0': 5000000000, 'back_second': 5000000000, 'fore_second': 5000000000}
VMEM = pl.BlockSpec(memory_space=pltpu.VMEM)
SMEM = pl.BlockSpec(memory_space=pltpu.SMEM)
ANY = pl.BlockSpec(memory_space=pl.ANY)
F32 = jnp.float32
BF16 = jnp.bfloat16


def spans(extent, width):
    return [(start, min(width, extent - start)) for start in range(0, extent, width)]


def shape(dims, dtype):
    return jax.ShapeDtypeStruct(tuple(dims), dtype)


def from_hbm(value):
    return pltpu.with_memory_space_constraint(value, pltpu.HBM)


def kernel_call(body, name, outs, args, scratch=(), limit=8 * MIB, smem=0, far=0):
    return pl.pallas_call(
        body,
        name=name,
        out_shape=outs,
        in_specs=[SMEM] * smem + [VMEM] * (len(args) - smem - far) + [ANY] * far,
        out_specs=[VMEM] * len(outs),
        scratch_shapes=list(scratch),
        compiler_params=pltpu.CompilerParams(vmem_limit_bytes=limit),
        cost_estimate=pl.CostEstimate(flops=COST.get(name, 0), bytes_accessed=0, transcendentals=0),
    )(*args)


def row_copies(source, target, sems, cuts):
    deep = target.shape[0] // cuts
    return [
        pltpu.make_async_copy(
            source.at[pl.ds(c * deep, deep), :], target.at[pl.ds(c * deep, deep), :], sems.at[c]
        )
        for c in range(cuts)
    ]


def prepare(place, gate, row_count, blocks):
    tokens, hidden = gate.shape
    own, rows = tokens // row_count, tokens // blocks
    direct = rows % 16 == 0

    def body(place_ref, gate_hbm, silu_ref, slope_ref, held_ref, sem, *wide):
        copy = pltpu.make_async_copy(gate_hbm, held_ref, sem)
        copy.start()
        copy.wait()
        gate_ref = held_ref if direct else wide[0]
        if not direct:
            gate_ref[...] = held_ref[...].astype(F32)
        start = pl.multiple_of(place_ref[1] * own, own)
        for at, wide in spans(hidden, 512):
            for k in range(blocks):
                from_row = pl.multiple_of(lax.bitwise_xor(place_ref[0], k) * rows, rows)
                value = gate_ref[pl.ds(from_row, rows), at : at + wide].astype(F32)
                silu_ref[k * rows : (k + 1) * rows, at : at + wide] = value / (1.0 + jnp.exp(-value))
            value = gate_ref[pl.ds(start, own), at : at + wide].astype(F32)
            sig = 1.0 / (1.0 + jnp.exp(-value))
            slope_ref[:, at : at + wide] = sig * (1.0 + value * (1.0 - sig))

    return kernel_call(
        body,
        "prepare",
        [shape((tokens, hidden), F32), shape((own, hidden), F32)],
        [place, from_hbm(gate)],
        scratch=[pltpu.VMEM(gate.shape, gate.dtype), pltpu.SemaphoreType.DMA]
        + ([] if direct else [pltpu.VMEM(gate.shape, F32)]),
        smem=1,
        far=1,
    )


def relay(values, after, name):
    count = len(values)

    def body(*refs):
        for k in range(count):
            refs[count + len(after) + k][...] = refs[k][...]

    return kernel_call(body, name, [shape(a.shape, a.dtype) for a in values], [*values, *after], far=len(after))


def first_product(pieces, weight, transposed, part, name, after=()):
    rows, inner = pieces[0].shape
    total = rows * len(pieces)
    base, hidden = part
    direct = rows % 16 == 0
    count = len(pieces)

    def body(*refs):
        piece_refs, weight_ref, (out_ref, *held) = refs[:count], refs[count], refs[count + 1 + len(after) :]
        for k, piece_ref in enumerate(piece_refs):
            held[-1][k * rows : (k + 1) * rows, :] = piece_ref[...].astype(held[-1].dtype)
        if not direct:
            held[0][...] = held[1][...].astype(BF16)
        for at, wide in spans(hidden, 512):
            cut = slice(base + at, base + at + wide)
            if transposed:
                value = lax.dot_general(
                    weight_ref[cut, :], held[0][...], (((1,), (1,)), ((), ())), preferred_element_type=F32
                ).T
            else:
                value = jnp.dot(held[0][...], weight_ref[:, cut], preferred_element_type=F32)
            out_ref[:, at : at + wide] = value

    return kernel_call(
        body,
        name,
        [shape((total, hidden), F32)],
        pieces + [weight] + list(after),
        scratch=[pltpu.VMEM((total, inner), BF16)] + ([] if direct else [pltpu.VMEM((total, inner), F32)]),
        far=len(after),
    )[0]


def second_product(silu, sums, parts, residual, weight, transposed, blocks, name, after=()):
    tokens, hidden = silu.shape
    width = residual.shape[1]
    rows = tokens // blocks
    odd = blocks // 2

    def body(silu_ref, residual_ref, weight_ref, *refs):
        even_out, odd_out, values_ref = refs[-2], refs[-3], refs[-1]
        for k, (base, extent) in enumerate(parts):
            mine_ref, theirs_ref = refs[2 * k], refs[2 * k + 1]
            for at, wide in spans(extent, 256):
                cut, whole = slice(at, at + wide), slice(base + at, base + at + wide)
                values_ref[:, whole] = (silu_ref[:, whole] * (mine_ref[:, cut] + theirs_ref[:, cut])).astype(BF16)
        for at, wide in spans(width, 512):
            cut = slice(at, at + wide)
            if transposed:
                value = lax.dot_general(
                    weight_ref[cut, :], values_ref[...], (((1,), (1,)), ((), ())), preferred_element_type=F32
                ).T
            else:
                value = jnp.dot(values_ref[...], weight_ref[:, cut], preferred_element_type=F32)
            for k in range(blocks):
                piece = value[k * rows : (k + 1) * rows, :]
                if k == 0:
                    piece = piece + residual_ref[:, cut].astype(F32)
                out_ref = odd_out if k % 2 else even_out
                low = k // 2 * rows
                out_ref[low : low + rows, cut] = piece.astype(out_ref.dtype)

    return kernel_call(
        body,
        name,
        [shape((odd * rows, width), BF16), shape((odd * rows, width), F32)],
        [silu, residual, weight] + [a for pair in sums for a in pair] + list(after),
        scratch=[pltpu.VMEM((tokens, hidden), BF16)],
        far=len(after),
    )


def pair_sums(mine, theirs, count, name, after=()):
    rows = mine.shape[0] // count

    def body(mine_ref, theirs_ref, *refs):
        outs = refs[len(after) :]
        for k in range(count):
            low = slice(k * rows, (k + 1) * rows)
            outs[k][...] = (mine_ref[low, :] + theirs_ref[low, :].astype(F32)).astype(BF16)

    return kernel_call(
        body,
        name,
        [shape((rows, mine.shape[1]), BF16)] * count,
        [mine, theirs] + list(after),
        far=len(after),
    )


def gate_gradient(place, slope, up_sums, back_sums, parts, blocks):
    own, hidden = slope.shape
    rows = up_sums[0][0].shape[0] // blocks
    count = own // rows

    def body(place_ref, slope_ref, *refs):
        out_ref = refs[-1]
        for p, (base, extent) in enumerate(parts):
            up_refs, back_refs = refs[2 * p : 2 * p + 2], refs[2 * (len(parts) + p) : 2 * (len(parts) + p) + 2]
            for at, wide in spans(extent, 256):
                cut, whole = slice(at, at + wide), slice(base + at, base + at + wide)
                found = []
                for k in range(count):
                    block = lax.bitwise_xor(place_ref[0], place_ref[1] * count + k)
                    low = pl.ds(pl.multiple_of(block * rows, rows), rows)
                    up = up_refs[0][low, cut] + up_refs[1][low, cut]
                    found.append((back_refs[0][low, cut] + back_refs[1][low, cut]) * up)
                out_ref[:, whole] = (jnp.concatenate(found, axis=0) * slope_ref[:, whole]).astype(BF16)

    return kernel_call(
        body,
        "gate_gradient",
        [shape((own, hidden), BF16)],
        [place, slope] + [a for pair in up_sums + back_sums for a in pair],
        smem=1,
    )[0]


def collect(pieces, name, after=()):
    def body(*refs):
        out_ref, token_ref = refs[-2:]
        total = refs[0][...].astype(F32)
        for ref in refs[1 : len(pieces)]:
            total = total + ref[...].astype(F32)
        out_ref[...] = total.astype(BF16)
        token_ref[...] = jnp.zeros_like(token_ref)

    return kernel_call(
        body,
        name,
        [shape(pieces[0].shape, BF16), shape((8, 128), F32)],
        list(pieces) + list(after),
        far=len(after),
    )


def shards(sections, cols, row_count, inputs, gate_pre, up_weight, down_weight, output_grad):
    own_x, own_g, gate = inputs[0], output_grad[0], gate_pre[0]
    place = jnp.stack([lax.axis_index("col"), lax.axis_index("row")]).astype(jnp.int32)

    def from_xor(value, k):
        return lax.ppermute(value, "col", [(c, c ^ k) for c in range(cols)])

    def to_block(value, k, step):
        pairs = [
            (s * cols + c, (s + step) % sections * cols + (c ^ k)) for s in range(sections) for c in range(cols)
        ]
        return lax.ppermute(value, ("section", "col"), pairs)

    def other_row(value):
        return lax.ppermute(value, "row", [(r, (r + 1) % row_count) for r in range(row_count)])

    even = list(range(2, cols, 2))
    parts = [(0, gate.shape[1])]

    def first_pieces(own):
        return {0: own, **{k: from_xor(own, k) for k in even + [1]}}

    def last_pieces(pieces, after, name):
        for k in even:
            pieces[k + 1] = from_xor(relay([pieces[k]], after, name)[0], 1)
        return [pieces[k] for k in range(cols)]

    def sums_of(pieces, weight, transposed, name, after=()):
        sums = []
        for part in parts:
            mine = first_product(pieces, weight, transposed, part, name + "_%d" % len(sums), after)
            sums.append((mine, other_row(mine)))
            after = [mine]
        return sums

    def finish(mine, theirs, step, name, after):
        blocks = pair_sums(mine, theirs, cols // 2, name, after)
        return blocks[0], [to_block(block, 2 * k, step) for k, block in enumerate(blocks)]

    x_pieces, g_pieces = first_pieces(own_x), first_pieces(own_g)
    silu, slope = prepare(place, gate, row_count, cols)
    x_pieces = last_pieces(x_pieces, [silu, x_pieces[1]], "relay_x")
    g_pieces = last_pieces(g_pieces, [x_pieces[-2]], "relay_g")
    up_sums = sums_of(x_pieces, up_weight, False, "fore_first")
    back_sums = sums_of(g_pieces, down_weight, True, "back_first", [up_sums[-1][0]])
    sent_x, kept_x = second_product(
        silu, up_sums, parts, own_x, down_weight, False, cols, "fore_second", [back_sums[-1][0]]
    )
    other_x = from_xor(sent_x, 1)
    sent_g, kept_g = second_product(silu, back_sums, parts, own_g, up_weight, True, cols, "back_second", [sent_x])
    other_g = from_xor(sent_g, 1)
    token, forward = finish(kept_x, other_x, 1, "fore_pair", [sent_g])
    _, backward = finish(kept_g, other_g, -1, "back_pair", [token])

    gate_grad = gate_gradient(place, slope, up_sums, back_sums, parts, cols)
    handed_forward, token = collect(forward, "fore_collect")
    handed_back, _ = collect(backward, "back_collect", [token])
    return handed_forward[None], gate_grad[None], handed_back[None]


def solution(mesh):
    placed = (
        P("section", "col", "row"),
        P("section", None, "col"),
        P("row", "col"),
        P("col", "row"),
        P("section", "col", "row"),
    )
    sizes = mesh.shape
    return jax.shard_map(
        functools.partial(shards, sizes["section"], sizes["col"], sizes["row"]),
        mesh=mesh,
        in_specs=placed,
        out_specs=(
            P("section", "col", "row"),
            P("section", "row", "col"),
            P("section", "col", "row"),
        ),
        check_vma=False,
    )
```

time: 159 us -> 58.7 us (0.37)
  matrix products: 39.5 us -> 0 us
  blocking collectives: 38.9 us -> 0 us
  waiting for transfers between devices: 56.4 us -> 18.5 us
  Pallas kernels: 0 us -> 18.4 us
  starting transfers between devices: 4.12 us -> 20.9 us
  between operations: 13.8 us -> 0.73 us
  other arithmetic: 4.67 us -> 0.07 us
    reduce_scatter x4 -> x0, waiting for transfers between devices: 51.8 us -> none  [the longest x2 41.9 us: col_product(): lax.psum_scatter(lax.dot_general(gathered, matrix, (contract, ((), ())),...]
    dot_general x4 -> x0, matrix products: 39.5 us -> none  [the longest x2 19.8 us: row_product(): lax.dot_general(gathered, matrix, (contract, ((), ())), preferred_element...]
    all_gather x4 -> x0, blocking collectives: 38.9 us -> none  [the longest x2 34 us: row_product(): gathered = lax.all_gather(pieces, 'col', axis=0, tiled=True)]
    pallas_call x0 -> x12, Pallas kernels: none -> 18.4 us  [kernel_call(): pl.pallas_call(body, name=name, out_shape=outs, in_specs=[SMEM] * smem +...]
    ppermute x2 -> x14, starting transfers between devices: 3.96 us -> 20.9 us  [the longest x4 10.4 us: to_block(): return lax.ppermute(value, ('section', 'col'), pairs)]
    ppermute x2 -> x14, waiting for transfers between devices: 4.49 us -> 18.5 us  [the longest x8 13.9 us: from_xor(): return lax.ppermute(value, 'col', [(c, c ^ k) for c in range(cols)])]
    convert_element_type x3 -> x0, other arithmetic: 4.67 us -> none  [the longest x1 2.72 us: shards(): up_grad = (hidden_grad * gate_used * sigmoid_gate).astype(jnp.bfloat16)]
  transfers between devices with their start and end apart: 6 -> 14, of which waited for: 4 -> 9; matrix products, arithmetic and copies ran while one was open for 12% -> 0% of each run, Pallas kernels for 0% -> 30%
where the time goes in v3:
time: 58.7 us; the launch traced here: 58.6 us
  starting transfers between devices  20.9 us (36%)
  waiting for transfers between devices  18.5 us (32%)
  Pallas kernels  18.4 us (31%)
  between operations  0.73 us (1%)
    pallas_call x12, Pallas kernels, kernel_call(): pl.pallas_call(body, name=name, out_shape=outs, in_specs=[SMEM] * smem +...  18.4 us
    ppermute x8, waiting for transfers between devices, from_xor(): return lax.ppermute(value, 'col', [(c, c ^ k) for c in range(cols)])  13.9 us
    ppermute x4, starting transfers between devices, to_block(): return lax.ppermute(value, ('section', 'col'), pairs)  10.4 us
    ppermute x8, starting transfers between devices, from_xor(): return lax.ppermute(value, 'col', [(c, c ^ k) for c in range(cols)])  10.3 us
    ppermute x4, waiting for transfers between devices, to_block(): return lax.ppermute(value, ('section', 'col'), pairs)  3.81 us
  transfers between devices with their start and end apart: 14, of which 9 were waited for; matrix products, arithmetic and copies ran while one was open for 0% of the time, Pallas kernels for 30%

profile of v3, /device:TPU:0, one launch (start us, length us, event | category | flops | bytes accessed | tf_op | source)
XLA Modules:
  0.0 58.6 jit_solution(10870388864811362225)
XLA Ops:
  0.6 4.1 %collective-permute-start.1 = (bf16[32,2048]{1,0:T(8,128)(2,1)}, bf16[32,2048]{1,0:T(8,128)(2,1)S(1)}, u32[]{:S(2)}, u32[]{:S(2)}) collective-permute-start(bf16[32,2048]{1,0:T(8,128)(2,1)} %bitcast.8), channel_id=1, source_target_pairs={{0,2},{1,3},{2,0},{3,1},{4,6},{5,7},{6,4},{7,5},{8,10},{9,11},{10,... | collective-permute-start | bytes 393224 | tf_op jit(solution)/shard_map/ppermute | solution.py:239
  4.7 1.6 %collective-permute-start = (bf16[32,2048]{1,0:T(8,128)(2,1)}, bf16[32,2048]{1,0:T(8,128)(2,1)S(1)}, u32[]{:S(2)}, u32[]{:S(2)}) collective-permute-start(bf16[32,2048]{1,0:T(8,128)(2,1)} %bitcast.9), channel_id=1, source_target_pairs={{0,1},{1,0},{2,3},{3,2},{4,5},{5,4},{6,7},{7,6},{8,9},{9,8},{10,11... | collective-permute-start | bytes 393224 | tf_op jit(solution)/shard_map/ppermute | solution.py:239
  6.3 0.3 collective-permute-start.5
  6.6 0.1 pad_add_fusion.place_ref
  6.7 2.7 %prepare.1 = (f32[128,3584]{1,0:T(8,128)S(1)}, f32[64,3584]{1,0:T(8,128)S(1)}) custom-call(s32[2]{0:T(128)S(1)} %pad_add_fusion.place_ref, bf16[128,3584]{1,0:T(8,128)(2,1)} %bitcast.17), custom_call_target="tpu_custom_call" | custom-call | flops 5000000000 | tf_op jit(solution)/shard_map/prepare/pallas_call | solution.py:32
  9.5 3.4 %collective-permute-done.1.refs_0_.refs_2_.refs_1_ = bf16[32,2048]{1,0:T(8,128)(2,1)S(1)} collective-permute-done((bf16[32,2048]{1,0:T(8,128)(2,1)}, bf16[32,2048]{1,0:T(8,128)(2,1)S(1)}, u32[]{:S(2)}, u32[]{:S(2)}) %collective-permute-start.1) | collective-permute-done | bytes 131104 | tf_op jit(solution)/shard_map/ppermute | solution.py:239
  12.9 1.3 %collective-permute-start.2 = (bf16[32,2048]{1,0:T(8,128)(2,1)S(1)}, bf16[32,2048]{1,0:T(8,128)(2,1)S(1)}, u32[]{:S(2)}, u32[]{:S(2)}) collective-permute-start(bf16[32,2048]{1,0:T(8,128)(2,1)S(1)} %relay_x.1), channel_id=1, source_target_pairs={{0,1},{1,0},{2,3},{3,2},{4,5},{5,4},{6,7},{7,6},{8,9},{9,8},{10,11... | collective-permute-start | bytes 393224 | tf_op jit(solution)/shard_map/ppermute | solution.py:239
  14.2 0.8 %collective-permute-start.4 = (bf16[32,2048]{1,0:T(8,128)(2,1)S(1)}, bf16[32,2048]{1,0:T(8,128)(2,1)S(1)}, u32[]{:S(2)}, u32[]{:S(2)}) collective-permute-start(bf16[32,2048]{1,0:T(8,128)(2,1)S(1)} %bitcast.13), channel_id=1, source_target_pairs={{0,1},{1,0},{2,3},{3,2},{4,5},{5,4},{6,7},{7,6},{8,9},{9,8},{10,11... | collective-permute-start | bytes 393224 | tf_op jit(solution)/shard_map/ppermute | solution.py:239
  15.0 2.0 %collective-permute-done.5.refs_0_.refs_2_ = bf16[32,2048]{1,0:T(8,128)(2,1)S(1)} collective-permute-done((bf16[32,2048]{1,0:T(8,128)(2,1)}, bf16[32,2048]{1,0:T(8,128)(2,1)S(1)}, u32[]{:S(2)}, u32[]{:S(2)}) %collective-permute-start.5) | collective-permute-done | bytes 131104 | tf_op jit(solution)/shard_map/ppermute | solution.py:239
  17.0 0.8 %collective-permute-start.6 = (bf16[32,2048]{1,0:T(8,128)(2,1)S(1)}, bf16[32,2048]{1,0:T(8,128)(2,1)S(1)}, u32[]{:S(2)}, u32[]{:S(2)}) collective-permute-start(bf16[32,2048]{1,0:T(8,128)(2,1)S(1)} %relay_g.1), channel_id=1, source_target_pairs={{0,1},{1,0},{2,3},{3,2},{4,5},{5,4},{6,7},{7,6},{8,9},{9,8},{10,11... | collective-permute-start | bytes 393224 | tf_op jit(solution)/shard_map/ppermute | solution.py:239
  17.8 1.9 %collective-permute-done.2.refs_3_ = bf16[32,2048]{1,0:T(8,128)(2,1)S(1)} collective-permute-done((bf16[32,2048]{1,0:T(8,128)(2,1)S(1)}, bf16[32,2048]{1,0:T(8,128)(2,1)S(1)}, u32[]{:S(2)}, u32[]{:S(2)}) %collective-permute-start.2) | collective-permute-done | bytes 131104 | tf_op jit(solution)/shard_map/ppermute | solution.py:239
  19.8 2.1 %fore_first_0.1.refs_5_.refs_0_ = f32[128,3584]{1,0:T(8,128)S(1)} custom-call(bf16[32,2048]{1,0:T(8,128)(2,1)S(1)} %bitcast.10, bf16[32,2048]{1,0:T(8,128)(2,1)S(1)} %collective-permute-done.refs_2_.refs_1_, bf16[32,2048]{1,0:T(8,128)(2,1)S(1)} %collective-permute-done.1.refs_0_.refs_2_.refs_1_, bf16[32,2048]{1,0:T(8,128)(2,1)S(1)} %collective-permute-done.2.refs_3_, ...), custom_call_target="tpu_custom_call" | custom-call | tf_op jit(solution)/shard_map/fore_first_0/pallas_call | solution.py:32
  21.8 0.1 collective-permute-start.3
  21.9 0.3 collective-permute-done.4.refs_1_
  22.3 1.4 %collective-permute-done.6.refs_3_ = bf16[32,2048]{1,0:T(8,128)(2,1)S(1)} collective-permute-done((bf16[32,2048]{1,0:T(8,128)(2,1)S(1)}, bf16[32,2048]{1,0:T(8,128)(2,1)S(1)}, u32[]{:S(2)}, u32[]{:S(2)}) %collective-permute-start.6) | collective-permute-done | bytes 131104 | tf_op jit(solution)/shard_map/ppermute | solution.py:239
  23.7 4.0 %back_first_0.1.refs_2_.refs_0_ = f32[128,3584]{1,0:T(8,128)S(1)} custom-call(bf16[32,2048]{1,0:T(8,128)(2,1)S(1)} %bitcast.14, bf16[32,2048]{1,0:T(8,128)(2,1)S(1)} %collective-permute-done.4.refs_1_, bf16[32,2048]{1,0:T(8,128)(2,1)S(1)} %collective-permute-done.5.refs_0_.refs_2_, bf16[32,2048]{1,0:T(8,128)(2,1)S(1)} %collective-permute-done.6.refs_3_, ...), custom_call_target="tpu_custom_call" | custom-call | flops 5000000000 | tf_op jit(solution)/shard_map/back_first_0/pallas_call | solution.py:32
  27.7 0.1 collective-permute-start.8
  27.8 2.3 %fore_second.1 = (bf16[64,2048]{1,0:T(8,128)(2,1)S(1)}, f32[64,2048]{1,0:T(8,128)S(1)}) custom-call(f32[128,3584]{1,0:T(8,128)S(1)} %get-tuple-element.16.refs_1_.silu_ref, bf16[32,2048]{1,0:T(8,128)(2,1)S(1)} %bitcast.11, bf16[3584,2048]{1,0:T(8,128)(2,1)S(1)} %copy-done.1, f32[128,3584]{1,0:T(8,128)S(1)} %fore_first_0.1.refs_5_.refs_0_, ...), custom_call_target="tpu_custom_call" | custom-call | flops 5000000000 | tf_op jit(solution)/shard_map/fore_second/pallas_call | solution.py:32
  30.1 0.7 %collective-permute-start.7 = (bf16[64,2048]{1,0:T(8,128)(2,1)S(1)}, bf16[64,2048]{1,0:T(8,128)(2,1)S(1)}, u32[]{:S(2)}, u32[]{:S(2)}) collective-permute-start(bf16[64,2048]{1,0:T(8,128)(2,1)S(1)} %get-tuple-element.18.refs_2_), channel_id=1, source_target_pairs={{0,1},{1,0},{2,3},{3,2},{4,5},{5,4},{6,7},{7,6},{8,9},{9,8},{10,11... | collective-permute-start | bytes 786440 | tf_op jit(solution)/shard_map/ppermute | solution.py:239
  30.8 0.8 %collective-permute-done.8.refs_1_.refs_3_ = f32[128,3584]{1,0:T(8,128)S(1)} collective-permute-done((f32[128,3584]{1,0:T(8,128)S(1)}, f32[128,3584]{1,0:T(8,128)S(1)}, u32[]{:S(2)}, u32[]{:S(2)}) %collective-permute-start.8) | collective-permute-done | bytes 1835040 | tf_op jit(solution)/shard_map/ppermute | solution.py:248
  31.6 4.1 %back_second.1 = (bf16[64,2048]{1,0:T(8,128)(2,1)S(1)}, f32[64,2048]{1,0:T(8,128)S(1)}) custom-call(f32[128,3584]{1,0:T(8,128)S(1)} %get-tuple-element.16.refs_1_.silu_ref, bf16[32,2048]{1,0:T(8,128)(2,1)S(1)} %bitcast.15, bf16[2048,3584]{1,0:T(8,128)(2,1)S(1)} %copy-done, f32[128,3584]{1,0:T(8,128)S(1)} %back_first_0.1.refs_2_.refs_0_, ...), custom_call_target="tpu_custom_call" | custom-call | flops 5000000000 | tf_op jit(solution)/shard_map/back_second/pallas_call | solution.py:32
  35.7 0.7 %collective-permute-start.11 = (bf16[64,2048]{1,0:T(8,128)(2,1)S(1)}, bf16[64,2048]{1,0:T(8,128)(2,1)S(1)}, u32[]{:S(2)}, u32[]{:S(2)}) collective-permute-start(bf16[64,2048]{1,0:T(8,128)(2,1)S(1)} %get-tuple-element.19.refs_0_), channel_id=1, source_target_pairs={{0,1},{1,0},{2,3},{3,2},{4,5},{5,4},{6,7},{7,6},{8,9},{9,8},{10,11... | collective-permute-start | bytes 786440 | tf_op jit(solution)/shard_map/ppermute | solution.py:239
  36.4 2.9 %collective-permute-done.7.theirs_ref = bf16[64,2048]{1,0:T(8,128)(2,1)S(1)} collective-permute-done((bf16[64,2048]{1,0:T(8,128)(2,1)S(1)}, bf16[64,2048]{1,0:T(8,128)(2,1)S(1)}, u32[]{:S(2)}, u32[]{:S(2)}) %collective-permute-start.7) | collective-permute-done | bytes 262176 | tf_op jit(solution)/shard_map/ppermute | solution.py:239
  39.3 4.6 %collective-permute-start.10 = (bf16[32,2048]{1,0:T(8,128)(2,1)S(1)}, bf16[32,2048]{1,0:T(8,128)(2,1)S(1)}, u32[]{:S(2)}, u32[]{:S(2)}) collective-permute-start(bf16[32,2048]{1,0:T(8,128)(2,1)S(1)} %get-tuple-element.21), channel_id=1, source_target_pairs={{0,10},{1,11},{2,8},{3,9},{8,18},{9,19},{10,16},{11,17},{16,26},{1... | collective-permute-start | bytes 393224 | tf_op jit(solution)/shard_map/ppermute | solution.py:245
  43.9 1.5 %collective-permute-start.9 = (bf16[32,2048]{1,0:T(8,128)(2,1)S(1)}, bf16[32,2048]{1,0:T(8,128)(2,1)S(1)}, u32[]{:S(2)}, u32[]{:S(2)}) collective-permute-start(bf16[32,2048]{1,0:T(8,128)(2,1)S(1)} %get-tuple-element.20.refs_0_), channel_id=1, source_target_pairs={{0,8},{1,9},{2,10},{3,11},{8,16},{9,17},{10,18},{11,19},{16,24},{1... | collective-permute-start | bytes 393224 | tf_op jit(solution)/shard_map/ppermute | solution.py:245
  45.4 1.9 %collective-permute-done.11.theirs_ref = bf16[64,2048]{1,0:T(8,128)(2,1)S(1)} collective-permute-done((bf16[64,2048]{1,0:T(8,128)(2,1)S(1)}, bf16[64,2048]{1,0:T(8,128)(2,1)S(1)}, u32[]{:S(2)}, u32[]{:S(2)}) %collective-permute-start.11) | collective-permute-done | bytes 262176 | tf_op jit(solution)/shard_map/ppermute | solution.py:239
  47.4 2.5 %collective-permute-start.12 = (bf16[32,2048]{1,0:T(8,128)(2,1)S(1)}, bf16[32,2048]{1,0:T(8,128)(2,1)S(1)}, u32[]{:S(2)}, u32[]{:S(2)}) collective-permute-start(bf16[32,2048]{1,0:T(8,128)(2,1)S(1)} %get-tuple-element.25), channel_id=1, source_target_pairs={{0,24},{1,25},{2,26},{3,27},{8,0},{9,1},{10,2},{11,3},{16,8},{17,9... | collective-permute-start | bytes 393224 | tf_op jit(solution)/shard_map/ppermute | solution.py:245
  49.9 1.8 %collective-permute-start.13 = (bf16[32,2048]{1,0:T(8,128)(2,1)S(1)}, bf16[32,2048]{1,0:T(8,128)(2,1)S(1)}, u32[]{:S(2)}, u32[]{:S(2)}) collective-permute-start(bf16[32,2048]{1,0:T(8,128)(2,1)S(1)} %get-tuple-element.26), channel_id=1, source_target_pairs={{0,26},{1,27},{2,24},{3,25},{8,2},{9,3},{10,0},{11,1},{16,10},{17,... | collective-permute-start | bytes 393224 | tf_op jit(solution)/shard_map/ppermute | solution.py:245
  51.7 1.6 %gate_gradient.1 = bf16[64,3584]{1,0:T(8,128)(2,1)} custom-call(s32[2]{0:T(128)S(1)} %pad_add_fusion.place_ref, f32[64,3584]{1,0:T(8,128)S(1)} %get-tuple-element.23.slope_ref, f32[128,3584]{1,0:T(8,128)S(1)} %fore_first_0.1.refs_5_.refs_0_, f32[128,3584]{1,0:T(8,128)S(1)} %collective-permute-done.3.refs_1_, f32[128,3584]{1,0:T(8,128)S(1)} %back_first_0.1.refs_2_.refs_0_, ...), custom_call_target="tpu_custom_call" | custom-call | tf_op jit(solution)/shard_map/gate_gradient/pallas_call | solution.py:32
  53.4 0.7 %fore_collect.1 = (bf16[32,2048]{1,0:T(8,128)(2,1)}, f32[8,128]{1,0:T(8,128)S(1)}) custom-call(bf16[32,2048]{1,0:T(8,128)(2,1)S(1)} %collective-permute-done.9.refs_0_, bf16[32,2048]{1,0:T(8,128)(2,1)S(1)} %collective-permute-done.10.refs_1_), custom_call_target="tpu_custom_call" | custom-call | tf_op jit(solution)/shard_map/fore_collect/pallas_call | solution.py:32
  54.1 3.8 %collective-permute-done.13.refs_1_ = bf16[32,2048]{1,0:T(8,128)(2,1)S(1)} collective-permute-done((bf16[32,2048]{1,0:T(8,128)(2,1)S(1)}, bf16[32,2048]{1,0:T(8,128)(2,1)S(1)}, u32[]{:S(2)}, u32[]{:S(2)}) %collective-permute-start.13) | collective-permute-done | bytes 131104 | tf_op jit(solution)/shard_map/ppermute | solution.py:245
  57.9 0.7 %back_collect.1 = (bf16[32,2048]{1,0:T(8,128)(2,1)}, f32[8,128]{1,0:T(8,128)}) custom-call(bf16[32,2048]{1,0:T(8,128)(2,1)S(1)} %collective-permute-done.12.refs_0_, bf16[32,2048]{1,0:T(8,128)(2,1)S(1)} %collective-permute-done.13.refs_1_, f32[8,128]{1,0:T(8,128)S(1)} %get-tuple-element.27.refs_2_), custom_call_target="tpu_custom_call" | custom-call | tf_op jit(solution)/shard_map/back_collect/pallas_call | solution.py:32
  (17 shorter events, 0.1 us)
Async XLA Ops:
  0.6 12.3 %collective-permute-start.1 = (bf16[32,2048]{1,0:T(8,128)(2,1)}, bf16[32,2048]{1,0:T(8,128)(2,1)S(1)}, u32[]{:S(2)}, u32[]{:S(2)}) collective-permute-start(bf16[32,2048]{1,0:T(8,128)(2,1)} %bitcast.8), channel_id=1, source_target_pairs={{0,2},{1,3},{2,0},{3,1},{4,6},{5,7},{6,4},{7,5},{8,10},{9,11},{10,... | collective-permute-start | bytes 393224 | tf_op jit(solution)/shard_map/ppermute | solution.py:239
  4.7 8.2 %collective-permute-start = (bf16[32,2048]{1,0:T(8,128)(2,1)}, bf16[32,2048]{1,0:T(8,128)(2,1)S(1)}, u32[]{:S(2)}, u32[]{:S(2)}) collective-permute-start(bf16[32,2048]{1,0:T(8,128)(2,1)} %bitcast.9), channel_id=1, source_target_pairs={{0,1},{1,0},{2,3},{3,2},{4,5},{5,4},{6,7},{7,6},{8,9},{9,8},{10,11... | collective-permute-start | bytes 393224 | tf_op jit(solution)/shard_map/ppermute | solution.py:239
  6.3 10.7 %collective-permute-start.5 = (bf16[32,2048]{1,0:T(8,128)(2,1)}, bf16[32,2048]{1,0:T(8,128)(2,1)S(1)}, u32[]{:S(2)}, u32[]{:S(2)}) collective-permute-start(bf16[32,2048]{1,0:T(8,128)(2,1)} %bitcast.12), channel_id=1, source_target_pairs={{0,2},{1,3},{2,0},{3,1},{4,6},{5,7},{6,4},{7,5},{8,10},{9,11},{10,... | collective-permute-start | bytes 393224 | tf_op jit(solution)/shard_map/ppermute | solution.py:239
  6.7 13.1 %copy-start = (bf16[2048,3584]{1,0:T(8,128)(2,1)S(1)}, bf16[2048,3584]{1,0:T(8,128)(2,1)}, u32[]{:S(2)}) copy-start(bf16[2048,3584]{1,0:T(8,128)(2,1)} %weight_ref.3) | copy-start | bytes 44040196
  9.5 4.8 %copy-start.3 = (bf16[1,32,2048]{2,1,0:T(8,128)(2,1)S(1)}, bf16[1,32,2048]{2,1,0:T(8,128)(2,1)}, u32[]{:S(2)}) copy-start(bf16[1,32,2048]{2,1,0:T(8,128)(2,1)} %param.9) | copy-start | bytes 393220
  9.5 10.3 %copy-start.2 = (bf16[1,32,2048]{2,1,0:T(8,128)(2,1)S(1)}, bf16[1,32,2048]{2,1,0:T(8,128)(2,1)}, u32[]{:S(2)}) copy-start(bf16[1,32,2048]{2,1,0:T(8,128)(2,1)} %param.5) | copy-start | bytes 393220
  12.9 6.9 %collective-permute-start.2 = (bf16[32,2048]{1,0:T(8,128)(2,1)S(1)}, bf16[32,2048]{1,0:T(8,128)(2,1)S(1)}, u32[]{:S(2)}, u32[]{:S(2)}) collective-permute-start(bf16[32,2048]{1,0:T(8,128)(2,1)S(1)} %relay_x.1), channel_id=1, source_target_pairs={{0,1},{1,0},{2,3},{3,2},{4,5},{5,4},{6,7},{7,6},{8,9},{9,8},{10,11... | collective-permute-start | bytes 393224 | tf_op jit(solution)/shard_map/ppermute | solution.py:239
  14.2 8.0 %collective-permute-start.4 = (bf16[32,2048]{1,0:T(8,128)(2,1)S(1)}, bf16[32,2048]{1,0:T(8,128)(2,1)S(1)}, u32[]{:S(2)}, u32[]{:S(2)}) collective-permute-start(bf16[32,2048]{1,0:T(8,128)(2,1)S(1)} %bitcast.13), channel_id=1, source_target_pairs={{0,1},{1,0},{2,3},{3,2},{4,5},{5,4},{6,7},{7,6},{8,9},{9,8},{10,11... | collective-permute-start | bytes 393224 | tf_op jit(solution)/shard_map/ppermute | solution.py:239
  17.0 6.7 %copy-start.1 = (bf16[3584,2048]{1,0:T(8,128)(2,1)S(1)}, bf16[3584,2048]{1,0:T(8,128)(2,1)}, u32[]{:S(2)}) copy-start(bf16[3584,2048]{1,0:T(8,128)(2,1)} %weight_ref.2) | copy-start | bytes 44040196
  17.0 6.7 %collective-permute-start.6 = (bf16[32,2048]{1,0:T(8,128)(2,1)S(1)}, bf16[32,2048]{1,0:T(8,128)(2,1)S(1)}, u32[]{:S(2)}, u32[]{:S(2)}) collective-permute-start(bf16[32,2048]{1,0:T(8,128)(2,1)S(1)} %relay_g.1), channel_id=1, source_target_pairs={{0,1},{1,0},{2,3},{3,2},{4,5},{5,4},{6,7},{7,6},{8,9},{9,8},{10,11... | collective-permute-start | bytes 393224 | tf_op jit(solution)/shard_map/ppermute | solution.py:239
  21.8 5.9 %collective-permute-start.3 = (f32[128,3584]{1,0:T(8,128)S(1)}, f32[128,3584]{1,0:T(8,128)S(1)}, u32[]{:S(2)}, u32[]{:S(2)}) collective-permute-start(f32[128,3584]{1,0:T(8,128)S(1)} %fore_first_0.1.refs_5_.refs_0_), channel_id=1, source_target_pairs={{0,4},{4,0},{1,5},{5,1},{2,6},{6,2},{3,7},{7,3},{8,12},{12,8},{9,1... | collective-permute-start | bytes 5505032 | tf_op jit(solution)/shard_map/ppermute | solution.py:248
  27.7 3.8 %collective-permute-start.8 = (f32[128,3584]{1,0:T(8,128)S(1)}, f32[128,3584]{1,0:T(8,128)S(1)}, u32[]{:S(2)}, u32[]{:S(2)}) collective-permute-start(f32[128,3584]{1,0:T(8,128)S(1)} %back_first_0.1.refs_2_.refs_0_), channel_id=1, source_target_pairs={{0,4},{4,0},{1,5},{5,1},{2,6},{6,2},{3,7},{7,3},{8,12},{12,8},{9,1... | collective-permute-start | bytes 5505032 | tf_op jit(solution)/shard_map/ppermute | solution.py:248
  30.1 9.2 %collective-permute-start.7 = (bf16[64,2048]{1,0:T(8,128)(2,1)S(1)}, bf16[64,2048]{1,0:T(8,128)(2,1)S(1)}, u32[]{:S(2)}, u32[]{:S(2)}) collective-permute-start(bf16[64,2048]{1,0:T(8,128)(2,1)S(1)} %get-tuple-element.18.refs_2_), channel_id=1, source_target_pairs={{0,1},{1,0},{2,3},{3,2},{4,5},{5,4},{6,7},{7,6},{8,9},{9,8},{10,11... | collective-permute-start | bytes 786440 | tf_op jit(solution)/shard_map/ppermute | solution.py:239
  35.7 11.6 %collective-permute-start.11 = (bf16[64,2048]{1,0:T(8,128)(2,1)S(1)}, bf16[64,2048]{1,0:T(8,128)(2,1)S(1)}, u32[]{:S(2)}, u32[]{:S(2)}) collective-permute-start(bf16[64,2048]{1,0:T(8,128)(2,1)S(1)} %get-tuple-element.19.refs_0_), channel_id=1, source_target_pairs={{0,1},{1,0},{2,3},{3,2},{4,5},{5,4},{6,7},{7,6},{8,9},{9,8},{10,11... | collective-permute-start | bytes 786440 | tf_op jit(solution)/shard_map/ppermute | solution.py:239
  39.3 14.0 %collective-permute-start.10 = (bf16[32,2048]{1,0:T(8,128)(2,1)S(1)}, bf16[32,2048]{1,0:T(8,128)(2,1)S(1)}, u32[]{:S(2)}, u32[]{:S(2)}) collective-permute-start(bf16[32,2048]{1,0:T(8,128)(2,1)S(1)} %get-tuple-element.21), channel_id=1, source_target_pairs={{0,10},{1,11},{2,8},{3,9},{8,18},{9,19},{10,16},{11,17},{16,26},{1... | collective-permute-start | bytes 393224 | tf_op jit(solution)/shard_map/ppermute | solution.py:245
  43.9 9.5 %collective-permute-start.9 = (bf16[32,2048]{1,0:T(8,128)(2,1)S(1)}, bf16[32,2048]{1,0:T(8,128)(2,1)S(1)}, u32[]{:S(2)}, u32[]{:S(2)}) collective-permute-start(bf16[32,2048]{1,0:T(8,128)(2,1)S(1)} %get-tuple-element.20.refs_0_), channel_id=1, source_target_pairs={{0,8},{1,9},{2,10},{3,11},{8,16},{9,17},{10,18},{11,19},{16,24},{1... | collective-permute-start | bytes 393224 | tf_op jit(solution)/shard_map/ppermute | solution.py:245
  47.4 6.7 %collective-permute-start.12 = (bf16[32,2048]{1,0:T(8,128)(2,1)S(1)}, bf16[32,2048]{1,0:T(8,128)(2,1)S(1)}, u32[]{:S(2)}, u32[]{:S(2)}) collective-permute-start(bf16[32,2048]{1,0:T(8,128)(2,1)S(1)} %get-tuple-element.25), channel_id=1, source_target_pairs={{0,24},{1,25},{2,26},{3,27},{8,0},{9,1},{10,2},{11,3},{16,8},{17,9... | collective-permute-start | bytes 393224 | tf_op jit(solution)/shard_map/ppermute | solution.py:245
  49.9 8.0 %collective-permute-start.13 = (bf16[32,2048]{1,0:T(8,128)(2,1)S(1)}, bf16[32,2048]{1,0:T(8,128)(2,1)S(1)}, u32[]{:S(2)}, u32[]{:S(2)}) collective-permute-start(bf16[32,2048]{1,0:T(8,128)(2,1)S(1)} %get-tuple-element.26), channel_id=1, source_target_pairs={{0,26},{1,27},{2,24},{3,25},{8,2},{9,3},{10,0},{11,1},{16,10},{17,... | collective-permute-start | bytes 393224 | tf_op jit(solution)/shard_map/ppermute | solution.py:245

commit v4 on v3

--- a/solution.py
+++ b/solution.py
@@ -8,7 +8,7 @@
 from jax.sharding import PartitionSpec as P
 
 MIB = 1 << 20
-COST = {'prepare': 5000000000, 'back_first_0': 5000000000, 'back_second': 5000000000, 'fore_second': 5000000000}
+COST = {"prepare": 5_000_000_000, "back_first_0": 5_000_000_000, "back_second": 5_000_000_000, "fore_second": 5_000_000_000}
 VMEM = pl.BlockSpec(memory_space=pltpu.VMEM)
 SMEM = pl.BlockSpec(memory_space=pltpu.SMEM)
 ANY = pl.BlockSpec(memory_space=pl.ANY)
@@ -39,16 +39,6 @@
         compiler_params=pltpu.CompilerParams(vmem_limit_bytes=limit),
         cost_estimate=pl.CostEstimate(flops=COST.get(name, 0), bytes_accessed=0, transcendentals=0),
     )(*args)
-
-
-def row_copies(source, target, sems, cuts):
-    deep = target.shape[0] // cuts
-    return [
-        pltpu.make_async_copy(
-            source.at[pl.ds(c * deep, deep), :], target.at[pl.ds(c * deep, deep), :], sems.at[c]
-        )
-        for c in range(cuts)
-    ]
 
 
 def prepare(place, gate, row_count, blocks):
@@ -128,14 +118,14 @@
     )[0]
 
 
-def second_product(silu, sums, parts, residual, weight, transposed, blocks, name, after=()):
+def second_product(silu, sums, parts, residual, weight, transposed, blocks, groups, name, after=()):
     tokens, hidden = silu.shape
     width = residual.shape[1]
     rows = tokens // blocks
     odd = blocks // 2
 
     def body(silu_ref, residual_ref, weight_ref, *refs):
-        even_out, odd_out, values_ref = refs[-2], refs[-3], refs[-1]
+        odd_outs, even_out, values_ref = refs[-2 - len(groups) : -2], refs[-2], refs[-1]
         for k, (base, extent) in enumerate(parts):
             mine_ref, theirs_ref = refs[2 * k], refs[2 * k + 1]
             for at, wide in spans(extent, 256):
@@ -153,33 +143,36 @@
                 piece = value[k * rows : (k + 1) * rows, :]
                 if k == 0:
                     piece = piece + residual_ref[:, cut].astype(F32)
-                out_ref = odd_out if k % 2 else even_out
-                low = k // 2 * rows
+                out_ref, low = even_out, k // 2 * rows
+                if k % 2:
+                    out_ref, low = next(
+                        (ref, group.index(k // 2) * rows) for ref, group in zip(odd_outs, groups) if k // 2 in group
+                    )
                 out_ref[low : low + rows, cut] = piece.astype(out_ref.dtype)
 
     return kernel_call(
         body,
         name,
-        [shape((odd * rows, width), BF16), shape((odd * rows, width), F32)],
+        [shape((len(group) * rows, width), BF16) for group in groups] + [shape((odd * rows, width), F32)],
         [silu, residual, weight] + [a for pair in sums for a in pair] + list(after),
         scratch=[pltpu.VMEM((tokens, hidden), BF16)],
         far=len(after),
     )
 
 
-def pair_sums(mine, theirs, count, name, after=()):
+def pair_sums(mine, theirs, group, count, name, after=()):
     rows = mine.shape[0] // count
 
     def body(mine_ref, theirs_ref, *refs):
         outs = refs[len(after) :]
-        for k in range(count):
-            low = slice(k * rows, (k + 1) * rows)
-            outs[k][...] = (mine_ref[low, :] + theirs_ref[low, :].astype(F32)).astype(BF16)
+        for k, j in enumerate(group):
+            near, far = slice(j * rows, (j + 1) * rows), slice(k * rows, (k + 1) * rows)
+            outs[k][...] = (mine_ref[near, :] + theirs_ref[far, :].astype(F32)).astype(BF16)
 
     return kernel_call(
         body,
         name,
-        [shape((rows, mine.shape[1]), BF16)] * count,
+        [shape((rows, mine.shape[1]), BF16)] * len(group),
         [mine, theirs] + list(after),
         far=len(after),
     )
@@ -266,9 +259,13 @@
             after = [mine]
         return sums
 
-    def finish(mine, theirs, step, name, after):
-        blocks = pair_sums(mine, theirs, cols // 2, name, after)
-        return blocks[0], [to_block(block, 2 * k, step) for k, block in enumerate(blocks)]
+    def finish(mine, theirs, groups, step, name, after):
+        arrived = []
+        for array, group in zip(theirs, groups):
+            blocks = pair_sums(mine, array, group, cols // 2, name + "_%d" % len(arrived), after)
+            arrived += [to_block(block, 2 * j, step) for j, block in zip(group, blocks)]
+            after = [blocks[0]]
+        return after[0], arrived
 
     x_pieces, g_pieces = first_pieces(own_x), first_pieces(own_g)
     silu, slope = prepare(place, gate, row_count, cols)
@@ -276,14 +273,17 @@
     g_pieces = last_pieces(g_pieces, [x_pieces[-2]], "relay_g")
     up_sums = sums_of(x_pieces, up_weight, False, "fore_first")
     back_sums = sums_of(g_pieces, down_weight, True, "back_first", [up_sums[-1][0]])
-    sent_x, kept_x = second_product(
-        silu, up_sums, parts, own_x, down_weight, False, cols, "fore_second", [back_sums[-1][0]]
-    )
-    other_x = from_xor(sent_x, 1)
-    sent_g, kept_g = second_product(silu, back_sums, parts, own_g, up_weight, True, cols, "back_second", [sent_x])
-    other_g = from_xor(sent_g, 1)
-    token, forward = finish(kept_x, other_x, 1, "fore_pair", [sent_g])
-    _, backward = finish(kept_g, other_g, -1, "back_pair", [token])
+    groups = [list(range(1, cols // 2)), [0]]
+    *sent_x, kept_x = second_product(
+        silu, up_sums, parts, own_x, down_weight, False, cols, groups, "fore_second", [back_sums[-1][0]]
+    )
+    other_x = [from_xor(sent, 1) for sent in sent_x]
+    *sent_g, kept_g = second_product(
+        silu, back_sums, parts, own_g, up_weight, True, cols, groups, "back_second", sent_x[:1]
+    )
+    other_g = [from_xor(sent, 1) for sent in sent_g]
+    token, forward = finish(kept_x, other_x, groups, 1, "fore_pair", sent_g[:1])
+    _, backward = finish(kept_g, other_g, groups, -1, "back_pair", [token])
 
     gate_grad = gate_gradient(place, slope, up_sums, back_sums, parts, cols)
     handed_forward, token = collect(forward, "fore_collect")

time: 58.7 us -> 58.2 us (level)
  waiting for transfers between devices: 18.5 us -> 14.6 us
  starting transfers between devices: 20.9 us -> 24.2 us
    ppermute x8 -> x10, starting transfers between devices: 10.3 us -> 13.1 us  [from_xor(): return lax.ppermute(value, 'col', [(c, c ^ k) for c in range(cols)])]
    ppermute x8 -> x10, waiting for transfers between devices: 13.9 us -> 11.4 us  [from_xor(): return lax.ppermute(value, 'col', [(c, c ^ k) for c in range(cols)])]
    ppermute x2, waiting for transfers between devices: 0.77 us -> 0.01 us  [other_row(): lax.ppermute(value, 'row', [(r, (r + 1) % row_count) for r in range(row_c...]
    pallas_call x12 -> x14, Pallas kernels: 18.4 us -> 18.4 us  [kernel_call(): pl.pallas_call(body, name=name, out_shape=outs, in_specs=[SMEM] * smem +...]
  transfers between devices with their start and end apart: 14 -> 16, of which waited for: 9 -> 8; matrix products, arithmetic and copies ran while one was open for 0% -> 0% of each run, Pallas kernels for 30% -> 30%
where the time goes in v4:
time: 58.2 us; the launch traced here: 58.1 us
  starting transfers between devices  24.2 us (42%)
  Pallas kernels  18.4 us (32%)
  waiting for transfers between devices  14.6 us (25%)
  between operations  0.74 us (1%)
    pallas_call x14, Pallas kernels, kernel_call(): pl.pallas_call(body, name=name, out_shape=outs, in_specs=[SMEM] * smem +...  18.4 us
    ppermute x10, starting transfers between devices, from_xor(): return lax.ppermute(value, 'col', [(c, c ^ k) for c in range(cols)])  13.1 us
    ppermute x10, waiting for transfers between devices, from_xor(): return lax.ppermute(value, 'col', [(c, c ^ k) for c in range(cols)])  11.4 us
    ppermute x4, starting transfers between devices, to_block(): return lax.ppermute(value, ('section', 'col'), pairs)  11 us
    ppermute x4, waiting for transfers between devices, to_block(): return lax.ppermute(value, ('section', 'col'), pairs)  3.26 us
  transfers between devices with their start and end apart: 16, of which 8 were waited for; matrix products, arithmetic and copies ran while one was open for 0% of the time, Pallas kernels for 30%

profile of v4, /device:TPU:0, one launch (start us, length us, event | category | flops | bytes accessed | tf_op | source)
XLA Modules:
  0.0 58.1 jit_solution(13914547292361327968)
XLA Ops:
  0.6 4.1 %collective-permute-start.1 = (bf16[32,2048]{1,0:T(8,128)(2,1)}, bf16[32,2048]{1,0:T(8,128)(2,1)S(1)}, u32[]{:S(2)}, u32[]{:S(2)}) collective-permute-start(bf16[32,2048]{1,0:T(8,128)(2,1)} %bitcast.8), channel_id=1, source_target_pairs={{0,2},{1,3},{2,0},{3,1},{4,6},{5,7},{6,4},{7,5},{8,10},{9,11},{10,... | collective-permute-start | bytes 393224 | tf_op jit(solution)/shard_map/ppermute | solution.py:232
  4.7 1.6 %collective-permute-start = (bf16[32,2048]{1,0:T(8,128)(2,1)}, bf16[32,2048]{1,0:T(8,128)(2,1)S(1)}, u32[]{:S(2)}, u32[]{:S(2)}) collective-permute-start(bf16[32,2048]{1,0:T(8,128)(2,1)} %bitcast.9), channel_id=1, source_target_pairs={{0,1},{1,0},{2,3},{3,2},{4,5},{5,4},{6,7},{7,6},{8,9},{9,8},{10,11... | collective-permute-start | bytes 393224 | tf_op jit(solution)/shard_map/ppermute | solution.py:232
  6.3 0.3 collective-permute-start.5
  6.6 0.1 pad_add_fusion.place_ref
  6.7 2.7 %prepare.1 = (f32[128,3584]{1,0:T(8,128)S(1)}, f32[64,3584]{1,0:T(8,128)S(1)}) custom-call(s32[2]{0:T(128)S(1)} %pad_add_fusion.place_ref, bf16[128,3584]{1,0:T(8,128)(2,1)} %bitcast.17), custom_call_target="tpu_custom_call" | custom-call | flops 5000000000 | tf_op jit(solution)/shard_map/prepare/pallas_call | solution.py:32
  9.5 3.4 %collective-permute-done.1.refs_0_.refs_2_.refs_1_ = bf16[32,2048]{1,0:T(8,128)(2,1)S(1)} collective-permute-done((bf16[32,2048]{1,0:T(8,128)(2,1)}, bf16[32,2048]{1,0:T(8,128)(2,1)S(1)}, u32[]{:S(2)}, u32[]{:S(2)}) %collective-permute-start.1) | collective-permute-done | bytes 131104 | tf_op jit(solution)/shard_map/ppermute | solution.py:232
  12.9 1.3 %collective-permute-start.2 = (bf16[32,2048]{1,0:T(8,128)(2,1)S(1)}, bf16[32,2048]{1,0:T(8,128)(2,1)S(1)}, u32[]{:S(2)}, u32[]{:S(2)}) collective-permute-start(bf16[32,2048]{1,0:T(8,128)(2,1)S(1)} %relay_x.1), channel_id=1, source_target_pairs={{0,1},{1,0},{2,3},{3,2},{4,5},{5,4},{6,7},{7,6},{8,9},{9,8},{10,11... | collective-permute-start | bytes 393224 | tf_op jit(solution)/shard_map/ppermute | solution.py:232
  14.2 0.8 %collective-permute-start.4 = (bf16[32,2048]{1,0:T(8,128)(2,1)S(1)}, bf16[32,2048]{1,0:T(8,128)(2,1)S(1)}, u32[]{:S(2)}, u32[]{:S(2)}) collective-permute-start(bf16[32,2048]{1,0:T(8,128)(2,1)S(1)} %bitcast.13), channel_id=1, source_target_pairs={{0,1},{1,0},{2,3},{3,2},{4,5},{5,4},{6,7},{7,6},{8,9},{9,8},{10,11... | collective-permute-start | bytes 393224 | tf_op jit(solution)/shard_map/ppermute | solution.py:232
  15.0 2.0 %collective-permute-done.5.refs_0_.refs_2_ = bf16[32,2048]{1,0:T(8,128)(2,1)S(1)} collective-permute-done((bf16[32,2048]{1,0:T(8,128)(2,1)}, bf16[32,2048]{1,0:T(8,128)(2,1)S(1)}, u32[]{:S(2)}, u32[]{:S(2)}) %collective-permute-start.5) | collective-permute-done | bytes 131104 | tf_op jit(solution)/shard_map/ppermute | solution.py:232
  17.0 0.8 %collective-permute-start.6 = (bf16[32,2048]{1,0:T(8,128)(2,1)S(1)}, bf16[32,2048]{1,0:T(8,128)(2,1)S(1)}, u32[]{:S(2)}, u32[]{:S(2)}) collective-permute-start(bf16[32,2048]{1,0:T(8,128)(2,1)S(1)} %relay_g.1), channel_id=1, source_target_pairs={{0,1},{1,0},{2,3},{3,2},{4,5},{5,4},{6,7},{7,6},{8,9},{9,8},{10,11... | collective-permute-start | bytes 393224 | tf_op jit(solution)/shard_map/ppermute | solution.py:232
  17.8 1.9 %collective-permute-done.2.refs_3_ = bf16[32,2048]{1,0:T(8,128)(2,1)S(1)} collective-permute-done((bf16[32,2048]{1,0:T(8,128)(2,1)S(1)}, bf16[32,2048]{1,0:T(8,128)(2,1)S(1)}, u32[]{:S(2)}, u32[]{:S(2)}) %collective-permute-start.2) | collective-permute-done | bytes 131104 | tf_op jit(solution)/shard_map/ppermute | solution.py:232
  19.8 2.1 %fore_first_0.1.refs_5_.refs_0_ = f32[128,3584]{1,0:T(8,128)S(1)} custom-call(bf16[32,2048]{1,0:T(8,128)(2,1)S(1)} %bitcast.10, bf16[32,2048]{1,0:T(8,128)(2,1)S(1)} %collective-permute-done.refs_2_.refs_1_, bf16[32,2048]{1,0:T(8,128)(2,1)S(1)} %collective-permute-done.1.refs_0_.refs_2_.refs_1_, bf16[32,2048]{1,0:T(8,128)(2,1)S(1)} %collective-permute-done.2.refs_3_, ...), custom_call_target="tpu_custom_call" | custom-call | tf_op jit(solution)/shard_map/fore_first_0/pallas_call | solution.py:32
  21.8 0.1 collective-permute-start.3
  21.9 0.3 collective-permute-done.4.refs_1_
  22.3 1.4 %collective-permute-done.6.refs_3_ = bf16[32,2048]{1,0:T(8,128)(2,1)S(1)} collective-permute-done((bf16[32,2048]{1,0:T(8,128)(2,1)S(1)}, bf16[32,2048]{1,0:T(8,128)(2,1)S(1)}, u32[]{:S(2)}, u32[]{:S(2)}) %collective-permute-start.6) | collective-permute-done | bytes 131104 | tf_op jit(solution)/shard_map/ppermute | solution.py:232
  23.7 4.0 %back_first_0.1.refs_2_.refs_0_ = f32[128,3584]{1,0:T(8,128)S(1)} custom-call(bf16[32,2048]{1,0:T(8,128)(2,1)S(1)} %bitcast.14, bf16[32,2048]{1,0:T(8,128)(2,1)S(1)} %collective-permute-done.4.refs_1_, bf16[32,2048]{1,0:T(8,128)(2,1)S(1)} %collective-permute-done.5.refs_0_.refs_2_, bf16[32,2048]{1,0:T(8,128)(2,1)S(1)} %collective-permute-done.6.refs_3_, ...), custom_call_target="tpu_custom_call" | custom-call | flops 5000000000 | tf_op jit(solution)/shard_map/back_first_0/pallas_call | solution.py:32
  27.8 2.3 %fore_second.1 = (bf16[32,2048]{1,0:T(8,128)(2,1)S(1)}, bf16[32,2048]{1,0:T(8,128)(2,1)S(1)}, f32[64,2048]{1,0:T(8,128)S(1)}) custom-call(f32[128,3584]{1,0:T(8,128)S(1)} %get-tuple-element.14.refs_1_.silu_ref, bf16[32,2048]{1,0:T(8,128)(2,1)S(1)} %bitcast.11, bf16[3584,2048]{1,0:T(8,128)(2,1)S(1)} %copy-done.1, ...), custom_call_target="tpu_custom_call" | custom-call | flops 5000000000 | tf_op jit(solution)/shard_map/fore_second/pallas_call | solution.py:32
  30.1 0.7 %collective-permute-start.10 = (bf16[32,2048]{1,0:T(8,128)(2,1)S(1)}, bf16[32,2048]{1,0:T(8,128)(2,1)S(1)}, u32[]{:S(2)}, u32[]{:S(2)}) collective-permute-start(bf16[32,2048]{1,0:T(8,128)(2,1)S(1)} %get-tuple-element.18), channel_id=1, source_target_pairs={{0,1},{1,0},{2,3},{3,2},{4,5},{5,4},{6,7},{7,6},{8,9},{9,8},{10,11... | collective-permute-start | bytes 393224 | tf_op jit(solution)/shard_map/ppermute | solution.py:232
  30.8 1.4 %collective-permute-start.7 = (bf16[32,2048]{1,0:T(8,128)(2,1)S(1)}, bf16[32,2048]{1,0:T(8,128)(2,1)S(1)}, u32[]{:S(2)}, u32[]{:S(2)}) collective-permute-start(bf16[32,2048]{1,0:T(8,128)(2,1)S(1)} %get-tuple-element.16.refs_2_), channel_id=1, source_target_pairs={{0,1},{1,0},{2,3},{3,2},{4,5},{5,4},{6,7},{7,6},{8,9},{9,8},{10,11... | collective-permute-start | bytes 393224 | tf_op jit(solution)/shard_map/ppermute | solution.py:232
  32.2 4.1 %back_second.1 = (bf16[32,2048]{1,0:T(8,128)(2,1)S(1)}, bf16[32,2048]{1,0:T(8,128)(2,1)S(1)}, f32[64,2048]{1,0:T(8,128)S(1)}) custom-call(f32[128,3584]{1,0:T(8,128)S(1)} %get-tuple-element.14.refs_1_.silu_ref, bf16[32,2048]{1,0:T(8,128)(2,1)S(1)} %bitcast.15, bf16[2048,3584]{1,0:T(8,128)(2,1)S(1)} %copy-done, f32[128,3584]{1,0:T(8,128)S(1)} %back_first_0.1.refs_2_.refs_0_, ...), custom_call_target="tpu_custom_call" | custom-call | flops 5000000000 | tf_op jit(solution)/shard_map/back_second/pallas_call | solution.py:32
  36.3 0.7 %collective-permute-start.12 = (bf16[32,2048]{1,0:T(8,128)(2,1)S(1)}, bf16[32,2048]{1,0:T(8,128)(2,1)S(1)}, u32[]{:S(2)}, u32[]{:S(2)}) collective-permute-start(bf16[32,2048]{1,0:T(8,128)(2,1)S(1)} %get-tuple-element.17.refs_0_), channel_id=1, source_target_pairs={{0,1},{1,0},{2,3},{3,2},{4,5},{5,4},{6,7},{7,6},{8,9},{9,8},{10,11... | collective-permute-start | bytes 393224 | tf_op jit(solution)/shard_map/ppermute | solution.py:232
  37.0 1.4 %collective-permute-start.14 = (bf16[32,2048]{1,0:T(8,128)(2,1)S(1)}, bf16[32,2048]{1,0:T(8,128)(2,1)S(1)}, u32[]{:S(2)}, u32[]{:S(2)}) collective-permute-start(bf16[32,2048]{1,0:T(8,128)(2,1)S(1)} %get-tuple-element.22), channel_id=1, source_target_pairs={{0,1},{1,0},{2,3},{3,2},{4,5},{5,4},{6,7},{7,6},{8,9},{9,8},{10,11... | collective-permute-start | bytes 393224 | tf_op jit(solution)/shard_map/ppermute | solution.py:232
  38.4 0.5 collective-permute-done.7.theirs_ref
  38.9 5.0 %collective-permute-start.9 = (bf16[32,2048]{1,0:T(8,128)(2,1)S(1)}, bf16[32,2048]{1,0:T(8,128)(2,1)S(1)}, u32[]{:S(2)}, u32[]{:S(2)}) collective-permute-start(bf16[32,2048]{1,0:T(8,128)(2,1)S(1)} %fore_pair_0.1.refs_0_), channel_id=1, source_target_pairs={{0,10},{1,11},{2,8},{3,9},{8,18},{9,19},{10,16},{11,17},{16,26},{1... | collective-permute-start | bytes 393224 | tf_op jit(solution)/shard_map/ppermute | solution.py:238
  43.9 1.5 %collective-permute-start.11 = (bf16[32,2048]{1,0:T(8,128)(2,1)S(1)}, bf16[32,2048]{1,0:T(8,128)(2,1)S(1)}, u32[]{:S(2)}, u32[]{:S(2)}) collective-permute-start(bf16[32,2048]{1,0:T(8,128)(2,1)S(1)} %fore_pair_1.1.refs_0_), channel_id=1, source_target_pairs={{0,8},{1,9},{2,10},{3,11},{8,16},{9,17},{10,18},{11,19},{16,24},{1... | collective-permute-start | bytes 393224 | tf_op jit(solution)/shard_map/ppermute | solution.py:238
  45.5 1.8 %collective-permute-done.14.theirs_ref = bf16[32,2048]{1,0:T(8,128)(2,1)S(1)} collective-permute-done((bf16[32,2048]{1,0:T(8,128)(2,1)S(1)}, bf16[32,2048]{1,0:T(8,128)(2,1)S(1)}, u32[]{:S(2)}, u32[]{:S(2)}) %collective-permute-start.14) | collective-permute-done | bytes 131104 | tf_op jit(solution)/shard_map/ppermute | solution.py:232
  47.4 2.5 %collective-permute-start.15 = (bf16[32,2048]{1,0:T(8,128)(2,1)S(1)}, bf16[32,2048]{1,0:T(8,128)(2,1)S(1)}, u32[]{:S(2)}, u32[]{:S(2)}) collective-permute-start(bf16[32,2048]{1,0:T(8,128)(2,1)S(1)} %back_pair_1.1), channel_id=1, source_target_pairs={{0,24},{1,25},{2,26},{3,27},{8,0},{9,1},{10,2},{11,3},{16,8},{17,9... | collective-permute-start | bytes 393224 | tf_op jit(solution)/shard_map/ppermute | solution.py:238
  49.9 1.9 %collective-permute-start.13 = (bf16[32,2048]{1,0:T(8,128)(2,1)S(1)}, bf16[32,2048]{1,0:T(8,128)(2,1)S(1)}, u32[]{:S(2)}, u32[]{:S(2)}) collective-permute-start(bf16[32,2048]{1,0:T(8,128)(2,1)S(1)} %back_pair_0.1.refs_0_), channel_id=1, source_target_pairs={{0,26},{1,27},{2,24},{3,25},{8,2},{9,3},{10,0},{11,1},{16,10},{17,... | collective-permute-start | bytes 393224 | tf_op jit(solution)/shard_map/ppermute | solution.py:238
  51.8 1.6 %gate_gradient.1 = bf16[64,3584]{1,0:T(8,128)(2,1)} custom-call(s32[2]{0:T(128)S(1)} %pad_add_fusion.place_ref, f32[64,3584]{1,0:T(8,128)S(1)} %get-tuple-element.20.slope_ref, f32[128,3584]{1,0:T(8,128)S(1)} %fore_first_0.1.refs_5_.refs_0_, f32[128,3584]{1,0:T(8,128)S(1)} %collective-permute-done.3.refs_1_, f32[128,3584]{1,0:T(8,128)S(1)} %back_first_0.1.refs_2_.refs_0_, ...), custom_call_target="tpu_custom_call" | custom-call | tf_op jit(solution)/shard_map/gate_gradient/pallas_call | solution.py:32
  53.4 0.7 %fore_collect.1 = (bf16[32,2048]{1,0:T(8,128)(2,1)}, f32[8,128]{1,0:T(8,128)S(1)}) custom-call(bf16[32,2048]{1,0:T(8,128)(2,1)S(1)} %collective-permute-done.9.refs_0_, bf16[32,2048]{1,0:T(8,128)(2,1)S(1)} %collective-permute-done.11.refs_1_), custom_call_target="tpu_custom_call" | custom-call | tf_op jit(solution)/shard_map/fore_collect/pallas_call | solution.py:32
  54.1 3.2 %collective-permute-done.13.refs_0_ = bf16[32,2048]{1,0:T(8,128)(2,1)S(1)} collective-permute-done((bf16[32,2048]{1,0:T(8,128)(2,1)S(1)}, bf16[32,2048]{1,0:T(8,128)(2,1)S(1)}, u32[]{:S(2)}, u32[]{:S(2)}) %collective-permute-start.13) | collective-permute-done | bytes 131104 | tf_op jit(solution)/shard_map/ppermute | solution.py:238
  57.4 0.7 %back_collect.1 = (bf16[32,2048]{1,0:T(8,128)(2,1)}, f32[8,128]{1,0:T(8,128)}) custom-call(bf16[32,2048]{1,0:T(8,128)(2,1)S(1)} %collective-permute-done.13.refs_0_, bf16[32,2048]{1,0:T(8,128)(2,1)S(1)} %collective-permute-done.15.refs_1_, f32[8,128]{1,0:T(8,128)S(1)} %get-tuple-element.23.refs_2_), custom_call_target="tpu_custom_call" | custom-call | tf_op jit(solution)/shard_map/back_collect/pallas_call | solution.py:32
  (23 shorter events, 0.2 us)
Async XLA Ops:
  0.6 12.3 %collective-permute-start.1 = (bf16[32,2048]{1,0:T(8,128)(2,1)}, bf16[32,2048]{1,0:T(8,128)(2,1)S(1)}, u32[]{:S(2)}, u32[]{:S(2)}) collective-permute-start(bf16[32,2048]{1,0:T(8,128)(2,1)} %bitcast.8), channel_id=1, source_target_pairs={{0,2},{1,3},{2,0},{3,1},{4,6},{5,7},{6,4},{7,5},{8,10},{9,11},{10,... | collective-permute-start | bytes 393224 | tf_op jit(solution)/shard_map/ppermute | solution.py:232
  4.7 8.2 %collective-permute-start = (bf16[32,2048]{1,0:T(8,128)(2,1)}, bf16[32,2048]{1,0:T(8,128)(2,1)S(1)}, u32[]{:S(2)}, u32[]{:S(2)}) collective-permute-start(bf16[32,2048]{1,0:T(8,128)(2,1)} %bitcast.9), channel_id=1, source_target_pairs={{0,1},{1,0},{2,3},{3,2},{4,5},{5,4},{6,7},{7,6},{8,9},{9,8},{10,11... | collective-permute-start | bytes 393224 | tf_op jit(solution)/shard_map/ppermute | solution.py:232
  6.3 10.7 %collective-permute-start.5 = (bf16[32,2048]{1,0:T(8,128)(2,1)}, bf16[32,2048]{1,0:T(8,128)(2,1)S(1)}, u32[]{:S(2)}, u32[]{:S(2)}) collective-permute-start(bf16[32,2048]{1,0:T(8,128)(2,1)} %bitcast.12), channel_id=1, source_target_pairs={{0,2},{1,3},{2,0},{3,1},{4,6},{5,7},{6,4},{7,5},{8,10},{9,11},{10,... | collective-permute-start | bytes 393224 | tf_op jit(solution)/shard_map/ppermute | solution.py:232
  6.7 13.1 %copy-start = (bf16[2048,3584]{1,0:T(8,128)(2,1)S(1)}, bf16[2048,3584]{1,0:T(8,128)(2,1)}, u32[]{:S(2)}) copy-start(bf16[2048,3584]{1,0:T(8,128)(2,1)} %weight_ref.3) | copy-start | bytes 44040196
  9.5 4.8 %copy-start.3 = (bf16[1,32,2048]{2,1,0:T(8,128)(2,1)S(1)}, bf16[1,32,2048]{2,1,0:T(8,128)(2,1)}, u32[]{:S(2)}) copy-start(bf16[1,32,2048]{2,1,0:T(8,128)(2,1)} %param.9) | copy-start | bytes 393220
  9.5 10.3 %copy-start.2 = (bf16[1,32,2048]{2,1,0:T(8,128)(2,1)S(1)}, bf16[1,32,2048]{2,1,0:T(8,128)(2,1)}, u32[]{:S(2)}) copy-start(bf16[1,32,2048]{2,1,0:T(8,128)(2,1)} %param.5) | copy-start | bytes 393220
  12.9 6.9 %collective-permute-start.2 = (bf16[32,2048]{1,0:T(8,128)(2,1)S(1)}, bf16[32,2048]{1,0:T(8,128)(2,1)S(1)}, u32[]{:S(2)}, u32[]{:S(2)}) collective-permute-start(bf16[32,2048]{1,0:T(8,128)(2,1)S(1)} %relay_x.1), channel_id=1, source_target_pairs={{0,1},{1,0},{2,3},{3,2},{4,5},{5,4},{6,7},{7,6},{8,9},{9,8},{10,11... | collective-permute-start | bytes 393224 | tf_op jit(solution)/shard_map/ppermute | solution.py:232
  14.2 8.0 %collective-permute-start.4 = (bf16[32,2048]{1,0:T(8,128)(2,1)S(1)}, bf16[32,2048]{1,0:T(8,128)(2,1)S(1)}, u32[]{:S(2)}, u32[]{:S(2)}) collective-permute-start(bf16[32,2048]{1,0:T(8,128)(2,1)S(1)} %bitcast.13), channel_id=1, source_target_pairs={{0,1},{1,0},{2,3},{3,2},{4,5},{5,4},{6,7},{7,6},{8,9},{9,8},{10,11... | collective-permute-start | bytes 393224 | tf_op jit(solution)/shard_map/ppermute | solution.py:232
  17.0 6.7 %copy-start.1 = (bf16[3584,2048]{1,0:T(8,128)(2,1)S(1)}, bf16[3584,2048]{1,0:T(8,128)(2,1)}, u32[]{:S(2)}) copy-start(bf16[3584,2048]{1,0:T(8,128)(2,1)} %weight_ref.2) | copy-start | bytes 44040196
  17.0 6.7 %collective-permute-start.6 = (bf16[32,2048]{1,0:T(8,128)(2,1)S(1)}, bf16[32,2048]{1,0:T(8,128)(2,1)S(1)}, u32[]{:S(2)}, u32[]{:S(2)}) collective-permute-start(bf16[32,2048]{1,0:T(8,128)(2,1)S(1)} %relay_g.1), channel_id=1, source_target_pairs={{0,1},{1,0},{2,3},{3,2},{4,5},{5,4},{6,7},{7,6},{8,9},{9,8},{10,11... | collective-permute-start | bytes 393224 | tf_op jit(solution)/shard_map/ppermute | solution.py:232
  21.8 5.9 %collective-permute-start.3 = (f32[128,3584]{1,0:T(8,128)S(1)}, f32[128,3584]{1,0:T(8,128)S(1)}, u32[]{:S(2)}, u32[]{:S(2)}) collective-permute-start(f32[128,3584]{1,0:T(8,128)S(1)} %fore_first_0.1.refs_5_.refs_0_), channel_id=1, source_target_pairs={{0,4},{4,0},{1,5},{5,1},{2,6},{6,2},{3,7},{7,3},{8,12},{12,8},{9,1... | collective-permute-start | bytes 5505032 | tf_op jit(solution)/shard_map/ppermute | solution.py:241
  27.7 4.5 %collective-permute-start.8 = (f32[128,3584]{1,0:T(8,128)S(1)}, f32[128,3584]{1,0:T(8,128)S(1)}, u32[]{:S(2)}, u32[]{:S(2)}) collective-permute-start(f32[128,3584]{1,0:T(8,128)S(1)} %back_first_0.1.refs_2_.refs_0_), channel_id=1, source_target_pairs={{0,4},{4,0},{1,5},{5,1},{2,6},{6,2},{3,7},{7,3},{8,12},{12,8},{9,1... | collective-permute-start | bytes 5505032 | tf_op jit(solution)/shard_map/ppermute | solution.py:241
  30.1 13.8 %collective-permute-start.10 = (bf16[32,2048]{1,0:T(8,128)(2,1)S(1)}, bf16[32,2048]{1,0:T(8,128)(2,1)S(1)}, u32[]{:S(2)}, u32[]{:S(2)}) collective-permute-start(bf16[32,2048]{1,0:T(8,128)(2,1)S(1)} %get-tuple-element.18), channel_id=1, source_target_pairs={{0,1},{1,0},{2,3},{3,2},{4,5},{5,4},{6,7},{7,6},{8,9},{9,8},{10,11... | collective-permute-start | bytes 393224 | tf_op jit(solution)/shard_map/ppermute | solution.py:232
  30.8 8.1 %collective-permute-start.7 = (bf16[32,2048]{1,0:T(8,128)(2,1)S(1)}, bf16[32,2048]{1,0:T(8,128)(2,1)S(1)}, u32[]{:S(2)}, u32[]{:S(2)}) collective-permute-start(bf16[32,2048]{1,0:T(8,128)(2,1)S(1)} %get-tuple-element.16.refs_2_), channel_id=1, source_target_pairs={{0,1},{1,0},{2,3},{3,2},{4,5},{5,4},{6,7},{7,6},{8,9},{9,8},{10,11... | collective-permute-start | bytes 393224 | tf_op jit(solution)/shard_map/ppermute | solution.py:232
  36.3 9.1 %collective-permute-start.12 = (bf16[32,2048]{1,0:T(8,128)(2,1)S(1)}, bf16[32,2048]{1,0:T(8,128)(2,1)S(1)}, u32[]{:S(2)}, u32[]{:S(2)}) collective-permute-start(bf16[32,2048]{1,0:T(8,128)(2,1)S(1)} %get-tuple-element.17.refs_0_), channel_id=1, source_target_pairs={{0,1},{1,0},{2,3},{3,2},{4,5},{5,4},{6,7},{7,6},{8,9},{9,8},{10,11... | collective-permute-start | bytes 393224 | tf_op jit(solution)/shard_map/ppermute | solution.py:232
  37.0 10.3 %collective-permute-start.14 = (bf16[32,2048]{1,0:T(8,128)(2,1)S(1)}, bf16[32,2048]{1,0:T(8,128)(2,1)S(1)}, u32[]{:S(2)}, u32[]{:S(2)}) collective-permute-start(bf16[32,2048]{1,0:T(8,128)(2,1)S(1)} %get-tuple-element.22), channel_id=1, source_target_pairs={{0,1},{1,0},{2,3},{3,2},{4,5},{5,4},{6,7},{7,6},{8,9},{9,8},{10,11... | collective-permute-start | bytes 393224 | tf_op jit(solution)/shard_map/ppermute | solution.py:232
  38.9 14.5 %collective-permute-start.9 = (bf16[32,2048]{1,0:T(8,128)(2,1)S(1)}, bf16[32,2048]{1,0:T(8,128)(2,1)S(1)}, u32[]{:S(2)}, u32[]{:S(2)}) collective-permute-start(bf16[32,2048]{1,0:T(8,128)(2,1)S(1)} %fore_pair_0.1.refs_0_), channel_id=1, source_target_pairs={{0,10},{1,11},{2,8},{3,9},{8,18},{9,19},{10,16},{11,17},{16,26},{1... | collective-permute-start | bytes 393224 | tf_op jit(solution)/shard_map/ppermute | solution.py:238
  43.9 9.5 %collective-permute-start.11 = (bf16[32,2048]{1,0:T(8,128)(2,1)S(1)}, bf16[32,2048]{1,0:T(8,128)(2,1)S(1)}, u32[]{:S(2)}, u32[]{:S(2)}) collective-permute-start(bf16[32,2048]{1,0:T(8,128)(2,1)S(1)} %fore_pair_1.1.refs_0_), channel_id=1, source_target_pairs={{0,8},{1,9},{2,10},{3,11},{8,16},{9,17},{10,18},{11,19},{16,24},{1... | collective-permute-start | bytes 393224 | tf_op jit(solution)/shard_map/ppermute | solution.py:238
  47.4 6.8 %collective-permute-start.15 = (bf16[32,2048]{1,0:T(8,128)(2,1)S(1)}, bf16[32,2048]{1,0:T(8,128)(2,1)S(1)}, u32[]{:S(2)}, u32[]{:S(2)}) collective-permute-start(bf16[32,2048]{1,0:T(8,128)(2,1)S(1)} %back_pair_1.1), channel_id=1, source_target_pairs={{0,24},{1,25},{2,26},{3,27},{8,0},{9,1},{10,2},{11,3},{16,8},{17,9... | collective-permute-start | bytes 393224 | tf_op jit(solution)/shard_map/ppermute | solution.py:238
  49.9 7.5 %collective-permute-start.13 = (bf16[32,2048]{1,0:T(8,128)(2,1)S(1)}, bf16[32,2048]{1,0:T(8,128)(2,1)S(1)}, u32[]{:S(2)}, u32[]{:S(2)}) collective-permute-start(bf16[32,2048]{1,0:T(8,128)(2,1)S(1)} %back_pair_0.1.refs_0_), channel_id=1, source_target_pairs={{0,26},{1,27},{2,24},{3,25},{8,2},{9,3},{10,0},{11,1},{16,10},{17,... | collective-permute-start | bytes 393224 | tf_op jit(solution)/shard_map/ppermute | solution.py:238

commit v5 on v4

--- a/solution.py
+++ b/solution.py
@@ -8,7 +8,7 @@
 from jax.sharding import PartitionSpec as P
 
 MIB = 1 << 20
-COST = {"prepare": 5_000_000_000, "back_first_0": 5_000_000_000, "back_second": 5_000_000_000, "fore_second": 5_000_000_000}
+COST = dict.fromkeys(("prepare", "back_first_0", "back_second", "fore_second", "mark"), 5_000_000_000)
 VMEM = pl.BlockSpec(memory_space=pltpu.VMEM)
 SMEM = pl.BlockSpec(memory_space=pltpu.SMEM)
 ANY = pl.BlockSpec(memory_space=pl.ANY)
@@ -270,23 +270,24 @@
     x_pieces, g_pieces = first_pieces(own_x), first_pieces(own_g)
     silu, slope = prepare(place, gate, row_count, cols)
     x_pieces = last_pieces(x_pieces, [silu, x_pieces[1]], "relay_x")
-    g_pieces = last_pieces(g_pieces, [x_pieces[-2]], "relay_g")
+    g_pieces = last_pieces(g_pieces, [x_pieces[-2], g_pieces[1]], "relay_g")
     up_sums = sums_of(x_pieces, up_weight, False, "fore_first")
     back_sums = sums_of(g_pieces, down_weight, True, "back_first", [up_sums[-1][0]])
-    groups = [list(range(1, cols // 2)), [0]]
+    x_groups, g_groups = [list(range(cols // 2))], [list(range(1, cols // 2)), [0]]
     *sent_x, kept_x = second_product(
-        silu, up_sums, parts, own_x, down_weight, False, cols, groups, "fore_second", [back_sums[-1][0]]
+        silu, up_sums, parts, own_x, down_weight, False, cols, x_groups, "fore_second", [back_sums[-1][0]]
     )
     other_x = [from_xor(sent, 1) for sent in sent_x]
     *sent_g, kept_g = second_product(
-        silu, back_sums, parts, own_g, up_weight, True, cols, groups, "back_second", sent_x[:1]
+        silu, back_sums, parts, own_g, up_weight, True, cols, g_groups, "back_second", sent_x[:1]
     )
     other_g = [from_xor(sent, 1) for sent in sent_g]
-    token, forward = finish(kept_x, other_x, groups, 1, "fore_pair", sent_g[:1])
-    _, backward = finish(kept_g, other_g, groups, -1, "back_pair", [token])
+    token, forward = finish(kept_x, other_x, x_groups, 1, "fore_pair", sent_g[:1])
+    _, backward = finish(kept_g, other_g, g_groups, -1, "back_pair", [token])
 
     gate_grad = gate_gradient(place, slope, up_sums, back_sums, parts, cols)
     handed_forward, token = collect(forward, "fore_collect")
+    (token,) = relay([token], backward[:1], "mark")
     handed_back, _ = collect(backward, "back_collect", [token])
     return handed_forward[None], gate_grad[None], handed_back[None]
 

time: 58.2 us -> 57.1 us (0.981)
  starting transfers between devices: 24.2 us -> 20 us
  waiting for transfers between devices: 14.6 us -> 17.6 us
    ppermute x4, waiting for transfers between devices: 3.26 us -> 5.54 us  [to_block(): return lax.ppermute(value, ('section', 'col'), pairs)]
    ppermute x10 -> x9, starting transfers between devices: 13.1 us -> 10.8 us  [from_xor(): return lax.ppermute(value, 'col', [(c, c ^ k) for c in range(cols)])]
    ppermute x4, starting transfers between devices: 11 us -> 8.93 us  [to_block(): return lax.ppermute(value, ('section', 'col'), pairs)]
    ppermute x10 -> x9, waiting for transfers between devices: 11.4 us -> 11.9 us  [from_xor(): return lax.ppermute(value, 'col', [(c, c ^ k) for c in range(cols)])]
  transfers between devices with their start and end apart: 16 -> 15, of which waited for: 8 -> 11; matrix products, arithmetic and copies ran while one was open for 0% -> 0% of each run, Pallas kernels for 30% -> 31%
where the time goes in v5:
time: 57.1 us; the launch traced here: 56.9 us
  starting transfers between devices  20 us (35%)
  Pallas kernels  18.4 us (32%)
  waiting for transfers between devices  17.6 us (31%)
  between operations  0.73 us (1%)
    pallas_call x14, Pallas kernels, kernel_call(): pl.pallas_call(body, name=name, out_shape=outs, in_specs=[SMEM] * smem +...  18.4 us
    ppermute x9, waiting for transfers between devices, from_xor(): return lax.ppermute(value, 'col', [(c, c ^ k) for c in range(cols)])  11.9 us
    ppermute x9, starting transfers between devices, from_xor(): return lax.ppermute(value, 'col', [(c, c ^ k) for c in range(cols)])  10.8 us
    ppermute x4, starting transfers between devices, to_block(): return lax.ppermute(value, ('section', 'col'), pairs)  8.93 us
    ppermute x4, waiting for transfers between devices, to_block(): return lax.ppermute(value, ('section', 'col'), pairs)  5.54 us
  transfers between devices with their start and end apart: 15, of which 11 were waited for; matrix products, arithmetic and copies ran while one was open for 0% of the time, Pallas kernels for 31%

profile of v5, /device:TPU:0, one launch (start us, length us, event | category | flops | bytes accessed | tf_op | source)
XLA Modules:
  0.0 56.9 jit_solution(17851899347070856678)
XLA Ops:
  0.6 4.1 %collective-permute-start.1 = (bf16[32,2048]{1,0:T(8,128)(2,1)}, bf16[32,2048]{1,0:T(8,128)(2,1)S(1)}, u32[]{:S(2)}, u32[]{:S(2)}) collective-permute-start(bf16[32,2048]{1,0:T(8,128)(2,1)} %bitcast.8), channel_id=1, source_target_pairs={{0,2},{1,3},{2,0},{3,1},{4,6},{5,7},{6,4},{7,5},{8,10},{9,11},{10,... | collective-permute-start | bytes 393224 | tf_op jit(solution)/shard_map/ppermute | solution.py:232
  4.7 1.6 %collective-permute-start = (bf16[32,2048]{1,0:T(8,128)(2,1)}, bf16[32,2048]{1,0:T(8,128)(2,1)S(1)}, u32[]{:S(2)}, u32[]{:S(2)}) collective-permute-start(bf16[32,2048]{1,0:T(8,128)(2,1)} %bitcast.9), channel_id=1, source_target_pairs={{0,1},{1,0},{2,3},{3,2},{4,5},{5,4},{6,7},{7,6},{8,9},{9,8},{10,11... | collective-permute-start | bytes 393224 | tf_op jit(solution)/shard_map/ppermute | solution.py:232
  6.3 0.3 collective-permute-start.5
  6.6 0.2 collective-permute-start.4
  6.9 2.7 %prepare.1 = (f32[128,3584]{1,0:T(8,128)S(1)}, f32[64,3584]{1,0:T(8,128)S(1)}) custom-call(s32[2]{0:T(128)S(1)} %pad_add_fusion.place_ref, bf16[128,3584]{1,0:T(8,128)(2,1)} %bitcast.17), custom_call_target="tpu_custom_call" | custom-call | flops 5000000000 | tf_op jit(solution)/shard_map/prepare/pallas_call | solution.py:32
  9.7 3.2 %collective-permute-done.1.refs_0_.refs_2_.refs_1_ = bf16[32,2048]{1,0:T(8,128)(2,1)S(1)} collective-permute-done((bf16[32,2048]{1,0:T(8,128)(2,1)}, bf16[32,2048]{1,0:T(8,128)(2,1)S(1)}, u32[]{:S(2)}, u32[]{:S(2)}) %collective-permute-start.1) | collective-permute-done | bytes 131104 | tf_op jit(solution)/shard_map/ppermute | solution.py:232
  12.9 1.3 %collective-permute-done.refs_2_.refs_1_ = bf16[32,2048]{1,0:T(8,128)(2,1)S(1)} collective-permute-done((bf16[32,2048]{1,0:T(8,128)(2,1)}, bf16[32,2048]{1,0:T(8,128)(2,1)S(1)}, u32[]{:S(2)}, u32[]{:S(2)}) %collective-permute-start) | collective-permute-done | bytes 131104 | tf_op jit(solution)/shard_map/ppermute | solution.py:232
  14.3 2.7 %collective-permute-done.5.refs_0_.refs_2_ = bf16[32,2048]{1,0:T(8,128)(2,1)S(1)} collective-permute-done((bf16[32,2048]{1,0:T(8,128)(2,1)}, bf16[32,2048]{1,0:T(8,128)(2,1)S(1)}, u32[]{:S(2)}, u32[]{:S(2)}) %collective-permute-start.5) | collective-permute-done | bytes 131104 | tf_op jit(solution)/shard_map/ppermute | solution.py:232
  17.0 1.6 %collective-permute-done.4.refs_2_.refs_1_ = bf16[32,2048]{1,0:T(8,128)(2,1)S(1)} collective-permute-done((bf16[32,2048]{1,0:T(8,128)(2,1)}, bf16[32,2048]{1,0:T(8,128)(2,1)S(1)}, u32[]{:S(2)}, u32[]{:S(2)}) %collective-permute-start.4) | collective-permute-done | bytes 131104 | tf_op jit(solution)/shard_map/ppermute | solution.py:232
  18.6 1.3 %collective-permute-start.6 = (bf16[32,2048]{1,0:T(8,128)(2,1)S(1)}, bf16[32,2048]{1,0:T(8,128)(2,1)S(1)}, u32[]{:S(2)}, u32[]{:S(2)}) collective-permute-start(bf16[32,2048]{1,0:T(8,128)(2,1)S(1)} %relay_g.1), channel_id=1, source_target_pairs={{0,1},{1,0},{2,3},{3,2},{4,5},{5,4},{6,7},{7,6},{8,9},{9,8},{10,11... | collective-permute-start | bytes 393224 | tf_op jit(solution)/shard_map/ppermute | solution.py:232
  19.9 1.3 %collective-permute-done.2.refs_3_ = bf16[32,2048]{1,0:T(8,128)(2,1)S(1)} collective-permute-done((bf16[32,2048]{1,0:T(8,128)(2,1)S(1)}, bf16[32,2048]{1,0:T(8,128)(2,1)S(1)}, u32[]{:S(2)}, u32[]{:S(2)}) %collective-permute-start.2) | collective-permute-done | bytes 131104 | tf_op jit(solution)/shard_map/ppermute | solution.py:232
  21.2 2.1 %fore_first_0.1.refs_5_.refs_0_ = f32[128,3584]{1,0:T(8,128)S(1)} custom-call(bf16[32,2048]{1,0:T(8,128)(2,1)S(1)} %bitcast.10, bf16[32,2048]{1,0:T(8,128)(2,1)S(1)} %collective-permute-done.refs_2_.refs_1_, bf16[32,2048]{1,0:T(8,128)(2,1)S(1)} %collective-permute-done.1.refs_0_.refs_2_.refs_1_, bf16[32,2048]{1,0:T(8,128)(2,1)S(1)} %collective-permute-done.2.refs_3_, ...), custom_call_target="tpu_custom_call" | custom-call | tf_op jit(solution)/shard_map/fore_first_0/pallas_call | solution.py:32
  23.3 0.3 collective-permute-done.6.refs_3_
  23.8 4.0 %back_first_0.1.refs_2_.refs_0_ = f32[128,3584]{1,0:T(8,128)S(1)} custom-call(bf16[32,2048]{1,0:T(8,128)(2,1)S(1)} %bitcast.14, bf16[32,2048]{1,0:T(8,128)(2,1)S(1)} %collective-permute-done.4.refs_2_.refs_1_, bf16[32,2048]{1,0:T(8,128)(2,1)S(1)} %collective-permute-done.5.refs_0_.refs_2_, bf16[32,2048]{1,0:T(8,128)(2,1)S(1)} %collective-permute-done.6.refs_3_, ...), custom_call_target="tpu_custom_call" | custom-call | flops 5000000000 | tf_op jit(solution)/shard_map/back_first_0/pallas_call | solution.py:32
  27.8 0.1 collective-permute-start.8
  27.9 2.3 %fore_second.1 = (bf16[64,2048]{1,0:T(8,128)(2,1)S(1)}, f32[64,2048]{1,0:T(8,128)S(1)}) custom-call(f32[128,3584]{1,0:T(8,128)S(1)} %get-tuple-element.15.refs_1_.silu_ref, bf16[32,2048]{1,0:T(8,128)(2,1)S(1)} %bitcast.11, bf16[3584,2048]{1,0:T(8,128)(2,1)S(1)} %copy-done.1, f32[128,3584]{1,0:T(8,128)S(1)} %fore_first_0.1.refs_5_.refs_0_, ...), custom_call_target="tpu_custom_call" | custom-call | flops 5000000000 | tf_op jit(solution)/shard_map/fore_second/pallas_call | solution.py:32
  30.2 1.2 %collective-permute-start.7 = (bf16[64,2048]{1,0:T(8,128)(2,1)S(1)}, bf16[64,2048]{1,0:T(8,128)(2,1)S(1)}, u32[]{:S(2)}, u32[]{:S(2)}) collective-permute-start(bf16[64,2048]{1,0:T(8,128)(2,1)S(1)} %get-tuple-element.17.refs_2_), channel_id=1, source_target_pairs={{0,1},{1,0},{2,3},{3,2},{4,5},{5,4},{6,7},{7,6},{8,9},{9,8},{10,11... | collective-permute-start | bytes 786440 | tf_op jit(solution)/shard_map/ppermute | solution.py:232
  31.5 0.2 collective-permute-done.8.refs_1_.refs_3_
  31.7 4.1 %back_second.1 = (bf16[32,2048]{1,0:T(8,128)(2,1)S(1)}, bf16[32,2048]{1,0:T(8,128)(2,1)S(1)}, f32[64,2048]{1,0:T(8,128)S(1)}) custom-call(f32[128,3584]{1,0:T(8,128)S(1)} %get-tuple-element.15.refs_1_.silu_ref, bf16[32,2048]{1,0:T(8,128)(2,1)S(1)} %bitcast.15, bf16[2048,3584]{1,0:T(8,128)(2,1)S(1)} %copy-done, f32[128,3584]{1,0:T(8,128)S(1)} %back_first_0.1.refs_2_.refs_0_, ...), custom_call_target="tpu_custom_call" | custom-call | flops 5000000000 | tf_op jit(solution)/shard_map/back_second/pallas_call | solution.py:32
  35.8 1.3 %collective-permute-start.11 = (bf16[32,2048]{1,0:T(8,128)(2,1)S(1)}, bf16[32,2048]{1,0:T(8,128)(2,1)S(1)}, u32[]{:S(2)}, u32[]{:S(2)}) collective-permute-start(bf16[32,2048]{1,0:T(8,128)(2,1)S(1)} %get-tuple-element.18.refs_0_), channel_id=1, source_target_pairs={{0,1},{1,0},{2,3},{3,2},{4,5},{5,4},{6,7},{7,6},{8,9},{9,8},{10,11... | collective-permute-start | bytes 393224 | tf_op jit(solution)/shard_map/ppermute | solution.py:232
  37.0 0.8 %collective-permute-start.13 = (bf16[32,2048]{1,0:T(8,128)(2,1)S(1)}, bf16[32,2048]{1,0:T(8,128)(2,1)S(1)}, u32[]{:S(2)}, u32[]{:S(2)}) collective-permute-start(bf16[32,2048]{1,0:T(8,128)(2,1)S(1)} %get-tuple-element.24), channel_id=1, source_target_pairs={{0,1},{1,0},{2,3},{3,2},{4,5},{5,4},{6,7},{7,6},{8,9},{9,8},{10,11... | collective-permute-start | bytes 393224 | tf_op jit(solution)/shard_map/ppermute | solution.py:232
  37.9 1.5 %collective-permute-done.7.theirs_ref = bf16[64,2048]{1,0:T(8,128)(2,1)S(1)} collective-permute-done((bf16[64,2048]{1,0:T(8,128)(2,1)S(1)}, bf16[64,2048]{1,0:T(8,128)(2,1)S(1)}, u32[]{:S(2)}, u32[]{:S(2)}) %collective-permute-start.7) | collective-permute-done | bytes 262176 | tf_op jit(solution)/shard_map/ppermute | solution.py:232
  39.4 1.7 %collective-permute-start.10 = (bf16[32,2048]{1,0:T(8,128)(2,1)S(1)}, bf16[32,2048]{1,0:T(8,128)(2,1)S(1)}, u32[]{:S(2)}, u32[]{:S(2)}) collective-permute-start(bf16[32,2048]{1,0:T(8,128)(2,1)S(1)} %get-tuple-element.20), channel_id=1, source_target_pairs={{0,10},{1,11},{2,8},{3,9},{8,18},{9,19},{10,16},{11,17},{16,26},{1... | collective-permute-start | bytes 393224 | tf_op jit(solution)/shard_map/ppermute | solution.py:238
  41.1 1.5 %collective-permute-start.9 = (bf16[32,2048]{1,0:T(8,128)(2,1)S(1)}, bf16[32,2048]{1,0:T(8,128)(2,1)S(1)}, u32[]{:S(2)}, u32[]{:S(2)}) collective-permute-start(bf16[32,2048]{1,0:T(8,128)(2,1)S(1)} %get-tuple-element.19.refs_0_), channel_id=1, source_target_pairs={{0,8},{1,9},{2,10},{3,11},{8,16},{9,17},{10,18},{11,19},{16,24},{1... | collective-permute-start | bytes 393224 | tf_op jit(solution)/shard_map/ppermute | solution.py:238
  42.6 3.2 %collective-permute-start.12 = (bf16[32,2048]{1,0:T(8,128)(2,1)S(1)}, bf16[32,2048]{1,0:T(8,128)(2,1)S(1)}, u32[]{:S(2)}, u32[]{:S(2)}) collective-permute-start(bf16[32,2048]{1,0:T(8,128)(2,1)S(1)} %back_pair_0.1.refs_0_), channel_id=1, source_target_pairs={{0,26},{1,27},{2,24},{3,25},{8,2},{9,3},{10,0},{11,1},{16,10},{17,... | collective-permute-start | bytes 393224 | tf_op jit(solution)/shard_map/ppermute | solution.py:238
  45.8 1.6 %gate_gradient.1 = bf16[64,3584]{1,0:T(8,128)(2,1)} custom-call(s32[2]{0:T(128)S(1)} %pad_add_fusion.place_ref, f32[64,3584]{1,0:T(8,128)S(1)} %get-tuple-element.22.slope_ref, f32[128,3584]{1,0:T(8,128)S(1)} %fore_first_0.1.refs_5_.refs_0_, f32[128,3584]{1,0:T(8,128)S(1)} %collective-permute-done.3.refs_1_, f32[128,3584]{1,0:T(8,128)S(1)} %back_first_0.1.refs_2_.refs_0_, ...), custom_call_target="tpu_custom_call" | custom-call | tf_op jit(solution)/shard_map/gate_gradient/pallas_call | solution.py:32
  47.5 2.5 %collective-permute-start.14 = (bf16[32,2048]{1,0:T(8,128)(2,1)S(1)}, bf16[32,2048]{1,0:T(8,128)(2,1)S(1)}, u32[]{:S(2)}, u32[]{:S(2)}) collective-permute-start(bf16[32,2048]{1,0:T(8,128)(2,1)S(1)} %back_pair_1.1), channel_id=1, source_target_pairs={{0,24},{1,25},{2,26},{3,27},{8,0},{9,1},{10,2},{11,3},{16,8},{17,9... | collective-permute-start | bytes 393224 | tf_op jit(solution)/shard_map/ppermute | solution.py:238
  50.0 3.2 %collective-permute-done.10.refs_1_ = bf16[32,2048]{1,0:T(8,128)(2,1)S(1)} collective-permute-done((bf16[32,2048]{1,0:T(8,128)(2,1)S(1)}, bf16[32,2048]{1,0:T(8,128)(2,1)S(1)}, u32[]{:S(2)}, u32[]{:S(2)}) %collective-permute-start.10) | collective-permute-done | bytes 131104 | tf_op jit(solution)/shard_map/ppermute | solution.py:238
  53.2 0.7 %fore_collect.1 = (bf16[32,2048]{1,0:T(8,128)(2,1)}, f32[8,128]{1,0:T(8,128)S(1)}) custom-call(bf16[32,2048]{1,0:T(8,128)(2,1)S(1)} %collective-permute-done.9.refs_0_, bf16[32,2048]{1,0:T(8,128)(2,1)S(1)} %collective-permute-done.10.refs_1_), custom_call_target="tpu_custom_call" | custom-call | tf_op jit(solution)/shard_map/fore_collect/pallas_call | solution.py:32
  53.9 1.6 %collective-permute-done.12.refs_1_.refs_0_ = bf16[32,2048]{1,0:T(8,128)(2,1)S(1)} collective-permute-done((bf16[32,2048]{1,0:T(8,128)(2,1)S(1)}, bf16[32,2048]{1,0:T(8,128)(2,1)S(1)}, u32[]{:S(2)}, u32[]{:S(2)}) %collective-permute-start.12) | collective-permute-done | bytes 131104 | tf_op jit(solution)/shard_map/ppermute | solution.py:238
  55.5 0.7 %collective-permute-done.14.refs_1_ = bf16[32,2048]{1,0:T(8,128)(2,1)S(1)} collective-permute-done((bf16[32,2048]{1,0:T(8,128)(2,1)S(1)}, bf16[32,2048]{1,0:T(8,128)(2,1)S(1)}, u32[]{:S(2)}, u32[]{:S(2)}) %collective-permute-start.14) | collective-permute-done | bytes 131104 | tf_op jit(solution)/shard_map/ppermute | solution.py:238
  56.2 0.7 %back_collect.1 = (bf16[32,2048]{1,0:T(8,128)(2,1)}, f32[8,128]{1,0:T(8,128)}) custom-call(bf16[32,2048]{1,0:T(8,128)(2,1)S(1)} %collective-permute-done.12.refs_1_.refs_0_, bf16[32,2048]{1,0:T(8,128)(2,1)S(1)} %collective-permute-done.14.refs_1_, f32[8,128]{1,0:T(8,128)S(1)} %mark.1.refs_2_), custom_call_target="tpu_custom_call" | custom-call | tf_op jit(solution)/shard_map/back_collect/pallas_call | solution.py:32
  (21 shorter events, 0.5 us)
Async XLA Ops:
  0.6 12.3 %collective-permute-start.1 = (bf16[32,2048]{1,0:T(8,128)(2,1)}, bf16[32,2048]{1,0:T(8,128)(2,1)S(1)}, u32[]{:S(2)}, u32[]{:S(2)}) collective-permute-start(bf16[32,2048]{1,0:T(8,128)(2,1)} %bitcast.8), channel_id=1, source_target_pairs={{0,2},{1,3},{2,0},{3,1},{4,6},{5,7},{6,4},{7,5},{8,10},{9,11},{10,... | collective-permute-start | bytes 393224 | tf_op jit(solution)/shard_map/ppermute | solution.py:232
  4.7 9.5 %collective-permute-start = (bf16[32,2048]{1,0:T(8,128)(2,1)}, bf16[32,2048]{1,0:T(8,128)(2,1)S(1)}, u32[]{:S(2)}, u32[]{:S(2)}) collective-permute-start(bf16[32,2048]{1,0:T(8,128)(2,1)} %bitcast.9), channel_id=1, source_target_pairs={{0,1},{1,0},{2,3},{3,2},{4,5},{5,4},{6,7},{7,6},{8,9},{9,8},{10,11... | collective-permute-start | bytes 393224 | tf_op jit(solution)/shard_map/ppermute | solution.py:232
  6.3 10.7 %collective-permute-start.5 = (bf16[32,2048]{1,0:T(8,128)(2,1)}, bf16[32,2048]{1,0:T(8,128)(2,1)S(1)}, u32[]{:S(2)}, u32[]{:S(2)}) collective-permute-start(bf16[32,2048]{1,0:T(8,128)(2,1)} %bitcast.12), channel_id=1, source_target_pairs={{0,2},{1,3},{2,0},{3,1},{4,6},{5,7},{6,4},{7,5},{8,10},{9,11},{10,... | collective-permute-start | bytes 393224 | tf_op jit(solution)/shard_map/ppermute | solution.py:232
  6.6 11.9 %collective-permute-start.4 = (bf16[32,2048]{1,0:T(8,128)(2,1)}, bf16[32,2048]{1,0:T(8,128)(2,1)S(1)}, u32[]{:S(2)}, u32[]{:S(2)}) collective-permute-start(bf16[32,2048]{1,0:T(8,128)(2,1)} %bitcast.13), channel_id=1, source_target_pairs={{0,1},{1,0},{2,3},{3,2},{4,5},{5,4},{6,7},{7,6},{8,9},{9,8},{10,11... | collective-permute-start | bytes 393224 | tf_op jit(solution)/shard_map/ppermute | solution.py:232
  6.9 14.2 %copy-start = (bf16[2048,3584]{1,0:T(8,128)(2,1)S(1)}, bf16[2048,3584]{1,0:T(8,128)(2,1)}, u32[]{:S(2)}) copy-start(bf16[2048,3584]{1,0:T(8,128)(2,1)} %weight_ref.3) | copy-start | bytes 44040196
  9.7 11.5 %copy-start.2 = (bf16[1,32,2048]{2,1,0:T(8,128)(2,1)S(1)}, bf16[1,32,2048]{2,1,0:T(8,128)(2,1)}, u32[]{:S(2)}) copy-start(bf16[1,32,2048]{2,1,0:T(8,128)(2,1)} %param.5) | copy-start | bytes 393220
  14.2 6.9 %collective-permute-start.2 = (bf16[32,2048]{1,0:T(8,128)(2,1)S(1)}, bf16[32,2048]{1,0:T(8,128)(2,1)S(1)}, u32[]{:S(2)}, u32[]{:S(2)}) collective-permute-start(bf16[32,2048]{1,0:T(8,128)(2,1)S(1)} %relay_x.1), channel_id=1, source_target_pairs={{0,1},{1,0},{2,3},{3,2},{4,5},{5,4},{6,7},{7,6},{8,9},{9,8},{10,11... | collective-permute-start | bytes 393224 | tf_op jit(solution)/shard_map/ppermute | solution.py:232
  18.6 5.2 %copy-start.1 = (bf16[3584,2048]{1,0:T(8,128)(2,1)S(1)}, bf16[3584,2048]{1,0:T(8,128)(2,1)}, u32[]{:S(2)}) copy-start(bf16[3584,2048]{1,0:T(8,128)(2,1)} %weight_ref.2) | copy-start | bytes 44040196
  18.6 5.2 %copy-start.3 = (bf16[1,32,2048]{2,1,0:T(8,128)(2,1)S(1)}, bf16[1,32,2048]{2,1,0:T(8,128)(2,1)}, u32[]{:S(2)}) copy-start(bf16[1,32,2048]{2,1,0:T(8,128)(2,1)} %param.9) | copy-start | bytes 393220
  18.6 5.0 %collective-permute-start.6 = (bf16[32,2048]{1,0:T(8,128)(2,1)S(1)}, bf16[32,2048]{1,0:T(8,128)(2,1)S(1)}, u32[]{:S(2)}, u32[]{:S(2)}) collective-permute-start(bf16[32,2048]{1,0:T(8,128)(2,1)S(1)} %relay_g.1), channel_id=1, source_target_pairs={{0,1},{1,0},{2,3},{3,2},{4,5},{5,4},{6,7},{7,6},{8,9},{9,8},{10,11... | collective-permute-start | bytes 393224 | tf_op jit(solution)/shard_map/ppermute | solution.py:232
  23.2 4.7 %collective-permute-start.3 = (f32[128,3584]{1,0:T(8,128)S(1)}, f32[128,3584]{1,0:T(8,128)S(1)}, u32[]{:S(2)}, u32[]{:S(2)}) collective-permute-start(f32[128,3584]{1,0:T(8,128)S(1)} %fore_first_0.1.refs_5_.refs_0_), channel_id=1, source_target_pairs={{0,4},{4,0},{1,5},{5,1},{2,6},{6,2},{3,7},{7,3},{8,12},{12,8},{9,1... | collective-permute-start | bytes 5505032 | tf_op jit(solution)/shard_map/ppermute | solution.py:241
  27.8 3.8 %collective-permute-start.8 = (f32[128,3584]{1,0:T(8,128)S(1)}, f32[128,3584]{1,0:T(8,128)S(1)}, u32[]{:S(2)}, u32[]{:S(2)}) collective-permute-start(f32[128,3584]{1,0:T(8,128)S(1)} %back_first_0.1.refs_2_.refs_0_), channel_id=1, source_target_pairs={{0,4},{4,0},{1,5},{5,1},{2,6},{6,2},{3,7},{7,3},{8,12},{12,8},{9,1... | collective-permute-start | bytes 5505032 | tf_op jit(solution)/shard_map/ppermute | solution.py:241
  30.2 9.1 %collective-permute-start.7 = (bf16[64,2048]{1,0:T(8,128)(2,1)S(1)}, bf16[64,2048]{1,0:T(8,128)(2,1)S(1)}, u32[]{:S(2)}, u32[]{:S(2)}) collective-permute-start(bf16[64,2048]{1,0:T(8,128)(2,1)S(1)} %get-tuple-element.17.refs_2_), channel_id=1, source_target_pairs={{0,1},{1,0},{2,3},{3,2},{4,5},{5,4},{6,7},{7,6},{8,9},{9,8},{10,11... | collective-permute-start | bytes 786440 | tf_op jit(solution)/shard_map/ppermute | solution.py:232
  35.8 6.8 %collective-permute-start.11 = (bf16[32,2048]{1,0:T(8,128)(2,1)S(1)}, bf16[32,2048]{1,0:T(8,128)(2,1)S(1)}, u32[]{:S(2)}, u32[]{:S(2)}) collective-permute-start(bf16[32,2048]{1,0:T(8,128)(2,1)S(1)} %get-tuple-element.18.refs_0_), channel_id=1, source_target_pairs={{0,1},{1,0},{2,3},{3,2},{4,5},{5,4},{6,7},{7,6},{8,9},{9,8},{10,11... | collective-permute-start | bytes 393224 | tf_op jit(solution)/shard_map/ppermute | solution.py:232
  37.0 10.5 %collective-permute-start.13 = (bf16[32,2048]{1,0:T(8,128)(2,1)S(1)}, bf16[32,2048]{1,0:T(8,128)(2,1)S(1)}, u32[]{:S(2)}, u32[]{:S(2)}) collective-permute-start(bf16[32,2048]{1,0:T(8,128)(2,1)S(1)} %get-tuple-element.24), channel_id=1, source_target_pairs={{0,1},{1,0},{2,3},{3,2},{4,5},{5,4},{6,7},{7,6},{8,9},{9,8},{10,11... | collective-permute-start | bytes 393224 | tf_op jit(solution)/shard_map/ppermute | solution.py:232
  39.4 13.8 %collective-permute-start.10 = (bf16[32,2048]{1,0:T(8,128)(2,1)S(1)}, bf16[32,2048]{1,0:T(8,128)(2,1)S(1)}, u32[]{:S(2)}, u32[]{:S(2)}) collective-permute-start(bf16[32,2048]{1,0:T(8,128)(2,1)S(1)} %get-tuple-element.20), channel_id=1, source_target_pairs={{0,10},{1,11},{2,8},{3,9},{8,18},{9,19},{10,16},{11,17},{16,26},{1... | collective-permute-start | bytes 393224 | tf_op jit(solution)/shard_map/ppermute | solution.py:238
  41.1 12.2 %collective-permute-start.9 = (bf16[32,2048]{1,0:T(8,128)(2,1)S(1)}, bf16[32,2048]{1,0:T(8,128)(2,1)S(1)}, u32[]{:S(2)}, u32[]{:S(2)}) collective-permute-start(bf16[32,2048]{1,0:T(8,128)(2,1)S(1)} %get-tuple-element.19.refs_0_), channel_id=1, source_target_pairs={{0,8},{1,9},{2,10},{3,11},{8,16},{9,17},{10,18},{11,19},{16,24},{1... | collective-permute-start | bytes 393224 | tf_op jit(solution)/shard_map/ppermute | solution.py:238
  42.6 12.9 %collective-permute-start.12 = (bf16[32,2048]{1,0:T(8,128)(2,1)S(1)}, bf16[32,2048]{1,0:T(8,128)(2,1)S(1)}, u32[]{:S(2)}, u32[]{:S(2)}) collective-permute-start(bf16[32,2048]{1,0:T(8,128)(2,1)S(1)} %back_pair_0.1.refs_0_), channel_id=1, source_target_pairs={{0,26},{1,27},{2,24},{3,25},{8,2},{9,3},{10,0},{11,1},{16,10},{17,... | collective-permute-start | bytes 393224 | tf_op jit(solution)/shard_map/ppermute | solution.py:238
  47.5 8.7 %collective-permute-start.14 = (bf16[32,2048]{1,0:T(8,128)(2,1)S(1)}, bf16[32,2048]{1,0:T(8,128)(2,1)S(1)}, u32[]{:S(2)}, u32[]{:S(2)}) collective-permute-start(bf16[32,2048]{1,0:T(8,128)(2,1)S(1)} %back_pair_1.1), channel_id=1, source_target_pairs={{0,24},{1,25},{2,26},{3,27},{8,0},{9,1},{10,2},{11,3},{16,8},{17,9... | collective-permute-start | bytes 393224 | tf_op jit(solution)/shard_map/ppermute | solution.py:238

commit v6 on v5

--- a/solution.py
+++ b/solution.py
@@ -178,7 +178,7 @@
     )
 
 
-def gate_gradient(place, slope, up_sums, back_sums, parts, blocks):
+def gate_gradient(place, slope, up_sums, back_sums, parts, blocks, after):
     own, hidden = slope.shape
     rows = up_sums[0][0].shape[0] // blocks
     count = own // rows
@@ -201,8 +201,9 @@
         body,
         "gate_gradient",
         [shape((own, hidden), BF16)],
-        [place, slope] + [a for pair in up_sums + back_sums for a in pair],
+        [place, slope] + [a for pair in up_sums + back_sums for a in pair] + after,
         smem=1,
+        far=len(after),
     )[0]
 
 
@@ -283,9 +284,9 @@
     )
     other_g = [from_xor(sent, 1) for sent in sent_g]
     token, forward = finish(kept_x, other_x, x_groups, 1, "fore_pair", sent_g[:1])
-    _, backward = finish(kept_g, other_g, g_groups, -1, "back_pair", [token])
-
-    gate_grad = gate_gradient(place, slope, up_sums, back_sums, parts, cols)
+    token, backward = finish(kept_g, other_g, g_groups, -1, "back_pair", [token])
+
+    gate_grad = gate_gradient(place, slope, up_sums, back_sums, parts, cols, [token])
     handed_forward, token = collect(forward, "fore_collect")
     (token,) = relay([token], backward[:1], "mark")
     handed_back, _ = collect(backward, "back_collect", [token])

time: 57.1 us -> 57.1 us (level)
  waiting for transfers between devices: 17.6 us -> 16.7 us
  starting transfers between devices: 20 us -> 20.9 us
    ppermute x4, waiting for transfers between devices: 5.54 us -> 3.92 us  [to_block(): return lax.ppermute(value, ('section', 'col'), pairs)]
    ppermute x4, starting transfers between devices: 8.93 us -> 9.86 us  [to_block(): return lax.ppermute(value, ('section', 'col'), pairs)]
    ppermute x9, waiting for transfers between devices: 11.9 us -> 12.6 us  [from_xor(): return lax.ppermute(value, 'col', [(c, c ^ k) for c in range(cols)])]
  transfers between devices with their start and end apart: 15 -> 15, of which waited for: 11 -> 12; matrix products, arithmetic and copies ran while one was open for 0% -> 0% of each run, Pallas kernels for 31% -> 31%
where the time goes in v6:
time: 57.1 us; the launch traced here: 56.9 us
  starting transfers between devices  20.9 us (37%)
  Pallas kernels  18.4 us (32%)
  waiting for transfers between devices  16.7 us (29%)
  between operations  0.73 us (1%)
    pallas_call x14, Pallas kernels, kernel_call(): pl.pallas_call(body, name=name, out_shape=outs, in_specs=[SMEM] * smem +...  18.4 us
    ppermute x9, waiting for transfers between devices, from_xor(): return lax.ppermute(value, 'col', [(c, c ^ k) for c in range(cols)])  12.6 us
    ppermute x9, starting transfers between devices, from_xor(): return lax.ppermute(value, 'col', [(c, c ^ k) for c in range(cols)])  10.8 us
    ppermute x4, starting transfers between devices, to_block(): return lax.ppermute(value, ('section', 'col'), pairs)  9.86 us
    ppermute x4, waiting for transfers between devices, to_block(): return lax.ppermute(value, ('section', 'col'), pairs)  3.92 us
  transfers between devices with their start and end apart: 15, of which 12 were waited for; matrix products, arithmetic and copies ran while one was open for 0% of the time, Pallas kernels for 31%

profile of v6, /device:TPU:0, one launch (start us, length us, event | category | flops | bytes accessed | tf_op | source)
XLA Modules:
  0.0 56.9 jit_solution(4791255262338398130)
XLA Ops:
  0.6 4.1 %collective-permute-start.1 = (bf16[32,2048]{1,0:T(8,128)(2,1)}, bf16[32,2048]{1,0:T(8,128)(2,1)S(1)}, u32[]{:S(2)}, u32[]{:S(2)}) collective-permute-start(bf16[32,2048]{1,0:T(8,128)(2,1)} %bitcast.8), channel_id=1, source_target_pairs={{0,2},{1,3},{2,0},{3,1},{4,6},{5,7},{6,4},{7,5},{8,10},{9,11},{10,... | collective-permute-start | bytes 393224 | tf_op jit(solution)/shard_map/ppermute | solution.py:233
  4.7 1.6 %collective-permute-start = (bf16[32,2048]{1,0:T(8,128)(2,1)}, bf16[32,2048]{1,0:T(8,128)(2,1)S(1)}, u32[]{:S(2)}, u32[]{:S(2)}) collective-permute-start(bf16[32,2048]{1,0:T(8,128)(2,1)} %bitcast.9), channel_id=1, source_target_pairs={{0,1},{1,0},{2,3},{3,2},{4,5},{5,4},{6,7},{7,6},{8,9},{9,8},{10,11... | collective-permute-start | bytes 393224 | tf_op jit(solution)/shard_map/ppermute | solution.py:233
  6.3 0.3 collective-permute-start.5
  6.6 0.2 collective-permute-start.4
  6.9 2.7 %prepare.1 = (f32[128,3584]{1,0:T(8,128)S(1)}, f32[64,3584]{1,0:T(8,128)S(1)}) custom-call(s32[2]{0:T(128)S(1)} %pad_add_fusion.place_ref, bf16[128,3584]{1,0:T(8,128)(2,1)} %bitcast.17), custom_call_target="tpu_custom_call" | custom-call | flops 5000000000 | tf_op jit(solution)/shard_map/prepare/pallas_call | solution.py:32
  9.7 3.2 %collective-permute-done.1.refs_0_.refs_2_.refs_1_ = bf16[32,2048]{1,0:T(8,128)(2,1)S(1)} collective-permute-done((bf16[32,2048]{1,0:T(8,128)(2,1)}, bf16[32,2048]{1,0:T(8,128)(2,1)S(1)}, u32[]{:S(2)}, u32[]{:S(2)}) %collective-permute-start.1) | collective-permute-done | bytes 131104 | tf_op jit(solution)/shard_map/ppermute | solution.py:233
  12.9 1.3 %collective-permute-done.refs_2_.refs_1_ = bf16[32,2048]{1,0:T(8,128)(2,1)S(1)} collective-permute-done((bf16[32,2048]{1,0:T(8,128)(2,1)}, bf16[32,2048]{1,0:T(8,128)(2,1)S(1)}, u32[]{:S(2)}, u32[]{:S(2)}) %collective-permute-start) | collective-permute-done | bytes 131104 | tf_op jit(solution)/shard_map/ppermute | solution.py:233
  14.3 2.7 %collective-permute-done.5.refs_0_.refs_2_ = bf16[32,2048]{1,0:T(8,128)(2,1)S(1)} collective-permute-done((bf16[32,2048]{1,0:T(8,128)(2,1)}, bf16[32,2048]{1,0:T(8,128)(2,1)S(1)}, u32[]{:S(2)}, u32[]{:S(2)}) %collective-permute-start.5) | collective-permute-done | bytes 131104 | tf_op jit(solution)/shard_map/ppermute | solution.py:233
  17.0 1.6 %collective-permute-done.4.refs_2_.refs_1_ = bf16[32,2048]{1,0:T(8,128)(2,1)S(1)} collective-permute-done((bf16[32,2048]{1,0:T(8,128)(2,1)}, bf16[32,2048]{1,0:T(8,128)(2,1)S(1)}, u32[]{:S(2)}, u32[]{:S(2)}) %collective-permute-start.4) | collective-permute-done | bytes 131104 | tf_op jit(solution)/shard_map/ppermute | solution.py:233
  18.6 1.3 %collective-permute-start.6 = (bf16[32,2048]{1,0:T(8,128)(2,1)S(1)}, bf16[32,2048]{1,0:T(8,128)(2,1)S(1)}, u32[]{:S(2)}, u32[]{:S(2)}) collective-permute-start(bf16[32,2048]{1,0:T(8,128)(2,1)S(1)} %relay_g.1), channel_id=1, source_target_pairs={{0,1},{1,0},{2,3},{3,2},{4,5},{5,4},{6,7},{7,6},{8,9},{9,8},{10,11... | collective-permute-start | bytes 393224 | tf_op jit(solution)/shard_map/ppermute | solution.py:233
  19.9 1.3 %collective-permute-done.2.refs_3_ = bf16[32,2048]{1,0:T(8,128)(2,1)S(1)} collective-permute-done((bf16[32,2048]{1,0:T(8,128)(2,1)S(1)}, bf16[32,2048]{1,0:T(8,128)(2,1)S(1)}, u32[]{:S(2)}, u32[]{:S(2)}) %collective-permute-start.2) | collective-permute-done | bytes 131104 | tf_op jit(solution)/shard_map/ppermute | solution.py:233
  21.2 2.1 %fore_first_0.1.refs_5_.refs_0_ = f32[128,3584]{1,0:T(8,128)S(1)} custom-call(bf16[32,2048]{1,0:T(8,128)(2,1)S(1)} %bitcast.10, bf16[32,2048]{1,0:T(8,128)(2,1)S(1)} %collective-permute-done.refs_2_.refs_1_, bf16[32,2048]{1,0:T(8,128)(2,1)S(1)} %collective-permute-done.1.refs_0_.refs_2_.refs_1_, bf16[32,2048]{1,0:T(8,128)(2,1)S(1)} %collective-permute-done.2.refs_3_, ...), custom_call_target="tpu_custom_call" | custom-call | tf_op jit(solution)/shard_map/fore_first_0/pallas_call | solution.py:32
  23.3 0.3 collective-permute-done.6.refs_3_
  23.8 4.0 %back_first_0.1.refs_2_.refs_0_ = f32[128,3584]{1,0:T(8,128)S(1)} custom-call(bf16[32,2048]{1,0:T(8,128)(2,1)S(1)} %bitcast.14, bf16[32,2048]{1,0:T(8,128)(2,1)S(1)} %collective-permute-done.4.refs_2_.refs_1_, bf16[32,2048]{1,0:T(8,128)(2,1)S(1)} %collective-permute-done.5.refs_0_.refs_2_, bf16[32,2048]{1,0:T(8,128)(2,1)S(1)} %collective-permute-done.6.refs_3_, ...), custom_call_target="tpu_custom_call" | custom-call | flops 5000000000 | tf_op jit(solution)/shard_map/back_first_0/pallas_call | solution.py:32
  27.9 2.3 %fore_second.1 = (bf16[64,2048]{1,0:T(8,128)(2,1)S(1)}, f32[64,2048]{1,0:T(8,128)S(1)}) custom-call(f32[128,3584]{1,0:T(8,128)S(1)} %get-tuple-element.15.refs_1_.silu_ref, bf16[32,2048]{1,0:T(8,128)(2,1)S(1)} %bitcast.11, bf16[3584,2048]{1,0:T(8,128)(2,1)S(1)} %copy-done.1, f32[128,3584]{1,0:T(8,128)S(1)} %fore_first_0.1.refs_5_.refs_0_, ...), custom_call_target="tpu_custom_call" | custom-call | flops 5000000000 | tf_op jit(solution)/shard_map/fore_second/pallas_call | solution.py:32
  30.2 1.2 %collective-permute-start.7 = (bf16[64,2048]{1,0:T(8,128)(2,1)S(1)}, bf16[64,2048]{1,0:T(8,128)(2,1)S(1)}, u32[]{:S(2)}, u32[]{:S(2)}) collective-permute-start(bf16[64,2048]{1,0:T(8,128)(2,1)S(1)} %get-tuple-element.17.refs_2_), channel_id=1, source_target_pairs={{0,1},{1,0},{2,3},{3,2},{4,5},{5,4},{6,7},{7,6},{8,9},{9,8},{10,11... | collective-permute-start | bytes 786440 | tf_op jit(solution)/shard_map/ppermute | solution.py:233
  31.5 0.2 collective-permute-done.8.refs_1_.refs_3_
  31.7 4.1 %back_second.1 = (bf16[32,2048]{1,0:T(8,128)(2,1)S(1)}, bf16[32,2048]{1,0:T(8,128)(2,1)S(1)}, f32[64,2048]{1,0:T(8,128)S(1)}) custom-call(f32[128,3584]{1,0:T(8,128)S(1)} %get-tuple-element.15.refs_1_.silu_ref, bf16[32,2048]{1,0:T(8,128)(2,1)S(1)} %bitcast.15, bf16[2048,3584]{1,0:T(8,128)(2,1)S(1)} %copy-done, f32[128,3584]{1,0:T(8,128)S(1)} %back_first_0.1.refs_2_.refs_0_, ...), custom_call_target="tpu_custom_call" | custom-call | flops 5000000000 | tf_op jit(solution)/shard_map/back_second/pallas_call | solution.py:32
  35.8 1.3 %collective-permute-start.12 = (bf16[32,2048]{1,0:T(8,128)(2,1)S(1)}, bf16[32,2048]{1,0:T(8,128)(2,1)S(1)}, u32[]{:S(2)}, u32[]{:S(2)}) collective-permute-start(bf16[32,2048]{1,0:T(8,128)(2,1)S(1)} %get-tuple-element.18.refs_0_), channel_id=1, source_target_pairs={{0,1},{1,0},{2,3},{3,2},{4,5},{5,4},{6,7},{7,6},{8,9},{9,8},{10,11... | collective-permute-start | bytes 393224 | tf_op jit(solution)/shard_map/ppermute | solution.py:233
  37.0 0.8 %collective-permute-start.11 = (bf16[32,2048]{1,0:T(8,128)(2,1)S(1)}, bf16[32,2048]{1,0:T(8,128)(2,1)S(1)}, u32[]{:S(2)}, u32[]{:S(2)}) collective-permute-start(bf16[32,2048]{1,0:T(8,128)(2,1)S(1)} %get-tuple-element.24), channel_id=1, source_target_pairs={{0,1},{1,0},{2,3},{3,2},{4,5},{5,4},{6,7},{7,6},{8,9},{9,8},{10,11... | collective-permute-start | bytes 393224 | tf_op jit(solution)/shard_map/ppermute | solution.py:233
  37.9 1.5 %collective-permute-done.7.theirs_ref = bf16[64,2048]{1,0:T(8,128)(2,1)S(1)} collective-permute-done((bf16[64,2048]{1,0:T(8,128)(2,1)S(1)}, bf16[64,2048]{1,0:T(8,128)(2,1)S(1)}, u32[]{:S(2)}, u32[]{:S(2)}) %collective-permute-start.7) | collective-permute-done | bytes 262176 | tf_op jit(solution)/shard_map/ppermute | solution.py:233
  39.4 1.7 %collective-permute-start.10 = (bf16[32,2048]{1,0:T(8,128)(2,1)S(1)}, bf16[32,2048]{1,0:T(8,128)(2,1)S(1)}, u32[]{:S(2)}, u32[]{:S(2)}) collective-permute-start(bf16[32,2048]{1,0:T(8,128)(2,1)S(1)} %get-tuple-element.20), channel_id=1, source_target_pairs={{0,10},{1,11},{2,8},{3,9},{8,18},{9,19},{10,16},{11,17},{16,26},{1... | collective-permute-start | bytes 393224 | tf_op jit(solution)/shard_map/ppermute | solution.py:239
  41.1 1.5 %collective-permute-start.9 = (bf16[32,2048]{1,0:T(8,128)(2,1)S(1)}, bf16[32,2048]{1,0:T(8,128)(2,1)S(1)}, u32[]{:S(2)}, u32[]{:S(2)}) collective-permute-start(bf16[32,2048]{1,0:T(8,128)(2,1)S(1)} %get-tuple-element.19.refs_0_), channel_id=1, source_target_pairs={{0,8},{1,9},{2,10},{3,11},{8,16},{9,17},{10,18},{11,19},{16,24},{1... | collective-permute-start | bytes 393224 | tf_op jit(solution)/shard_map/ppermute | solution.py:239
  42.6 3.2 %collective-permute-start.13 = (bf16[32,2048]{1,0:T(8,128)(2,1)S(1)}, bf16[32,2048]{1,0:T(8,128)(2,1)S(1)}, u32[]{:S(2)}, u32[]{:S(2)}) collective-permute-start(bf16[32,2048]{1,0:T(8,128)(2,1)S(1)} %back_pair_0.1.refs_0_), channel_id=1, source_target_pairs={{0,26},{1,27},{2,24},{3,25},{8,2},{9,3},{10,0},{11,1},{16,10},{17,... | collective-permute-start | bytes 393224 | tf_op jit(solution)/shard_map/ppermute | solution.py:239
  45.8 0.7 %collective-permute-done.11.theirs_ref = bf16[32,2048]{1,0:T(8,128)(2,1)S(1)} collective-permute-done((bf16[32,2048]{1,0:T(8,128)(2,1)S(1)}, bf16[32,2048]{1,0:T(8,128)(2,1)S(1)}, u32[]{:S(2)}, u32[]{:S(2)}) %collective-permute-start.11) | collective-permute-done | bytes 131104 | tf_op jit(solution)/shard_map/ppermute | solution.py:233
  46.6 3.4 %collective-permute-start.14 = (bf16[32,2048]{1,0:T(8,128)(2,1)S(1)}, bf16[32,2048]{1,0:T(8,128)(2,1)S(1)}, u32[]{:S(2)}, u32[]{:S(2)}) collective-permute-start(bf16[32,2048]{1,0:T(8,128)(2,1)S(1)} %back_pair_1.1.refs_4_), channel_id=1, source_target_pairs={{0,24},{1,25},{2,26},{3,27},{8,0},{9,1},{10,2},{11,3},{16,8},{17,9... | collective-permute-start | bytes 393224 | tf_op jit(solution)/shard_map/ppermute | solution.py:239
  50.0 1.6 %gate_gradient.1 = bf16[64,3584]{1,0:T(8,128)(2,1)} custom-call(s32[2]{0:T(128)S(1)} %pad_add_fusion.place_ref, f32[64,3584]{1,0:T(8,128)S(1)} %get-tuple-element.22.slope_ref, f32[128,3584]{1,0:T(8,128)S(1)} %fore_first_0.1.refs_5_.refs_0_, f32[128,3584]{1,0:T(8,128)S(1)} %collective-permute-done.3.refs_1_, f32[128,3584]{1,0:T(8,128)S(1)} %back_first_0.1.refs_2_.refs_0_, ...), custom_call_target="tpu_custom_call" | custom-call | tf_op jit(solution)/shard_map/gate_gradient/pallas_call | solution.py:32
  51.6 1.6 %collective-permute-done.10.refs_1_ = bf16[32,2048]{1,0:T(8,128)(2,1)S(1)} collective-permute-done((bf16[32,2048]{1,0:T(8,128)(2,1)S(1)}, bf16[32,2048]{1,0:T(8,128)(2,1)S(1)}, u32[]{:S(2)}, u32[]{:S(2)}) %collective-permute-start.10) | collective-permute-done | bytes 131104 | tf_op jit(solution)/shard_map/ppermute | solution.py:239
  53.2 0.7 %fore_collect.1 = (bf16[32,2048]{1,0:T(8,128)(2,1)}, f32[8,128]{1,0:T(8,128)S(1)}) custom-call(bf16[32,2048]{1,0:T(8,128)(2,1)S(1)} %collective-permute-done.9.refs_0_, bf16[32,2048]{1,0:T(8,128)(2,1)S(1)} %collective-permute-done.10.refs_1_), custom_call_target="tpu_custom_call" | custom-call | tf_op jit(solution)/shard_map/fore_collect/pallas_call | solution.py:32
  53.9 1.5 %collective-permute-done.13.refs_1_.refs_0_ = bf16[32,2048]{1,0:T(8,128)(2,1)S(1)} collective-permute-done((bf16[32,2048]{1,0:T(8,128)(2,1)S(1)}, bf16[32,2048]{1,0:T(8,128)(2,1)S(1)}, u32[]{:S(2)}, u32[]{:S(2)}) %collective-permute-start.13) | collective-permute-done | bytes 131104 | tf_op jit(solution)/shard_map/ppermute | solution.py:239
  55.4 0.8 %collective-permute-done.14.refs_1_ = bf16[32,2048]{1,0:T(8,128)(2,1)S(1)} collective-permute-done((bf16[32,2048]{1,0:T(8,128)(2,1)S(1)}, bf16[32,2048]{1,0:T(8,128)(2,1)S(1)}, u32[]{:S(2)}, u32[]{:S(2)}) %collective-permute-start.14) | collective-permute-done | bytes 131104 | tf_op jit(solution)/shard_map/ppermute | solution.py:239
  56.2 0.7 %back_collect.1 = (bf16[32,2048]{1,0:T(8,128)(2,1)}, f32[8,128]{1,0:T(8,128)}) custom-call(bf16[32,2048]{1,0:T(8,128)(2,1)S(1)} %collective-permute-done.13.refs_1_.refs_0_, bf16[32,2048]{1,0:T(8,128)(2,1)S(1)} %collective-permute-done.14.refs_1_, f32[8,128]{1,0:T(8,128)S(1)} %mark.1.refs_2_), custom_call_target="tpu_custom_call" | custom-call | tf_op jit(solution)/shard_map/back_collect/pallas_call | solution.py:32
  (21 shorter events, 0.6 us)
Async XLA Ops:
  0.6 12.3 %collective-permute-start.1 = (bf16[32,2048]{1,0:T(8,128)(2,1)}, bf16[32,2048]{1,0:T(8,128)(2,1)S(1)}, u32[]{:S(2)}, u32[]{:S(2)}) collective-permute-start(bf16[32,2048]{1,0:T(8,128)(2,1)} %bitcast.8), channel_id=1, source_target_pairs={{0,2},{1,3},{2,0},{3,1},{4,6},{5,7},{6,4},{7,5},{8,10},{9,11},{10,... | collective-permute-start | bytes 393224 | tf_op jit(solution)/shard_map/ppermute | solution.py:233
  4.7 9.5 %collective-permute-start = (bf16[32,2048]{1,0:T(8,128)(2,1)}, bf16[32,2048]{1,0:T(8,128)(2,1)S(1)}, u32[]{:S(2)}, u32[]{:S(2)}) collective-permute-start(bf16[32,2048]{1,0:T(8,128)(2,1)} %bitcast.9), channel_id=1, source_target_pairs={{0,1},{1,0},{2,3},{3,2},{4,5},{5,4},{6,7},{7,6},{8,9},{9,8},{10,11... | collective-permute-start | bytes 393224 | tf_op jit(solution)/shard_map/ppermute | solution.py:233
  6.3 10.7 %collective-permute-start.5 = (bf16[32,2048]{1,0:T(8,128)(2,1)}, bf16[32,2048]{1,0:T(8,128)(2,1)S(1)}, u32[]{:S(2)}, u32[]{:S(2)}) collective-permute-start(bf16[32,2048]{1,0:T(8,128)(2,1)} %bitcast.12), channel_id=1, source_target_pairs={{0,2},{1,3},{2,0},{3,1},{4,6},{5,7},{6,4},{7,5},{8,10},{9,11},{10,... | collective-permute-start | bytes 393224 | tf_op jit(solution)/shard_map/ppermute | solution.py:233
  6.6 11.9 %collective-permute-start.4 = (bf16[32,2048]{1,0:T(8,128)(2,1)}, bf16[32,2048]{1,0:T(8,128)(2,1)S(1)}, u32[]{:S(2)}, u32[]{:S(2)}) collective-permute-start(bf16[32,2048]{1,0:T(8,128)(2,1)} %bitcast.13), channel_id=1, source_target_pairs={{0,1},{1,0},{2,3},{3,2},{4,5},{5,4},{6,7},{7,6},{8,9},{9,8},{10,11... | collective-permute-start | bytes 393224 | tf_op jit(solution)/shard_map/ppermute | solution.py:233
  6.9 14.2 %copy-start = (bf16[2048,3584]{1,0:T(8,128)(2,1)S(1)}, bf16[2048,3584]{1,0:T(8,128)(2,1)}, u32[]{:S(2)}) copy-start(bf16[2048,3584]{1,0:T(8,128)(2,1)} %weight_ref.3) | copy-start | bytes 44040196
  9.7 11.5 %copy-start.2 = (bf16[1,32,2048]{2,1,0:T(8,128)(2,1)S(1)}, bf16[1,32,2048]{2,1,0:T(8,128)(2,1)}, u32[]{:S(2)}) copy-start(bf16[1,32,2048]{2,1,0:T(8,128)(2,1)} %param.5) | copy-start | bytes 393220
  14.2 6.9 %collective-permute-start.2 = (bf16[32,2048]{1,0:T(8,128)(2,1)S(1)}, bf16[32,2048]{1,0:T(8,128)(2,1)S(1)}, u32[]{:S(2)}, u32[]{:S(2)}) collective-permute-start(bf16[32,2048]{1,0:T(8,128)(2,1)S(1)} %relay_x.1), channel_id=1, source_target_pairs={{0,1},{1,0},{2,3},{3,2},{4,5},{5,4},{6,7},{7,6},{8,9},{9,8},{10,11... | collective-permute-start | bytes 393224 | tf_op jit(solution)/shard_map/ppermute | solution.py:233
  18.6 5.2 %copy-start.1 = (bf16[3584,2048]{1,0:T(8,128)(2,1)S(1)}, bf16[3584,2048]{1,0:T(8,128)(2,1)}, u32[]{:S(2)}) copy-start(bf16[3584,2048]{1,0:T(8,128)(2,1)} %weight_ref.2) | copy-start | bytes 44040196
  18.6 5.2 %copy-start.3 = (bf16[1,32,2048]{2,1,0:T(8,128)(2,1)S(1)}, bf16[1,32,2048]{2,1,0:T(8,128)(2,1)}, u32[]{:S(2)}) copy-start(bf16[1,32,2048]{2,1,0:T(8,128)(2,1)} %param.9) | copy-start | bytes 393220
  18.6 5.0 %collective-permute-start.6 = (bf16[32,2048]{1,0:T(8,128)(2,1)S(1)}, bf16[32,2048]{1,0:T(8,128)(2,1)S(1)}, u32[]{:S(2)}, u32[]{:S(2)}) collective-permute-start(bf16[32,2048]{1,0:T(8,128)(2,1)S(1)} %relay_g.1), channel_id=1, source_target_pairs={{0,1},{1,0},{2,3},{3,2},{4,5},{5,4},{6,7},{7,6},{8,9},{9,8},{10,11... | collective-permute-start | bytes 393224 | tf_op jit(solution)/shard_map/ppermute | solution.py:233
  23.2 4.7 %collective-permute-start.3 = (f32[128,3584]{1,0:T(8,128)S(1)}, f32[128,3584]{1,0:T(8,128)S(1)}, u32[]{:S(2)}, u32[]{:S(2)}) collective-permute-start(f32[128,3584]{1,0:T(8,128)S(1)} %fore_first_0.1.refs_5_.refs_0_), channel_id=1, source_target_pairs={{0,4},{4,0},{1,5},{5,1},{2,6},{6,2},{3,7},{7,3},{8,12},{12,8},{9,1... | collective-permute-start | bytes 5505032 | tf_op jit(solution)/shard_map/ppermute | solution.py:242
  27.8 3.8 %collective-permute-start.8 = (f32[128,3584]{1,0:T(8,128)S(1)}, f32[128,3584]{1,0:T(8,128)S(1)}, u32[]{:S(2)}, u32[]{:S(2)}) collective-permute-start(f32[128,3584]{1,0:T(8,128)S(1)} %back_first_0.1.refs_2_.refs_0_), channel_id=1, source_target_pairs={{0,4},{4,0},{1,5},{5,1},{2,6},{6,2},{3,7},{7,3},{8,12},{12,8},{9,1... | collective-permute-start | bytes 5505032 | tf_op jit(solution)/shard_map/ppermute | solution.py:242
  30.2 9.1 %collective-permute-start.7 = (bf16[64,2048]{1,0:T(8,128)(2,1)S(1)}, bf16[64,2048]{1,0:T(8,128)(2,1)S(1)}, u32[]{:S(2)}, u32[]{:S(2)}) collective-permute-start(bf16[64,2048]{1,0:T(8,128)(2,1)S(1)} %get-tuple-element.17.refs_2_), channel_id=1, source_target_pairs={{0,1},{1,0},{2,3},{3,2},{4,5},{5,4},{6,7},{7,6},{8,9},{9,8},{10,11... | collective-permute-start | bytes 786440 | tf_op jit(solution)/shard_map/ppermute | solution.py:233
  35.8 6.8 %collective-permute-start.12 = (bf16[32,2048]{1,0:T(8,128)(2,1)S(1)}, bf16[32,2048]{1,0:T(8,128)(2,1)S(1)}, u32[]{:S(2)}, u32[]{:S(2)}) collective-permute-start(bf16[32,2048]{1,0:T(8,128)(2,1)S(1)} %get-tuple-element.18.refs_0_), channel_id=1, source_target_pairs={{0,1},{1,0},{2,3},{3,2},{4,5},{5,4},{6,7},{7,6},{8,9},{9,8},{10,11... | collective-permute-start | bytes 393224 | tf_op jit(solution)/shard_map/ppermute | solution.py:233
  37.0 9.5 %collective-permute-start.11 = (bf16[32,2048]{1,0:T(8,128)(2,1)S(1)}, bf16[32,2048]{1,0:T(8,128)(2,1)S(1)}, u32[]{:S(2)}, u32[]{:S(2)}) collective-permute-start(bf16[32,2048]{1,0:T(8,128)(2,1)S(1)} %get-tuple-element.24), channel_id=1, source_target_pairs={{0,1},{1,0},{2,3},{3,2},{4,5},{5,4},{6,7},{7,6},{8,9},{9,8},{10,11... | collective-permute-start | bytes 393224 | tf_op jit(solution)/shard_map/ppermute | solution.py:233
  39.4 13.8 %collective-permute-start.10 = (bf16[32,2048]{1,0:T(8,128)(2,1)S(1)}, bf16[32,2048]{1,0:T(8,128)(2,1)S(1)}, u32[]{:S(2)}, u32[]{:S(2)}) collective-permute-start(bf16[32,2048]{1,0:T(8,128)(2,1)S(1)} %get-tuple-element.20), channel_id=1, source_target_pairs={{0,10},{1,11},{2,8},{3,9},{8,18},{9,19},{10,16},{11,17},{16,26},{1... | collective-permute-start | bytes 393224 | tf_op jit(solution)/shard_map/ppermute | solution.py:239
  41.1 12.2 %collective-permute-start.9 = (bf16[32,2048]{1,0:T(8,128)(2,1)S(1)}, bf16[32,2048]{1,0:T(8,128)(2,1)S(1)}, u32[]{:S(2)}, u32[]{:S(2)}) collective-permute-start(bf16[32,2048]{1,0:T(8,128)(2,1)S(1)} %get-tuple-element.19.refs_0_), channel_id=1, source_target_pairs={{0,8},{1,9},{2,10},{3,11},{8,16},{9,17},{10,18},{11,19},{16,24},{1... | collective-permute-start | bytes 393224 | tf_op jit(solution)/shard_map/ppermute | solution.py:239
  42.6 12.8 %collective-permute-start.13 = (bf16[32,2048]{1,0:T(8,128)(2,1)S(1)}, bf16[32,2048]{1,0:T(8,128)(2,1)S(1)}, u32[]{:S(2)}, u32[]{:S(2)}) collective-permute-start(bf16[32,2048]{1,0:T(8,128)(2,1)S(1)} %back_pair_0.1.refs_0_), channel_id=1, source_target_pairs={{0,26},{1,27},{2,24},{3,25},{8,2},{9,3},{10,0},{11,1},{16,10},{17,... | collective-permute-start | bytes 393224 | tf_op jit(solution)/shard_map/ppermute | solution.py:239
  46.6 9.7 %collective-permute-start.14 = (bf16[32,2048]{1,0:T(8,128)(2,1)S(1)}, bf16[32,2048]{1,0:T(8,128)(2,1)S(1)}, u32[]{:S(2)}, u32[]{:S(2)}) collective-permute-start(bf16[32,2048]{1,0:T(8,128)(2,1)S(1)} %back_pair_1.1.refs_4_), channel_id=1, source_target_pairs={{0,24},{1,25},{2,26},{3,27},{8,0},{9,1},{10,2},{11,3},{16,8},{17,9... | collective-permute-start | bytes 393224 | tf_op jit(solution)/shard_map/ppermute | solution.py:239
